TPU v7x, 32 devices: a whole 2x2x4 slice. The times are simulated.
32 devices in a mesh: dp: 8 (over z, core), expert: 4 (over y, x).
Axes of the slice: x: 2, y: 2, z: 4, core: 2. Of those that a mesh axis runs over, the one named last changes fastest.
Arguments:
- tokens: bfloat16 [4096, 2048], P(('dp', 'expert')), may hold values from -6 to 6
- expert_ids: int32 [4096, 4], P(('dp', 'expert')), may hold values from 0 to 7, as said below
- gate_weights: float32 [4096, 4], P(('dp', 'expert')), may hold values from 0.1 to 0.6
- hot_ids: int32 [2], replicated, may hold values from 0 to 7, as said below
- w_gate: bfloat16 [8, 2048, 768], P('expert', 'dp'), may hold values from -0.125 to 0.125
- w_up: bfloat16 [8, 2048, 768], P('expert', 'dp'), may hold values from -0.125 to 0.125
- w_down: bfloat16 [8, 768, 2048], P('expert', None, 'dp'), may hold values from -0.21875 to 0.21875
Outputs:
- moe_out: bfloat16 [4096, 2048], P(('dp', 'expert'))
Inputs may be any that keep to these rules, and one draw needn't show every extreme that they name: `expert_ids`: tokens are in aligned blocks of 128 rows, one block a device. Column 0 of each row names an expert of hot_ids, each listed expert exactly 64 times in every block. Columns 1 to 3 name experts outside hot_ids, all different within a row; each such expert appears at most 128 times in a block, and one of them exactly 128 times in every block. `hot_ids`: the listed experts are all different, and one of them is expert 8 - 1.
All inputs are finite; a program needn't handle non-finite values.
Results may differ from a plain program's by a relative error of at most 0.0057.
Values may be sent and summed in bfloat16 or wider, within the bound.
No kernel may reach another device: no remote copies, remote signals or barrier semaphores. Data moves between devices by JAX's collectives and lax.ppermute only.
A program may use at most 384 MiB of HBM per device.

v0:
```python
import jax
import jax.numpy as jnp
from jax import lax
from jax.sharding import PartitionSpec as P


def capacity(tok_rows, top_k, hot_count, experts):
    return min(tok_rows, max(8, 8 * (2 * tok_rows * (top_k - 1) // ((experts - hot_count) * 8))))


def expert_ffn(token_rows, gate_weight, up_weight, down_weight):
    gate_part = jnp.einsum(
        "aecd,edf->aecf",
        token_rows,
        lax.all_gather(gate_weight, "dp", axis=1, tiled=True),
        preferred_element_type=jnp.float32,
    )
    up_part = jnp.einsum(
        "aecd,edf->aecf",
        token_rows,
        lax.all_gather(up_weight, "dp", axis=1, tiled=True),
        preferred_element_type=jnp.float32,
    )
    hidden = (jax.nn.silu(gate_part) * up_part).astype(jnp.bfloat16)
    return jnp.einsum(
        "aecf,efn->aecn",
        hidden,
        lax.all_gather(down_weight, "dp", axis=2, tiled=True),
        preferred_element_type=jnp.float32,
    ).astype(jnp.bfloat16)


def send_to_owners(
    tokens, pair_ids, pair_gates, per_token, slot_cap, gate_weight, up_weight, down_weight
):
    tok_rows, model_width = tokens.shape
    expert_count = lax.axis_size("expert")
    local_count = gate_weight.shape[0]
    experts = expert_count * local_count
    pair_count = pair_ids.shape[0]
    onehot = (pair_ids[:, None] == jnp.arange(experts, dtype=jnp.int32)[None, :]).astype(jnp.int32)
    rank_index = jnp.sum(jnp.cumsum(onehot, axis=0) * onehot, axis=1) - 1
    slot_index = pair_ids * slot_cap + rank_index
    pair_token = jnp.arange(pair_count, dtype=jnp.int32) // per_token
    slot_table = jnp.full((experts * slot_cap,), tok_rows, jnp.int32).at[slot_index].set(pair_token)
    padded = jnp.concatenate([tokens, jnp.zeros((1, model_width), jnp.bfloat16)], axis=0)
    outgoing = padded[slot_table].reshape(expert_count, local_count, slot_cap, model_width)
    arrived = lax.all_to_all(outgoing, "expert", split_axis=0, concat_axis=0, tiled=True)
    expert_out = expert_ffn(arrived, gate_weight, up_weight, down_weight)
    returned = lax.all_to_all(
        expert_out, "expert", split_axis=0, concat_axis=0, tiled=True
    ).reshape(experts * slot_cap, model_width)
    picked = returned[slot_index].astype(jnp.float32) * pair_gates[:, None]
    return jnp.sum(picked.reshape(tok_rows, per_token, model_width), axis=1)


def shards(tokens, expert_ids, gate_weights, hot_ids, w_gate, w_up, w_down):
    tok_rows, top_k = expert_ids.shape
    hot_count = hot_ids.shape[0]
    local_count = w_gate.shape[0]
    experts = lax.axis_size("expert") * local_count
    cold_cap = capacity(tok_rows, top_k, hot_count, experts)
    hot_cap = tok_rows // hot_count
    output_sum = send_to_owners(
        tokens,
        expert_ids.reshape(tok_rows * top_k),
        gate_weights.reshape(tok_rows * top_k),
        top_k,
        max(cold_cap, hot_cap),
        w_gate,
        w_up,
        w_down,
    )
    return output_sum.astype(jnp.bfloat16)


def solution(mesh):
    placed = (
        P(("dp", "expert"), None),
        P(("dp", "expert"), None),
        P(("dp", "expert"), None),
        P(),
        P("expert", "dp", None),
        P("expert", "dp", None),
        P("expert", None, "dp"),
    )
    return jax.shard_map(
        shards, mesh=mesh, in_specs=placed, out_specs=P(("dp", "expert"), None), check_vma=False
    )
```

profile of v0, /device:TPU:16, one launch (start us, length us, event | category | flops | bytes accessed | tf_op | source)
XLA Modules:
  0.0 288.3 jit_solution(12962817602030378855)
XLA Ops:
  6.5 0.0 all-gather.6.cloned.1.call-start
  6.5 0.7 all-gather.6.cloned.1.call-update
  7.3 0.0 all-gather.4.cloned.1.call-start
  7.3 0.7 all-gather.4.cloned.1.call-update
  8.0 0.0 all-gather.8.cloned.1.call-start
  8.1 0.7 all-gather.8.cloned.1.call-update
  8.7 0.8 copy.15
  9.5 0.1 eq.29
  9.6 0.1 eq.25
  9.8 1.1 reduce-window.6
  10.9 0.2 slice_reduce_fusion
  11.2 0.7 broadcast_multiply_fusion
  11.9 0.1 copy.14
  12.0 0.1 mul.37
  12.1 1.1 concatenate.3
  13.2 0.1 fusion.18
  13.3 2.4 scatter_custom_fusion
  15.8 6.1 %gather_fusion = bf16[1024,2048]{1,0:T(8,128)(2,1)} fusion(bf16[129,2048]{1,0:T(8,128)(2,1)S(1)} %concatenate.3, s32[1024]{0:T(1024)S(1)} %fusion.20), kind=kCustom, calls=%fused_computation | custom fusion | bytes 8392704 | tf_op jit(solution)/shard_map/gather | solution.py:47
  21.8 53.8 %all_to_all.10 = bf16[4,2,128,2048]{3,2,1,0:T(8,128)(2,1)} all-to-all(bf16[4,2,128,2048]{3,2,1,0:T(8,128)(2,1)} %bitcast.49), channel_id=1, replica_groups=mesh['dp'=8,'expert'=4] {'expert'}, dimensions={0} | all-to-all | bytes 8388608 | tf_op jit(solution)/shard_map/all_to_all | solution.py:48
  75.6 0.0 all-gather.6.cloned.1.call-done
  75.6 9.2 %fusion.2 = f32[2,4,128,768]{3,2,1,0:T(8,128)} fusion(bf16[2,2048,768]{2,1,0:T(8,128)(2,1)} %all-gather.6.cloned.1.call-done, bf16[4,2,128,2048]{3,2,1,0:T(8,128)(2,1)} %all_to_all.10), kind=kOutput, calls=%fused_computation.5 | convolution fusion | flops 3221225472 | bytes 13631488 | tf_op jit(solution)/shard_map/aecd,edf->aecf/dot_general | solution.py:18
  84.8 53.7 %all-gather.4.cloned.1.call-done = bf16[2,2048,768]{2,1,0:T(8,128)(2,1)} async-done(((bf16[2,256,768]{2,1,0:T(8,128)(2,1)}), bf16[2,2048,768]{2,1,0:T(8,128)(2,1)}) %all-gather.4.cloned.1.call-update) | async-done | bytes 6291472 | tf_op jit(solution)/shard_map/all_gather | solution.py:15
  138.5 8.7 %fusion.10 = bf16[4,2,128,768]{3,2,0,1:T(8,128)(2,1)S(1)} fusion(f32[2,4,128,768]{3,2,1,0:T(8,128)} %fusion.2, bf16[2,2048,768]{2,1,0:T(8,128)(2,1)} %all-gather.4.cloned.1.call-done, bf16[4,2,128,2048]{3,2,1,0:T(8,128)(2,1)} %all_to_all.10), kind=kOutput, calls=%fused_computation.14 | convolution fusion | flops 3225944064 | bytes 15204352 | tf_op jit(solution)/shard_map/aecd,edf->aecf/dot_general | solution.py:12
  147.2 56.4 %all-gather.8.cloned.1.call-done = bf16[2,768,2048]{2,1,0:T(8,128)(2,1)} async-done(((bf16[2,768,256]{2,1,0:T(8,128)(2,1)}), bf16[2,768,2048]{2,1,0:T(8,128)(2,1)}) %all-gather.8.cloned.1.call-update) | async-done | bytes 6291472 | tf_op jit(solution)/shard_map/all_gather | solution.py:28
  203.6 6.5 %convert_bitcast_fusion = bf16[4,2,128,2048]{3,2,0,1:T(8,128)(2,1)S(1)} fusion(bf16[4,2,128,768]{3,2,0,1:T(8,128)(2,1)S(1)} %fusion.10, bf16[2,768,2048]{2,1,0:T(8,128)(2,1)} %all-gather.8.cloned.1.call-done), kind=kOutput, calls=%fused_computation.10 | convolution fusion | flops 3223322624 | bytes 12058624 | tf_op jit(solution)/shard_map/aecf,efn->aecn/dot_general | solution.py:25
  210.1 2.3 copy.19
  212.3 0.0 copy-start
  212.3 5.2 %all-to-all-start.1 = ((bf16[4,2,128,2048]{3,2,1,0:T(8,128)(2,1)}), bf16[4,2,128,2048]{3,2,1,0:T(8,128)(2,1)}, u32[]{:S(2)}, u32[]{:S(2)}) async-start(bf16[4,2,128,2048]{3,2,1,0:T(8,128)(2,1)} %copy.19), calls=%async_computation.1 | async-start | bytes 8388608 | tf_op jit(solution)/shard_map/all_to_all | solution.py:50
  217.5 0.0 copy-done
  217.5 0.1 copy.20
  217.6 47.8 %all-to-all-done.1 = bf16[4,2,128,2048]{3,2,1,0:T(8,128)(2,1)} async-done(((bf16[4,2,128,2048]{3,2,1,0:T(8,128)(2,1)}), bf16[4,2,128,2048]{3,2,1,0:T(8,128)(2,1)}, u32[]{:S(2)}, u32[]{:S(2)}) %all-to-all-start.1) | async-done | bytes 4194336 | tf_op jit(solution)/shard_map/all_to_all | solution.py:50
  265.4 7.1 %gather_fusion.1 = bf16[512,2048]{1,0:T(8,128)(2,1)S(1)} fusion(bf16[1024,2048]{1,0:T(8,128)(2,1)} %bitcast.14, s32[1024]{0:T(1024)S(1)} %pad_clamp_fusion), kind=kCustom, calls=%fused_computation.1 | custom fusion | bytes 4196352 | tf_op jit(solution)/shard_map/gather | solution.py:53
  272.6 3.0 %reshape.70 = f32[128,4,2048]{2,1,0:T(4,128)} reshape(bf16[512,2048]{1,0:T(8,128)(2,1)S(1)} %gather_fusion.1) | data formatting | bytes 6291456 | tf_op jit(solution)/shard_map/convert_element_type | solution.py:53
  275.6 6.2 %multiply_reduce_fusion = bf16[128,2048]{1,0:T(8,128)(2,1)} fusion(f32[128,4,2048]{2,1,0:T(4,128)} %reshape.70, f32[128,4]{1,0:T(8,128)S(1)} %copy.20), kind=kLoop, calls=%fused_computation.9 | loop fusion | flops 1835008 | bytes 4720640 | tf_op jit(solution)/shard_map/reduce_sum | solution.py:54
  (8 shorter events, 0.1 us)
Async XLA Ops:
  6.5 69.1 %all-gather.6.cloned.1.call-start = ((), (), s32[]{:S(2)}) async-start(), calls=%async_computation.3 | async-start | bytes 7077888 | tf_op jit(solution)/shard_map/all_gather | solution.py:21
  7.3 131.3 %all-gather.4.cloned.1.call-start = ((), (), s32[]{:S(2)}) async-start(), calls=%async_computation.2 | async-start | bytes 7077888 | tf_op jit(solution)/shard_map/all_gather | solution.py:15
  8.0 195.6 %all-gather.8.cloned.1.call-start = ((), (), s32[]{:S(2)}) async-start(), calls=%async_computation.4 | async-start | bytes 7077888 | tf_op jit(solution)/shard_map/all_gather | solution.py:28
  212.3 5.2 %copy-start = (f32[128,4]{0,1:T(4,128)S(1)}, f32[128,4]{0,1:T(4,128)}, u32[]{:S(2)}) copy-start(f32[128,4]{0,1:T(4,128)} %param.9) | copy-start | bytes 6148
  212.3 53.1 %all-to-all-start.1 = ((bf16[4,2,128,2048]{3,2,1,0:T(8,128)(2,1)}), bf16[4,2,128,2048]{3,2,1,0:T(8,128)(2,1)}, u32[]{:S(2)}, u32[]{:S(2)}) async-start(bf16[4,2,128,2048]{3,2,1,0:T(8,128)(2,1)} %copy.19), calls=%async_computation.1 | async-start | bytes 8388608 | tf_op jit(solution)/shard_map/all_to_all | solution.py:50
Sparse Core Ops, SparseCore 0:
  9.0 64.4 all-gather.5
  75.1 63.3 all-gather.3
  140.1 63.3 all-gather.7
where the time goes:
time: 292 us; the launch traced here: 288 us
  waiting for transfers between devices  160 us (55%)
  blocking collectives  53.8 us (18%)
  matrix products  24.3 us (8%)
  local copies, waits for them, and re-layouts  23.6 us (8%)
  between operations  13.2 us (5%)
  other arithmetic  8.2 us (3%)
  starting transfers between devices  5.25 us (2%)
    all_gather x1, waiting for transfers between devices, expert_ffn(): lax.all_gather(down_weight, 'dp', axis=2, tiled=True)  56.4 us
    all_to_all x1, blocking collectives, send_to_owners(): lax.all_to_all(outgoing, 'expert', split_axis=0, concat_axis=0, tiled=True)  53.8 us
    all_gather x1, waiting for transfers between devices, expert_ffn(): lax.all_gather(gate_weight, 'dp', axis=1, tiled=True)  53.7 us
    all_to_all x1, waiting for transfers between devices, send_to_owners(): lax.all_to_all(expert_out, 'expert', split_axis=0, concat_axis=0, tiled=T...  47.8 us
    dot_general x1, matrix products, expert_ffn(): jnp.einsum('aecd,edf->aecf', token_rows, lax.all_gather(up_weight, 'dp',...  9.17 us
    dot_general x1, matrix products, expert_ffn(): jnp.einsum('aecd,edf->aecf', token_rows, lax.all_gather(gate_weight, 'dp'...  8.66 us
    gather x1, local copies, waits for them, and re-layouts, send_to_owners(): picked = returned[slot_index].astype(jnp.float32) * pair_gates[:, None]  7.13 us
    dot_general x1, matrix products, expert_ffn(): jnp.einsum('aecf,efn->aecn', hidden, lax.all_gather(down_weight, 'dp', ax...  6.49 us
  transfers between devices with their start and end apart: 4, of which 3 were waited for; matrix products, arithmetic and copies ran while one was open for 11% of the time, Pallas kernels for 0%

commit v1 on v0

v1 whole, which is shorter than its diff:
```python
import functools

import jax
import jax.numpy as jnp
from jax import lax
from jax.experimental import pallas as pl
from jax.experimental.pallas import tpu as pltpu
from jax.sharding import PartitionSpec as P

LANES = 128
VMEM = 56 * 1024 * 1024


def gate_columns(expert_ids, gate_weights, experts):
    named = expert_ids[:, :, None] == jnp.arange(experts, dtype=jnp.int32)
    table = jnp.sum(jnp.where(named, gate_weights[:, :, None], 0.0), axis=1)
    parts = []
    rest = table
    for _ in range(3):
        part = lax.reduce_precision(rest, 8, 7)
        parts.append(part.astype(jnp.bfloat16))
        rest = rest - part
    packed = jnp.concatenate(parts, axis=1)
    width = -(-packed.shape[1] // LANES) * LANES
    return jnp.pad(packed, ((0, 0), (0, width - packed.shape[1])))


def hidden_kernel(slices, offsets_ref, rows_ref, *refs):
    gate_up, hidden_ref = refs[:slices], refs[slices]
    depth, both = gate_up[0].shape
    sums = jnp.zeros((rows_ref.shape[0], both), jnp.float32)
    for k in range(slices):
        columns = pl.ds(pl.multiple_of(offsets_ref[k], LANES), depth)
        sums += jnp.dot(rows_ref[:, columns], gate_up[k][...], preferred_element_type=jnp.float32)
    gate_sum, up_sum = sums[:, : both // 2], sums[:, both // 2 :]
    hidden_ref[...] = (gate_sum / (1.0 + jnp.exp(-gate_sum)) * up_sum).astype(jnp.bfloat16)


def hidden_of(rows, gate_up, offsets):
    count, width = rows.shape
    both = gate_up[0].shape[1]
    block = min(count, 512)
    return pl.pallas_call(
        functools.partial(hidden_kernel, len(gate_up)),
        grid=(count // block,),
        in_specs=[pl.BlockSpec(memory_space=pltpu.SMEM), pl.BlockSpec((block, width), lambda i: (i, 0))]
        + [pl.BlockSpec(w.shape, lambda i: (0, 0)) for w in gate_up],
        out_specs=pl.BlockSpec((block, both // 2), lambda i: (i, 0)),
        out_shape=jax.ShapeDtypeStruct((count, both // 2), jnp.bfloat16),
        compiler_params=pltpu.CompilerParams(vmem_limit_bytes=VMEM),
        cost_estimate=pl.CostEstimate(
            flops=2 * count * width * both, bytes_accessed=2 * width * (count + both), transcendentals=count * both // 2
        ),
    )(offsets, rows, *gate_up)


def down_kernel(slices, experts, offsets_ref, hidden_ref, gates_ref, *refs):
    down, out_ref = refs[:slices], refs[slices]
    lane = lax.broadcasted_iota(jnp.int32, gates_ref.shape, 1)
    expert = offsets_ref[slices]
    chosen = (lane < 3 * experts) & (lax.rem(lane, experts) == expert)
    gate = jnp.sum(jnp.where(chosen, gates_ref[...].astype(jnp.float32), 0.0), axis=1, keepdims=True)
    hidden = hidden_ref[...]
    for k in range(slices):
        part = jnp.dot(hidden, down[k][...], preferred_element_type=jnp.float32)
        part = part.astype(jnp.bfloat16).astype(jnp.float32) * gate
        columns = pl.ds(pl.multiple_of(offsets_ref[k], LANES), down[k].shape[1])
        out_ref[:, columns] = part.astype(jnp.bfloat16)


def outputs_of(hidden, rows, down, offsets, experts):
    count, inner = hidden.shape
    depth = down[0].shape[1]
    model = depth * len(down)
    extra = rows.shape[1] - model
    block = min(count, 512)
    return pl.pallas_call(
        functools.partial(down_kernel, len(down), experts),
        grid=(count // block,),
        in_specs=[
            pl.BlockSpec(memory_space=pltpu.SMEM),
            pl.BlockSpec((block, inner), lambda i: (i, 0)),
            pl.BlockSpec((block, extra), lambda i: (i, model // extra)),
        ]
        + [pl.BlockSpec(w.shape, lambda i: (0, 0)) for w in down],
        out_specs=pl.BlockSpec((block, model), lambda i: (i, 0)),
        out_shape=jax.ShapeDtypeStruct((count, model), jnp.bfloat16),
        compiler_params=pltpu.CompilerParams(vmem_limit_bytes=VMEM),
        cost_estimate=pl.CostEstimate(
            flops=2 * count * model * inner, bytes_accessed=2 * model * (count + inner), transcendentals=0
        ),
    )(offsets, hidden, rows, *down)


def shards(tokens, expert_ids, gate_weights, hot_ids, w_gate, w_up, w_down):
    del hot_ids
    tok_rows, model = tokens.shape
    places, lines = lax.axis_size("expert"), lax.axis_size("dp")
    layers = lines // 2
    half = layers // 2
    experts = places * w_gate.shape[0]
    depth = w_gate.shape[1]

    def swap_layer(array, mask):
        return lax.ppermute(array, "dp", [(i, i ^ (2 * mask)) for i in range(lines)])

    def swap_core(array):
        return lax.ppermute(array, "dp", [(i, i ^ 1) for i in range(lines)])

    def swap_place(array, mask):
        return lax.ppermute(array, "expert", [(i, i ^ mask) for i in range(places)])

    mirror = layers - 1
    line = lax.axis_index("dp")
    side = (line >= lines // 2).astype(jnp.int32)
    here = lax.axis_index("expert") * w_gate.shape[0] + side

    def pick(array, which):
        return lax.dynamic_index_in_dim(array, which, 0, keepdims=False)

    block = jnp.concatenate([tokens, gate_columns(expert_ids, gate_weights, experts)], axis=1)
    far_block = swap_layer(block, mirror)
    gate_up = jnp.concatenate([w_gate, w_up], axis=2)

    def spread(array):
        own = pick(array, side)
        far = swap_layer(pick(array, 1 - side), mirror)
        near = [(0, own), (mirror, far)]
        for mask in range(1, half):
            near.append((mask, swap_layer(own, mask)))
            near.append((mask ^ mirror, swap_layer(far, mask)))
        found = [(2 * mask, piece) for mask, piece in near]
        found += [(2 * mask + 1, swap_core(piece)) for mask, piece in near]
        return found

    def gather_places(rows):
        mask = 1
        while mask < places:
            rows = jnp.concatenate([rows, swap_place(rows, mask)], axis=0)
            mask *= 2
        return rows

    def home(parts):
        total = parts[:tok_rows].astype(jnp.float32)
        for mask in range(1, places):
            total += swap_place(parts[mask * tok_rows : (mask + 1) * tok_rows], mask).astype(jnp.float32)
        return total

    gate_up_found = spread(gate_up)
    down_found = spread(w_down)
    offsets = jnp.stack([(line ^ mask) * depth for mask, _ in gate_up_found] + [here]).astype(jnp.int32)
    gate_up_list = [piece for _, piece in gate_up_found]
    down_list = [piece for _, piece in down_found]

    rows, far_rows = gather_places(block), gather_places(far_block)
    far_hidden = hidden_of(far_rows, gate_up_list, offsets)
    far_parts = outputs_of(far_hidden, far_rows, down_list, offsets, experts)
    far_sum = swap_layer(home(far_parts).astype(jnp.bfloat16), mirror)
    hidden = hidden_of(rows, gate_up_list, offsets)
    parts = outputs_of(hidden, rows, down_list, offsets, experts)
    return (home(parts) + far_sum.astype(jnp.float32)).astype(jnp.bfloat16)


def solution(mesh):
    placed = (
        P(("dp", "expert"), None),
        P(("dp", "expert"), None),
        P(("dp", "expert"), None),
        P(),
        P("expert", "dp", None),
        P("expert", "dp", None),
        P("expert", None, "dp"),
    )
    return jax.shard_map(
        shards, mesh=mesh, in_specs=placed, out_specs=P(("dp", "expert"), None), check_vma=False
    )
```

time: 292 us -> 200 us (0.68); the launches traced: 288 us -> 199 us
  blocking collectives: 53.8 us -> 0 us
  waiting for transfers between devices: 160 us -> 131 us
  Pallas kernels: 0 us -> 27.3 us
  matrix products: 24.3 us -> 0 us
  starting transfers between devices: 5.25 us -> 18.6 us
  between operations: 13.2 us -> 0.26 us
  local copies, waits for them, and re-layouts: 23.6 us -> 11.5 us
    ppermute x0 -> x26, waiting for transfers between devices: none -> 131 us  [the longest x8 95.6 us: swap_layer(): return lax.ppermute(array, 'dp', [(i, i ^ 2 * mask) for i in range(lines)])]
    all_gather x3 -> x0, waiting for transfers between devices: 110 us -> none  [the longest x1 56.4 us: expert_ffn(): lax.all_gather(down_weight, 'dp', axis=2, tiled=True)]
    all_to_all x1 -> x0, blocking collectives: 53.8 us -> none  [send_to_owners(): lax.all_to_all(outgoing, 'expert', split_axis=0, concat_axis=0, tiled=True)]
    all_to_all x1 -> x0, waiting for transfers between devices: 47.8 us -> none  [send_to_owners(): lax.all_to_all(expert_out, 'expert', split_axis=0, concat_axis=0, tiled=T...]
    pallas_call x0 -> x4, Pallas kernels: none -> 27.3 us  [the longest x2 16.3 us: hidden_of(): pl.pallas_call(functools.partial(hidden_kernel, len(gate_up)), grid=(coun...]
    dot_general x3 -> x0, matrix products: 24.3 us -> none  [the longest x1 9.17 us: expert_ffn(): jnp.einsum('aecd,edf->aecf', token_rows, lax.all_gather(up_weight, 'dp',...]
    ppermute x0 -> x26, starting transfers between devices: none -> 18.6 us  [the longest x10 12.1 us: swap_place(): return lax.ppermute(array, 'expert', [(i, i ^ mask) for i in range(places)])]
    gather x2 -> x0, local copies, waits for them, and re-layouts: 13.2 us -> none  [the longest x1 7.13 us: send_to_owners(): picked = returned[slot_index].astype(jnp.float32) * pair_gates[:, None]]
  transfers between devices with their start and end apart: 4 -> 26, of which waited for: 3 -> 10; matrix products, arithmetic and copies ran while one was open for 11% -> 6% of each run, Pallas kernels for 0% -> 11%
where the time goes in v1:
time: 200 us; the launch traced here: 199 us
  waiting for transfers between devices  131 us (66%)
  Pallas kernels  27.3 us (14%)
  starting transfers between devices  18.6 us (9%)
  local copies, waits for them, and re-layouts  11.5 us (6%)
  other arithmetic  10.3 us (5%)
    ppermute x8, waiting for transfers between devices, swap_layer(): return lax.ppermute(array, 'dp', [(i, i ^ 2 * mask) for i in range(lines)])  95.6 us
    ppermute x10, waiting for transfers between devices, swap_place(): return lax.ppermute(array, 'expert', [(i, i ^ mask) for i in range(places)])  35.8 us
    pallas_call x2, Pallas kernels, hidden_of(): pl.pallas_call(functools.partial(hidden_kernel, len(gate_up)), grid=(coun...  16.3 us
    ppermute x10, starting transfers between devices, swap_place(): return lax.ppermute(array, 'expert', [(i, i ^ mask) for i in range(places)])  12.1 us
    pallas_call x2, Pallas kernels, outputs_of(): pl.pallas_call(functools.partial(down_kernel, len(down), experts), grid=(...  11 us
    ppermute x8, starting transfers between devices, swap_layer(): return lax.ppermute(array, 'dp', [(i, i ^ 2 * mask) for i in range(lines)])  5.43 us
    unnamed x29, local copies, waits for them, and re-layouts  5.33 us
  transfers between devices with their start and end apart: 26, of which 10 were waited for; matrix products, arithmetic and copies ran while one was open for 6% of the time, Pallas kernels for 11%

profile of v1, /device:TPU:16, one launch (start us, length us, event | category | flops | bytes accessed | tf_op | source)
XLA Modules:
  0.0 199.4 jit_solution(660030987376468681)
XLA Ops:
  0.0 0.7 select_reduce_fusion
  0.7 0.1 copy.12
  0.9 2.0 pad_maximum_fusion.3
  2.8 0.4 collective-permute-start.19
  3.3 1.5 collective-permute-start
  4.8 1.2 constant_dynamic-update-slice_fusion.1
  6.0 0.1 constant_dynamic-update-slice_fusion
  6.0 0.0 copy-start
  6.1 1.0 dynamic-slice_bitcast_fusion
  7.1 1.6 collective-permute-start.2
  8.6 47.1 %collective-permute-done.19 = bf16[128,2176]{1,0:T(8,128)(2,1)S(1)} collective-permute-done((bf16[128,2176]{1,0:T(8,128)(2,1)}, bf16[128,2176]{1,0:T(8,128)(2,1)S(1)}, u32[]{:S(2)}, u32[]{:S(2)}) %collective-permute-start.19) | collective-permute-done | bytes 557088 | tf_op jit(solution)/shard_map/ppermute | solution.py:105
  55.8 1.5 collective-permute-start.20
  57.3 1.2 dynamic-slice_bitcast_fusion.2
  58.4 0.0 copy-start.1
  58.4 0.3 collective-permute-start.9
  58.8 1.1 pad_maximum_fusion.1
  59.9 20.0 %collective-permute-done.9.refs_1_ = bf16[768,256]{1,0:T(8,128)(2,1)S(1)} collective-permute-done((bf16[768,256]{1,0:T(8,128)(2,1)S(1)}, bf16[768,256]{1,0:T(8,128)(2,1)S(1)}, u32[]{:S(2)}, u32[]{:S(2)}) %collective-permute-start.9) | collective-permute-done | bytes 393248 | tf_op jit(solution)/shard_map/ppermute | solution.py:105
  79.9 1.5 collective-permute-start.1
  81.4 0.0 collective-permute-done.2.refs_1_
  81.4 0.9 copy-done.10
  82.3 0.7 stack.39.offsets_ref
  83.0 0.0 collective-permute-done.20
  83.0 2.0 %collective-permute-start.4 = (bf16[256,1536]{1,0:T(8,128)(2,1)}, bf16[256,1536]{1,0:T(8,128)(2,1)S(1)}, u32[]{:S(2)}, u32[]{:S(2)}) collective-permute-start(bf16[256,1536]{1,0:T(8,128)(2,1)} %copy-done.10), channel_id=1, source_target_pairs={{0,8},{4,12},{8,0},{12,4},{16,24},{20,28},{24,16},{28,20},{1,9},{5... | collective-permute-start | bytes 2359304 | tf_op jit(solution)/shard_map/ppermute | solution.py:105
  85.0 0.1 pad_maximum_fusion.2
  85.1 9.4 %collective-permute-done.10.refs_2_ = bf16[768,256]{1,0:T(8,128)(2,1)} collective-permute-done((bf16[768,256]{1,0:T(8,128)(2,1)S(1)}, bf16[768,256]{1,0:T(8,128)(2,1)}, u32[]{:S(2)}, u32[]{:S(2)}) %collective-permute-start.10) | collective-permute-done | bytes 393248 | tf_op jit(solution)/shard_map/ppermute | solution.py:105
  94.5 0.0 collective-permute-start.6
  94.5 0.5 collective-permute-start.7
  95.0 0.5 collective-permute-start.21
  95.5 0.1 constant_dynamic-update-slice_fusion.3
  95.6 13.3 %collective-permute-done.4.refs_3_ = bf16[256,1536]{1,0:T(8,128)(2,1)S(1)} collective-permute-done((bf16[256,1536]{1,0:T(8,128)(2,1)}, bf16[256,1536]{1,0:T(8,128)(2,1)S(1)}, u32[]{:S(2)}, u32[]{:S(2)}) %collective-permute-start.4) | collective-permute-done | bytes 786464 | tf_op jit(solution)/shard_map/ppermute | solution.py:105
  108.9 0.3 collective-permute-start.11
  109.1 0.0 collective-permute-done.1
  109.2 0.0 collective-permute-start.8
  109.2 2.8 %pad_maximum_fusion.rows_ref.gates_ref = bf16[512,2176]{1,0:T(8,128)(2,1)} fusion(bf16[256,2176]{1,0:T(8,128)(2,1)} %collective-permute-done.1, bf16[128,2176]{1,0:T(8,128)(2,1)S(1)} %collective-permute-done, bf16[128,128]{1,0:T(8,128)(2,1)S(1)} %pad.4, bf16[128,2048]{1,0:T(8,128)(2,1)S(1)} %copy-done), kind=kLoop, calls=%fused_computation | loop fusion | flops 8912896 | bytes 4456448 | tf_op jit(solution)/shard_map/concatenate | solution.py:139
  111.9 5.8 %collective-permute-done.11.refs_3_ = bf16[768,256]{1,0:T(8,128)(2,1)S(1)} collective-permute-done((bf16[768,256]{1,0:T(8,128)(2,1)S(1)}, bf16[768,256]{1,0:T(8,128)(2,1)S(1)}, u32[]{:S(2)}, u32[]{:S(2)}) %collective-permute-start.11) | collective-permute-done | bytes 393248 | tf_op jit(solution)/shard_map/ppermute | solution.py:105
  117.8 0.5 collective-permute-start.13
  118.3 0.1 collective-permute-start.14
  118.4 11.1 %collective-permute-done.21 = bf16[256,2176]{1,0:T(8,128)(2,1)S(1)} collective-permute-done((bf16[256,2176]{1,0:T(8,128)(2,1)S(1)}, bf16[256,2176]{1,0:T(8,128)(2,1)S(1)}, u32[]{:S(2)}, u32[]{:S(2)}) %collective-permute-start.21) | collective-permute-done | bytes 1114144 | tf_op jit(solution)/shard_map/ppermute | solution.py:111
  129.4 0.1 constant_dynamic-update-slice_fusion.2.rows_ref.gates_ref
  129.6 1.4 copy-done.2
  131.0 8.2 %shard_map.66.hidden_ref = bf16[512,768]{1,0:T(8,128)(2,1)} custom-call(s32[9]{0:T(128)} %stack.39.offsets_ref, bf16[512,2176]{1,0:T(8,128)(2,1)} %copy-done.2, bf16[256,1536]{1,0:T(8,128)(2,1)} %get-tuple-element.12.refs_0_, bf16[256,1536]{1,0:T(8,128)(2,1)} %copy-done.10, bf16[256,1536]{1,0:T(8,128)(2,1)} %collective-permute-done.3.refs_2_, ...), custom_call_target="tpu_custom_call" | custom-call | flops 3422552064 | bytes 8912896 | tf_op jit(solution)/shard_map/pallas_call | solution.py:43
  139.2 0.7 copy-done.5
  139.9 0.1 copy-done.6
  140.1 0.2 copy-done.7
  140.2 0.8 copy-done.8
  141.0 5.5 %shard_map.67 = bf16[512,2048]{1,0:T(8,128)(2,1)} custom-call(s32[9]{0:T(128)} %stack.39.offsets_ref, bf16[512,768]{1,0:T(8,128)(2,1)} %shard_map.66.hidden_ref, bf16[512,2176]{1,0:T(8,128)(2,1)} %copy-done.2, bf16[768,256]{1,0:T(8,128)(2,1)} %copy-done.1, bf16[768,256]{1,0:T(8,128)(2,1)} %copy-done.3, bf16[768,256]{1,0:T(8,128)(2,1)} %collective-permute-done.10.refs_2_, ...), custom_call_target="tpu_custom_call" | custom-call | flops 1610612736 | bytes 5242880 | tf_op jit(solution)/shard_map/pallas_call | solution.py:77
  146.5 1.5 fusion.3
  148.0 2.5 %collective-permute-start.24 = (bf16[128,2048]{1,0:T(8,128)(2,1)S(1)}, bf16[128,2048]{1,0:T(8,128)(2,1)S(1)}, u32[]{:S(2)}, u32[]{:S(2)}) collective-permute-start(bf16[128,2048]{1,0:T(8,128)(2,1)S(1)} %get-tuple-element.9), channel_id=1, source_target_pairs={{0,3},{1,2},{2,1},{3,0},{4,7},{5,6},{6,5},{7,4},{8,11},{9,10},{10,... | collective-permute-start | bytes 1572872 | tf_op jit(solution)/shard_map/ppermute | solution.py:111
  150.5 0.5 collective-permute-start.23
  151.0 0.5 collective-permute-start.22
  151.6 8.2 %shard_map.64.hidden_ref = bf16[512,768]{1,0:T(8,128)(2,1)} custom-call(s32[9]{0:T(128)} %stack.39.offsets_ref, bf16[512,2176]{1,0:T(8,128)(2,1)} %pad_maximum_fusion.rows_ref.gates_ref, bf16[256,1536]{1,0:T(8,128)(2,1)} %get-tuple-element.12.refs_0_, bf16[256,1536]{1,0:T(8,128)(2,1)} %copy-done.10, bf16[256,1536]{1,0:T(8,128)(2,1)} %collective-permute-done.3.refs_2_, ...), custom_call_target="tpu_custom_call" | custom-call | flops 3422552064 | bytes 8912896 | tf_op jit(solution)/shard_map/pallas_call | solution.py:43
  159.7 5.5 %shard_map.65 = bf16[512,2048]{1,0:T(8,128)(2,1)} custom-call(s32[9]{0:T(128)} %stack.39.offsets_ref, bf16[512,768]{1,0:T(8,128)(2,1)} %shard_map.64.hidden_ref, bf16[512,2176]{1,0:T(8,128)(2,1)} %pad_maximum_fusion.rows_ref.gates_ref, bf16[768,256]{1,0:T(8,128)(2,1)} %copy-done.1, bf16[768,256]{1,0:T(8,128)(2,1)} %copy-done.3, ...), custom_call_target="tpu_custom_call" | custom-call | flops 1610612736 | bytes 5242880 | tf_op jit(solution)/shard_map/pallas_call | solution.py:77
  165.2 1.5 fusion.2
  166.8 2.5 %collective-permute-start.18 = (bf16[128,2048]{1,0:T(8,128)(2,1)S(1)}, bf16[128,2048]{1,0:T(8,128)(2,1)S(1)}, u32[]{:S(2)}, u32[]{:S(2)}) collective-permute-start(bf16[128,2048]{1,0:T(8,128)(2,1)S(1)} %get-tuple-element.6), channel_id=1, source_target_pairs={{0,3},{1,2},{2,1},{3,0},{4,7},{5,6},{6,5},{7,4},{8,11},{9,10},{10,... | collective-permute-start | bytes 1572872 | tf_op jit(solution)/shard_map/ppermute | solution.py:111
  169.3 0.5 collective-permute-start.17
  169.8 0.5 collective-permute-start.16
  170.3 4.7 %collective-permute-done.23 = bf16[128,2048]{1,0:T(8,128)(2,1)S(1)} collective-permute-done((bf16[128,2048]{1,0:T(8,128)(2,1)S(1)}, bf16[128,2048]{1,0:T(8,128)(2,1)S(1)}, u32[]{:S(2)}, u32[]{:S(2)}) %collective-permute-start.23) | collective-permute-done | bytes 524320 | tf_op jit(solution)/shard_map/ppermute | solution.py:111
  175.0 0.0 collective-permute-done.22
  175.0 1.4 add_convert_fusion.1
  176.4 0.8 collective-permute-start.25
  177.2 9.1 %collective-permute-done.18 = bf16[128,2048]{1,0:T(8,128)(2,1)S(1)} collective-permute-done((bf16[128,2048]{1,0:T(8,128)(2,1)S(1)}, bf16[128,2048]{1,0:T(8,128)(2,1)S(1)}, u32[]{:S(2)}, u32[]{:S(2)}) %collective-permute-start.18) | collective-permute-done | bytes 524320 | tf_op jit(solution)/shard_map/ppermute | solution.py:111
  186.3 10.8 %collective-permute-done.17 = bf16[128,2048]{1,0:T(8,128)(2,1)S(1)} collective-permute-done((bf16[128,2048]{1,0:T(8,128)(2,1)S(1)}, bf16[128,2048]{1,0:T(8,128)(2,1)S(1)}, u32[]{:S(2)}, u32[]{:S(2)}) %collective-permute-start.17) | collective-permute-done | bytes 524320 | tf_op jit(solution)/shard_map/ppermute | solution.py:111
  197.0 0.1 collective-permute-done.16
  197.2 2.3 %add_convert_fusion = bf16[128,2048]{1,0:T(8,128)(2,1)} fusion(bf16[128,2048]{1,0:T(8,128)(2,1)S(1)} %collective-permute-done.25, bf16[128,2048]{1,0:T(8,128)(2,1)S(1)} %collective-permute-done.18, bf16[128,2048]{1,0:T(8,128)(2,1)S(1)} %collective-permute-done.17, bf16[128,2048]{1,0:T(8,128)(2,1)S(1)} %collective-permute-done.16, bf16[512,2048]{1,0:T(8,128)(2,1)} %shard_map.65), kind=kLoop, calls=%fused_computation.3 | loop fusion | flops 2621440 | bytes 3145728 | tf_op jit(solution)/shard_map/convert_element_type | solution.py:161
  (39 shorter events, 0.1 us)
Async XLA Ops:
  0.8 5.1 %copy-start.9 = (bf16[2,256,768]{2,1,0:T(8,128)(2,1)S(1)}, bf16[2,256,768]{2,1,0:T(8,128)(2,1)}, u32[]{:S(2)}) copy-start(bf16[2,256,768]{2,1,0:T(8,128)(2,1)} %param.11) | copy-start | bytes 2359300
  2.8 52.9 %collective-permute-start.19 = (bf16[128,2176]{1,0:T(8,128)(2,1)}, bf16[128,2176]{1,0:T(8,128)(2,1)S(1)}, u32[]{:S(2)}, u32[]{:S(2)}) collective-permute-start(bf16[128,2176]{1,0:T(8,128)(2,1)} %pad_maximum_fusion.3), channel_id=1, source_target_pairs={{0,24},{4,28},{8,16},{12,20},{16,8},{20,12},{24,0},{28,4},{1,25},{... | collective-permute-start | bytes 1671176 | tf_op jit(solution)/shard_map/ppermute | solution.py:105
  3.3 55.5 %collective-permute-start = (bf16[128,2176]{1,0:T(8,128)(2,1)}, bf16[128,2176]{1,0:T(8,128)(2,1)S(1)}, u32[]{:S(2)}, u32[]{:S(2)}) collective-permute-start(bf16[128,2176]{1,0:T(8,128)(2,1)} %pad_maximum_fusion.3), channel_id=1, source_target_pairs={{0,1},{1,0},{2,3},{3,2},{4,5},{5,4},{6,7},{7,6},{8,9},{9,8},{10,11... | collective-permute-start | bytes 1671176 | tf_op jit(solution)/shard_map/ppermute | solution.py:111
  6.0 52.7 %copy-start = (bf16[128,2048]{1,0:T(8,128)(2,1)S(1)}, bf16[128,2048]{1,0:T(8,128)(2,1)}, u32[]{:S(2)}) copy-start(bf16[128,2048]{1,0:T(8,128)(2,1)} %param.7) | copy-start | bytes 1572868
  7.1 74.4 %collective-permute-start.2 = (bf16[256,1536]{1,0:T(8,128)(2,1)S(1)}, bf16[256,1536]{1,0:T(8,128)(2,1)S(1)}, u32[]{:S(2)}, u32[]{:S(2)}) collective-permute-start(bf16[256,1536]{1,0:T(8,128)(2,1)S(1)} %get-tuple-element.11), channel_id=1, source_target_pairs={{0,24},{4,28},{8,16},{12,20},{16,8},{20,12},{24,0},{28,4},{1,25},{... | collective-permute-start | bytes 2359304 | tf_op jit(solution)/shard_map/ppermute | solution.py:105
  55.8 27.2 %collective-permute-start.20 = (bf16[128,2176]{1,0:T(8,128)(2,1)S(1)}, bf16[128,2176]{1,0:T(8,128)(2,1)S(1)}, u32[]{:S(2)}, u32[]{:S(2)}) collective-permute-start(bf16[128,2176]{1,0:T(8,128)(2,1)S(1)} %collective-permute-done.19), channel_id=1, source_target_pairs={{0,1},{1,0},{2,3},{3,2},{4,5},{5,4},{6,7},{7,6},{8,9},{9,8},{10,11... | collective-permute-start | bytes 1671176 | tf_op jit(solution)/shard_map/ppermute | solution.py:111
  58.4 59.3 %copy-start.1 = (bf16[768,256]{1,0:T(8,128)(2,1)}, bf16[768,256]{1,0:T(8,128)(2,1)S(1)}, u32[]{:S(2)}) copy-start(bf16[768,256]{1,0:T(8,128)(2,1)S(1)} %get-tuple-element.14.refs_0_) | copy-start | bytes 1179652
  58.4 21.5 %collective-permute-start.9 = (bf16[768,256]{1,0:T(8,128)(2,1)S(1)}, bf16[768,256]{1,0:T(8,128)(2,1)S(1)}, u32[]{:S(2)}, u32[]{:S(2)}) collective-permute-start(bf16[768,256]{1,0:T(8,128)(2,1)S(1)} %get-tuple-element.13), channel_id=1, source_target_pairs={{0,24},{4,28},{8,16},{12,20},{16,8},{20,12},{24,0},{28,4},{1,25},{... | collective-permute-start | bytes 1179656 | tf_op jit(solution)/shard_map/ppermute | solution.py:105
  58.8 35.7 %collective-permute-start.3 = (bf16[256,1536]{1,0:T(8,128)(2,1)}, bf16[256,1536]{1,0:T(8,128)(2,1)}, u32[]{:S(2)}, u32[]{:S(2)}) collective-permute-start(bf16[256,1536]{1,0:T(8,128)(2,1)} %get-tuple-element.12.refs_0_), channel_id=1, source_target_pairs={{0,8},{4,12},{8,0},{12,4},{16,24},{20,28},{24,16},{28,20},{1,9},{5... | collective-permute-start | bytes 2359304 | tf_op jit(solution)/shard_map/ppermute | solution.py:105
  58.8 36.2 %collective-permute-start.5 = (bf16[256,1536]{1,0:T(8,128)(2,1)}, bf16[256,1536]{1,0:T(8,128)(2,1)}, u32[]{:S(2)}, u32[]{:S(2)}) collective-permute-start(bf16[256,1536]{1,0:T(8,128)(2,1)} %get-tuple-element.12.refs_0_), channel_id=1, source_target_pairs={{0,4},{4,0},{8,12},{12,8},{16,20},{20,16},{24,28},{28,24},{1,5},{5... | collective-permute-start | bytes 2359304 | tf_op jit(solution)/shard_map/ppermute | solution.py:108
  79.9 37.9 %copy-start.3 = (bf16[768,256]{1,0:T(8,128)(2,1)}, bf16[768,256]{1,0:T(8,128)(2,1)S(1)}, u32[]{:S(2)}) copy-start(bf16[768,256]{1,0:T(8,128)(2,1)S(1)} %collective-permute-done.9.refs_1_) | copy-start | bytes 1179652
  79.9 29.2 %collective-permute-start.1 = (bf16[256,2176]{1,0:T(8,128)(2,1)}, bf16[256,2176]{1,0:T(8,128)(2,1)}, u32[]{:S(2)}, u32[]{:S(2)}) collective-permute-start(bf16[256,2176]{1,0:T(8,128)(2,1)} %pad_maximum_fusion.1), channel_id=1, source_target_pairs={{0,2},{1,3},{2,0},{3,1},{4,6},{5,7},{6,4},{7,5},{8,10},{9,11},{10,... | collective-permute-start | bytes 3342344 | tf_op jit(solution)/shard_map/ppermute | solution.py:111
  81.4 0.9 copy-start.10
  82.3 12.2 %collective-permute-start.10 = (bf16[768,256]{1,0:T(8,128)(2,1)S(1)}, bf16[768,256]{1,0:T(8,128)(2,1)}, u32[]{:S(2)}, u32[]{:S(2)}) collective-permute-start(bf16[768,256]{1,0:T(8,128)(2,1)S(1)} %get-tuple-element.14.refs_0_), channel_id=1, source_target_pairs={{0,8},{4,12},{8,0},{12,4},{16,24},{20,28},{24,16},{28,20},{1,9},{5... | collective-permute-start | bytes 1179656 | tf_op jit(solution)/shard_map/ppermute | solution.py:105
  83.0 25.9 %collective-permute-start.4 = (bf16[256,1536]{1,0:T(8,128)(2,1)}, bf16[256,1536]{1,0:T(8,128)(2,1)S(1)}, u32[]{:S(2)}, u32[]{:S(2)}) collective-permute-start(bf16[256,1536]{1,0:T(8,128)(2,1)} %copy-done.10), channel_id=1, source_target_pairs={{0,8},{4,12},{8,0},{12,4},{16,24},{20,28},{24,16},{28,20},{1,9},{5... | collective-permute-start | bytes 2359304 | tf_op jit(solution)/shard_map/ppermute | solution.py:105
  94.5 23.3 %collective-permute-start.6 = (bf16[256,1536]{1,0:T(8,128)(2,1)}, bf16[256,1536]{1,0:T(8,128)(2,1)}, u32[]{:S(2)}, u32[]{:S(2)}) collective-permute-start(bf16[256,1536]{1,0:T(8,128)(2,1)} %copy-done.10), channel_id=1, source_target_pairs={{0,4},{4,0},{8,12},{12,8},{16,20},{20,16},{24,28},{28,24},{1,5},{5... | collective-permute-start | bytes 2359304 | tf_op jit(solution)/shard_map/ppermute | solution.py:108
  94.5 23.8 %collective-permute-start.7 = (bf16[256,1536]{1,0:T(8,128)(2,1)}, bf16[256,1536]{1,0:T(8,128)(2,1)S(1)}, u32[]{:S(2)}, u32[]{:S(2)}) collective-permute-start(bf16[256,1536]{1,0:T(8,128)(2,1)} %collective-permute-done.3.refs_2_), channel_id=1, source_target_pairs={{0,4},{4,0},{8,12},{12,8},{16,20},{20,16},{24,28},{28,24},{1,5},{5... | collective-permute-start | bytes 2359304 | tf_op jit(solution)/shard_map/ppermute | solution.py:108
  95.0 34.4 %collective-permute-start.21 = (bf16[256,2176]{1,0:T(8,128)(2,1)S(1)}, bf16[256,2176]{1,0:T(8,128)(2,1)S(1)}, u32[]{:S(2)}, u32[]{:S(2)}) collective-permute-start(bf16[256,2176]{1,0:T(8,128)(2,1)S(1)} %pad_maximum_fusion.2), channel_id=1, source_target_pairs={{0,2},{1,3},{2,0},{3,1},{4,6},{5,7},{6,4},{7,5},{8,10},{9,11},{10,... | collective-permute-start | bytes 3342344 | tf_op jit(solution)/shard_map/ppermute | solution.py:111
  108.9 20.7 %copy-start.11 = (bf16[256,1536]{1,0:T(8,128)(2,1)}, bf16[256,1536]{1,0:T(8,128)(2,1)S(1)}, u32[]{:S(2)}) copy-start(bf16[256,1536]{1,0:T(8,128)(2,1)S(1)} %collective-permute-done.4.refs_3_) | copy-start | bytes 2359300
  108.9 8.9 %collective-permute-start.11 = (bf16[768,256]{1,0:T(8,128)(2,1)S(1)}, bf16[768,256]{1,0:T(8,128)(2,1)S(1)}, u32[]{:S(2)}, u32[]{:S(2)}) collective-permute-start(bf16[768,256]{1,0:T(8,128)(2,1)S(1)} %collective-permute-done.9.refs_1_), channel_id=1, source_target_pairs={{0,8},{4,12},{8,0},{12,4},{16,24},{20,28},{24,16},{28,20},{1,9},{5... | collective-permute-start | bytes 1179656 | tf_op jit(solution)/shard_map/ppermute | solution.py:105
  109.2 20.5 %collective-permute-start.8 = (bf16[256,1536]{1,0:T(8,128)(2,1)S(1)}, bf16[256,1536]{1,0:T(8,128)(2,1)}, u32[]{:S(2)}, u32[]{:S(2)}) collective-permute-start(bf16[256,1536]{1,0:T(8,128)(2,1)S(1)} %collective-permute-done.4.refs_3_), channel_id=1, source_target_pairs={{0,4},{4,0},{8,12},{12,8},{16,20},{20,16},{24,28},{28,24},{1,5},{5... | collective-permute-start | bytes 2359304 | tf_op jit(solution)/shard_map/ppermute | solution.py:108
  117.8 21.4 %copy-start.4 = (bf16[768,256]{1,0:T(8,128)(2,1)}, bf16[768,256]{1,0:T(8,128)(2,1)S(1)}, u32[]{:S(2)}) copy-start(bf16[768,256]{1,0:T(8,128)(2,1)S(1)} %collective-permute-done.11.refs_3_) | copy-start | bytes 1179652
  117.8 21.4 %collective-permute-start.12 = (bf16[768,256]{1,0:T(8,128)(2,1)S(1)}, bf16[768,256]{1,0:T(8,128)(2,1)S(1)}, u32[]{:S(2)}, u32[]{:S(2)}) collective-permute-start(bf16[768,256]{1,0:T(8,128)(2,1)S(1)} %get-tuple-element.14.refs_0_), channel_id=1, source_target_pairs={{0,4},{4,0},{8,12},{12,8},{16,20},{20,16},{24,28},{28,24},{1,5},{5... | collective-permute-start | bytes 1179656 | tf_op jit(solution)/shard_map/ppermute | solution.py:108
  117.8 21.4 %collective-permute-start.13 = (bf16[768,256]{1,0:T(8,128)(2,1)S(1)}, bf16[768,256]{1,0:T(8,128)(2,1)S(1)}, u32[]{:S(2)}, u32[]{:S(2)}) collective-permute-start(bf16[768,256]{1,0:T(8,128)(2,1)S(1)} %collective-permute-done.9.refs_1_), channel_id=1, source_target_pairs={{0,4},{4,0},{8,12},{12,8},{16,20},{20,16},{24,28},{28,24},{1,5},{5... | collective-permute-start | bytes 1179656 | tf_op jit(solution)/shard_map/ppermute | solution.py:108
  118.3 11.3 %copy-start.12 = (bf16[256,1536]{1,0:T(8,128)(2,1)}, bf16[256,1536]{1,0:T(8,128)(2,1)S(1)}, u32[]{:S(2)}) copy-start(bf16[256,1536]{1,0:T(8,128)(2,1)S(1)} %collective-permute-done.7.refs_6_) | copy-start | bytes 2359300
  118.3 20.9 %collective-permute-start.14 = (bf16[768,256]{1,0:T(8,128)(2,1)}, bf16[768,256]{1,0:T(8,128)(2,1)S(1)}, u32[]{:S(2)}, u32[]{:S(2)}) collective-permute-start(bf16[768,256]{1,0:T(8,128)(2,1)} %collective-permute-done.10.refs_2_), channel_id=1, source_target_pairs={{0,4},{4,0},{8,12},{12,8},{16,20},{20,16},{24,28},{28,24},{1,5},{5... | collective-permute-start | bytes 1179656 | tf_op jit(solution)/shard_map/ppermute | solution.py:108
  129.4 9.8 %collective-permute-start.15 = (bf16[768,256]{1,0:T(8,128)(2,1)S(1)}, bf16[768,256]{1,0:T(8,128)(2,1)S(1)}, u32[]{:S(2)}, u32[]{:S(2)}) collective-permute-start(bf16[768,256]{1,0:T(8,128)(2,1)S(1)} %collective-permute-done.11.refs_3_), channel_id=1, source_target_pairs={{0,4},{4,0},{8,12},{12,8},{16,20},{20,16},{24,28},{28,24},{1,5},{5... | collective-permute-start | bytes 1179656 | tf_op jit(solution)/shard_map/ppermute | solution.py:108
  129.6 1.4 copy-start.2
  139.2 0.8 copy-start.5
  139.2 0.9 copy-start.6
  139.2 1.0 copy-start.7
  140.2 0.8 copy-start.8
  148.0 21.8 %collective-permute-start.24 = (bf16[128,2048]{1,0:T(8,128)(2,1)S(1)}, bf16[128,2048]{1,0:T(8,128)(2,1)S(1)}, u32[]{:S(2)}, u32[]{:S(2)}) collective-permute-start(bf16[128,2048]{1,0:T(8,128)(2,1)S(1)} %get-tuple-element.9), channel_id=1, source_target_pairs={{0,3},{1,2},{2,1},{3,0},{4,7},{5,6},{6,5},{7,4},{8,11},{9,10},{10,... | collective-permute-start | bytes 1572872 | tf_op jit(solution)/shard_map/ppermute | solution.py:111
  150.5 24.5 %collective-permute-start.23 = (bf16[128,2048]{1,0:T(8,128)(2,1)S(1)}, bf16[128,2048]{1,0:T(8,128)(2,1)S(1)}, u32[]{:S(2)}, u32[]{:S(2)}) collective-permute-start(bf16[128,2048]{1,0:T(8,128)(2,1)S(1)} %get-tuple-element.10), channel_id=1, source_target_pairs={{0,2},{1,3},{2,0},{3,1},{4,6},{5,7},{6,4},{7,5},{8,10},{9,11},{10,... | collective-permute-start | bytes 1572872 | tf_op jit(solution)/shard_map/ppermute | solution.py:111
  151.0 24.0 %collective-permute-start.22 = (bf16[128,2048]{1,0:T(8,128)(2,1)S(1)}, bf16[128,2048]{1,0:T(8,128)(2,1)S(1)}, u32[]{:S(2)}, u32[]{:S(2)}) collective-permute-start(bf16[128,2048]{1,0:T(8,128)(2,1)S(1)} %get-tuple-element.8), channel_id=1, source_target_pairs={{0,1},{1,0},{2,3},{3,2},{4,5},{5,4},{6,7},{7,6},{8,9},{9,8},{10,11... | collective-permute-start | bytes 1572872 | tf_op jit(solution)/shard_map/ppermute | solution.py:111
  166.8 19.5 %collective-permute-start.18 = (bf16[128,2048]{1,0:T(8,128)(2,1)S(1)}, bf16[128,2048]{1,0:T(8,128)(2,1)S(1)}, u32[]{:S(2)}, u32[]{:S(2)}) collective-permute-start(bf16[128,2048]{1,0:T(8,128)(2,1)S(1)} %get-tuple-element.6), channel_id=1, source_target_pairs={{0,3},{1,2},{2,1},{3,0},{4,7},{5,6},{6,5},{7,4},{8,11},{9,10},{10,... | collective-permute-start | bytes 1572872 | tf_op jit(solution)/shard_map/ppermute | solution.py:111
  169.3 27.8 %collective-permute-start.17 = (bf16[128,2048]{1,0:T(8,128)(2,1)S(1)}, bf16[128,2048]{1,0:T(8,128)(2,1)S(1)}, u32[]{:S(2)}, u32[]{:S(2)}) collective-permute-start(bf16[128,2048]{1,0:T(8,128)(2,1)S(1)} %get-tuple-element.7), channel_id=1, source_target_pairs={{0,2},{1,3},{2,0},{3,1},{4,6},{5,7},{6,4},{7,5},{8,10},{9,11},{10,... | collective-permute-start | bytes 1572872 | tf_op jit(solution)/shard_map/ppermute | solution.py:111
  169.8 27.4 %collective-permute-start.16 = (bf16[128,2048]{1,0:T(8,128)(2,1)S(1)}, bf16[128,2048]{1,0:T(8,128)(2,1)S(1)}, u32[]{:S(2)}, u32[]{:S(2)}) collective-permute-start(bf16[128,2048]{1,0:T(8,128)(2,1)S(1)} %get-tuple-element.5), channel_id=1, source_target_pairs={{0,1},{1,0},{2,3},{3,2},{4,5},{5,4},{6,7},{7,6},{8,9},{9,8},{10,11... | collective-permute-start | bytes 1572872 | tf_op jit(solution)/shard_map/ppermute | solution.py:111
  176.4 20.8 %collective-permute-start.25 = (bf16[128,2048]{1,0:T(8,128)(2,1)S(1)}, bf16[128,2048]{1,0:T(8,128)(2,1)S(1)}, u32[]{:S(2)}, u32[]{:S(2)}) collective-permute-start(bf16[128,2048]{1,0:T(8,128)(2,1)S(1)} %add_convert_fusion.1), channel_id=1, source_target_pairs={{0,24},{4,28},{8,16},{12,20},{16,8},{20,12},{24,0},{28,4},{1,25},{... | collective-permute-start | bytes 1572872 | tf_op jit(solution)/shard_map/ppermute | solution.py:105

commit v2 on v1

v2 whole, which is shorter than its diff:
```python
import functools

import jax
import jax.numpy as jnp
from jax import lax
from jax.experimental import pallas as pl
from jax.experimental.pallas import tpu as pltpu
from jax.sharding import PartitionSpec as P

LANES = 128
VMEM = 62 * 1024 * 1024
FREE = pl.CostEstimate(flops=0, bytes_accessed=0, transcendentals=0)
ANY = pl.BlockSpec(memory_space=pl.ANY)
SMEM = pl.BlockSpec(memory_space=pltpu.SMEM)


def gate_columns(expert_ids, gate_weights, experts):
    named = expert_ids[:, :, None] == jnp.arange(experts, dtype=jnp.int32)
    table = jnp.sum(jnp.where(named, gate_weights[:, :, None], 0.0), axis=1)
    parts = []
    rest = table
    for _ in range(3):
        part = lax.reduce_precision(rest, 8, 7)
        parts.append(part.astype(jnp.bfloat16))
        rest = rest - part
    packed = jnp.concatenate(parts, axis=1)
    width = -(-packed.shape[1] // LANES) * LANES
    return jnp.pad(packed, ((0, 0), (0, width - packed.shape[1])))


def after(array, *earlier):
    return lax.optimization_barrier((array, *earlier))[0]


class Loads:
    def __init__(self, sems):
        self.sems, self.used = sems, 0

    def add(self, source, target):
        self.used += 1
        return pltpu.make_async_copy(source, target, self.sems.at[self.used - 1])


def row_loads(loads, row_refs, rows, numbers_ref, slices, depth):
    tok_rows, span = row_refs[0].shape[0], 4 * depth
    copies = []
    for j in range(slices // 4):
        columns = pl.ds(pl.multiple_of(numbers_ref[slices + j], LANES), span)
        for b, row_ref in enumerate(row_refs):
            target = rows.at[pl.ds(b * tok_rows, tok_rows), pl.ds(j * span, span)]
            copies.append(loads.add(row_ref.at[:, columns], target))
    return copies


def weight_loads(loads, weight_refs, weights, numbers_ref, tiles, tile):
    depth, both = weight_refs[0].shape
    copies = []
    for t in range(tiles):
        copies.append([])
        for k, weight_ref in enumerate(weight_refs):
            place = pl.ds(pl.multiple_of((k // 4) * 4 * depth + numbers_ref[k], LANES), depth)
            for part in range(2):
                source = weight_ref.at[:, pl.ds(part * (both // 2) + t * tile, tile)]
                target = weights.at[t, place, pl.ds(part * tile, tile)]
                copies[t].append(loads.add(source, target))
    return copies


def early_kernel(blocks, slices, numbers_ref, *refs):
    row_refs, refs = refs[:blocks], refs[blocks:]
    weight_refs, (gate_out, up_out, rows, weights, sems) = refs[:slices], refs[slices:]
    tiles, _, twice = weights.shape
    tile = twice // 2
    step = pl.program_id(0)
    loads = Loads(sems)
    first = row_loads(loads, row_refs, rows, numbers_ref, slices, weight_refs[0].shape[0])
    by_tile = weight_loads(loads, weight_refs, weights, numbers_ref, tiles, tile)

    @pl.when(step == 0)
    def _():
        for copy in first + [copy for copies in by_tile for copy in copies]:
            copy.start()
        for copy in first:
            copy.wait()

    for t in range(tiles):

        @pl.when(step == t)
        def _():
            for copy in by_tile[t]:
                copy.wait()
            sums = jnp.dot(rows[...], weights[t], preferred_element_type=jnp.float32)
            gate_out[...] = sums[:, :tile]
            up_out[...] = sums[:, tile:]


def late_kernel(blocks, slices, down_slices, experts, model, numbers_ref, *refs):
    row_refs, refs = refs[:blocks], refs[blocks:]
    weight_refs, refs = refs[:slices], refs[slices:]
    down_refs, refs = refs[:down_slices], refs[down_slices:]
    gate_in, up_in, hidden_out, refs = refs[0], refs[1], refs[2], refs[3:]
    out_refs, (rows, weights, hidden, down, gates, sems) = refs[:blocks], refs[blocks:]
    tok_rows = row_refs[0].shape[0]
    tiles, _, twice = weights.shape
    tile = twice // 2
    step = pl.program_id(0)
    loads = Loads(sems)
    first = row_loads(loads, row_refs, rows, numbers_ref, slices, weight_refs[0].shape[0])
    by_tile = weight_loads(loads, weight_refs, weights, numbers_ref, tiles, tile)
    final = [loads.add(ref, down.at[k]) for k, ref in enumerate(down_refs)]
    for b, row_ref in enumerate(row_refs):
        source = row_ref.at[:, pl.ds(model, gates.shape[1])]
        final.append(loads.add(source, gates.at[pl.ds(b * tok_rows, tok_rows)]))

    @pl.when(step == 0)
    def _():
        for copy in first + [copy for copies in by_tile for copy in copies] + final:
            copy.start()
        for copy in first:
            copy.wait()

    for t in range(tiles):

        @pl.when(step == t)
        def _():
            for copy in by_tile[t]:
                copy.wait()
            sums = jnp.dot(rows[...], weights[t], preferred_element_type=jnp.float32)
            gate_sum = sums[:, :tile] + gate_in[...]
            up_sum = sums[:, tile:] + up_in[...]
            hidden[:, t * tile : (t + 1) * tile] = (gate_sum / (1.0 + jnp.exp(-gate_sum)) * up_sum).astype(jnp.bfloat16)

    @pl.when(step == tiles - 1)
    def _():
        for copy in final:
            copy.wait()
        first_down = slices + slices // 4
        weigh_out(hidden, [down.at[k] for k in range(down_slices)], gates, out_refs, experts, numbers_ref, first_down)
        hidden_out[...] = hidden[...]


def weigh_out(hidden, down, gates, out_refs, experts, numbers_ref, at):
    tok_rows = out_refs[0].shape[0]
    lane = lax.broadcasted_iota(jnp.int32, gates.shape, 1)
    chosen = (lane < 3 * experts) & (lax.rem(lane, experts) == numbers_ref[at + len(down)])
    gate = jnp.sum(jnp.where(chosen, gates[...].astype(jnp.float32), 0.0), axis=1, keepdims=True)
    for k, weights in enumerate(down):
        part = jnp.dot(hidden[...], weights[...], preferred_element_type=jnp.float32)
        part = (part.astype(jnp.bfloat16).astype(jnp.float32) * gate).astype(jnp.bfloat16)
        columns = pl.ds(pl.multiple_of(numbers_ref[at + k], LANES), part.shape[1])
        for b, out_ref in enumerate(out_refs):
            out_ref[:, columns] = part[b * tok_rows : (b + 1) * tok_rows]


def early_sums(row_blocks, gate_up, numbers):
    blocks, slices = len(row_blocks), len(gate_up)
    depth, both = gate_up[0].shape
    count, inner = blocks * row_blocks[0].shape[0], both // 2
    tile = 256 if inner % 256 == 0 else inner
    tiles = inner // tile
    spec = pl.BlockSpec((count, tile), lambda i: (0, i))
    return pl.pallas_call(
        functools.partial(early_kernel, blocks, slices),
        grid=(tiles,),
        in_specs=[SMEM] + [ANY] * (blocks + slices),
        out_specs=[spec, spec],
        out_shape=[jax.ShapeDtypeStruct((count, inner), jnp.float32)] * 2,
        scratch_shapes=[
            pltpu.VMEM((count, slices * depth), jnp.bfloat16),
            pltpu.VMEM((tiles, slices * depth, 2 * tile), jnp.bfloat16),
            pltpu.SemaphoreType.DMA((slices // 4 * blocks + 2 * tiles * slices,)),
        ],
        compiler_params=pltpu.CompilerParams(vmem_limit_bytes=VMEM),
        cost_estimate=FREE,
    )(numbers, *row_blocks, *gate_up)


def late_outputs(row_blocks, gate_up, down, numbers, early, experts):
    blocks, slices, down_slices = len(row_blocks), len(gate_up), len(down)
    depth, both = gate_up[0].shape
    tok_rows, width = row_blocks[0].shape
    extra = -(-3 * experts // LANES) * LANES
    count, inner = blocks * tok_rows, both // 2
    tile = 256 if inner % 256 == 0 else inner
    tiles = inner // tile
    spec = pl.BlockSpec((count, tile), lambda i: (0, i))
    out = (tok_rows, down_slices * depth)
    results = pl.pallas_call(
        functools.partial(late_kernel, blocks, slices, down_slices, experts, width - extra),
        grid=(tiles,),
        in_specs=[SMEM] + [ANY] * (blocks + slices + down_slices) + [spec, spec],
        out_specs=[pl.BlockSpec((count, inner), lambda i: (0, 0))] + [pl.BlockSpec(out, lambda i: (0, 0))] * blocks,
        out_shape=[jax.ShapeDtypeStruct((count, inner), jnp.bfloat16)] + [jax.ShapeDtypeStruct(out, jnp.bfloat16)] * blocks,
        scratch_shapes=[
            pltpu.VMEM((count, slices * depth), jnp.bfloat16),
            pltpu.VMEM((tiles, slices * depth, 2 * tile), jnp.bfloat16),
            pltpu.VMEM((count, inner), jnp.bfloat16),
            pltpu.VMEM((down_slices, inner, depth), jnp.bfloat16),
            pltpu.VMEM((count, extra), jnp.bfloat16),
            pltpu.SemaphoreType.DMA((slices // 4 * blocks + 2 * tiles * slices + down_slices + blocks,)),
        ],
        compiler_params=pltpu.CompilerParams(vmem_limit_bytes=VMEM),
        cost_estimate=FREE,
    )(numbers, *row_blocks, *gate_up, *down, *early)
    return results[0], results[1:]


def down_kernel(blocks, slices, experts, model, numbers_ref, hidden_ref, *refs):
    row_refs, refs = refs[:blocks], refs[blocks:]
    weight_refs, refs = refs[:slices], refs[slices:]
    out_refs, (gates, sems) = refs[:blocks], refs[blocks:]
    tok_rows = row_refs[0].shape[0]
    loads = Loads(sems)
    copies = []
    for b, row_ref in enumerate(row_refs):
        source = row_ref.at[:, pl.ds(model, gates.shape[1])]
        copies.append(loads.add(source, gates.at[pl.ds(b * tok_rows, tok_rows)]))
    for copy in copies:
        copy.start()
    for copy in copies:
        copy.wait()
    weigh_out(hidden_ref, weight_refs, gates, out_refs, experts, numbers_ref, 0)


def outputs_of(hidden, row_blocks, down, offsets, experts):
    blocks, slices = len(row_blocks), len(down)
    count, inner = hidden.shape
    depth = down[0].shape[1]
    tok_rows = row_blocks[0].shape[0]
    extra = -(-3 * experts // LANES) * LANES
    model = row_blocks[0].shape[1] - extra
    whole = pl.BlockSpec(memory_space=pltpu.VMEM)
    return pl.pallas_call(
        functools.partial(down_kernel, blocks, slices, experts, model),
        in_specs=[SMEM, whole] + [ANY] * blocks + [whole] * slices,
        out_specs=[whole] * blocks,
        out_shape=[jax.ShapeDtypeStruct((tok_rows, slices * depth), jnp.bfloat16)] * blocks,
        scratch_shapes=[pltpu.VMEM((count, extra), jnp.bfloat16), pltpu.SemaphoreType.DMA((blocks,))],
        compiler_params=pltpu.CompilerParams(vmem_limit_bytes=VMEM),
        cost_estimate=FREE,
    )(offsets, hidden, *row_blocks, *down)


def finish_kernel(mine, bases_ref, *refs):
    parts, sums, out_ref = refs[:mine], refs[mine:-1], refs[-1]
    for group, ref in enumerate(sums):
        columns = pl.ds(pl.multiple_of(bases_ref[group], LANES), ref.shape[1])
        total = ref[...].astype(jnp.float32)
        for part in parts:
            total += part[:, columns].astype(jnp.float32)
        out_ref[:, columns] = total.astype(jnp.bfloat16)


def shards(tokens, expert_ids, gate_weights, hot_ids, w_gate, w_up, w_down):
    del hot_ids
    tok_rows, model = tokens.shape
    places, lines = lax.axis_size("expert"), lax.axis_size("dp")
    layers = lines // 2
    half = layers // 2
    mirror = layers - 1
    local_count, depth = w_gate.shape[:2]
    experts = places * local_count
    assert local_count == 2 and half % 2 == 0

    def swap_layer(array, mask):
        return lax.ppermute(array, "dp", [(i, i ^ (2 * mask)) for i in range(lines)])

    def swap_core(array):
        return lax.ppermute(array, "dp", [(i, i ^ 1) for i in range(lines)])

    def swap_place(array, mask):
        return lax.ppermute(array, "expert", [(i, i ^ mask) for i in range(places)])

    line = lax.axis_index("dp")
    layer = line // 2
    parity = lax.rem(layer, 2)
    side = line // (lines // 2)
    here = lax.axis_index("expert") * local_count + side
    near, away = list(range(half)), list(range(half, layers))

    def pick(array, which):
        return lax.dynamic_index_in_dim(array, which, 0, keepdims=False)

    def numbers(values):
        return jnp.stack([jnp.asarray(v, jnp.int32) for v in values])

    def lines_of(masks):
        return [line ^ (2 * mask + core) for mask in masks for core in range(2)]

    def places_of(masks):
        first = [(layer - parity) ^ mask for mask in masks[::2]]
        return numbers([lax.rem(v, 4) * depth for v in lines_of(masks)] + [2 * v * depth for v in first])

    def both_cores(found, found_core, masks):
        return [piece for mask in masks for piece in (found[mask], found_core[mask])]

    block = jnp.concatenate([tokens, gate_columns(expert_ids, gate_weights, experts)], axis=1)
    far_block = swap_layer(block, mirror)
    own = [block] + [swap_place(block, mask) for mask in range(1, places)]

    singles = [1 << i for i in range(places.bit_length() - 1)]
    ready = after(side, block)
    mine, theirs = [jnp.concatenate([pick(w_gate, which), pick(w_up, which)], axis=1) for which in (ready, 1 - ready)]
    dn_mine, dn_theirs = pick(w_down, side), pick(w_down, 1 - side)
    gu, dn = {0: mine}, {0: dn_mine}
    for mask in near[1:]:
        gu[mask] = swap_layer(mine, mask)
    gu[mirror] = swap_layer(after(theirs, far_block, *[own[mask] for mask in singles]), mirror)
    far = [far_block] + [swap_place(after(far_block, own[mask]), mask) for mask in range(1, places)]
    for mask in near[1:]:
        dn[mask] = swap_layer(after(dn_mine, gu[mask]), mask)
    gu_core = {mask: swap_core(gu[mask]) for mask in near}
    pieces = both_cores(gu, gu_core, near)
    chunks = {"far": [far[i : i + 4] for i in range(0, places, 4)], "own": [own[i : i + 4] for i in range(0, places, 4)]}
    early = {"own": [early_sums(chunk, pieces, places_of(near)) for chunk in chunks["own"]]}
    settled = [*own[1:], *far[1:], *[dn[mask] for mask in near], *[sums for pair in early["own"] for sums in pair]]
    for mask in near[1:]:
        gu[mask ^ mirror] = swap_layer(after(gu[mirror], gu[mask], *settled), mask)
    dn[mirror] = swap_layer(after(dn_theirs, gu[mirror]), mirror)
    early["far"] = [early_sums(chunk, pieces, places_of(near)) for chunk in chunks["far"]]
    dn_core = {mask: swap_core(dn[mask]) for mask in near}
    settled = [sums for pair in early["far"] for sums in pair] + [dn_core[mask] for mask in near] + [dn[mirror]]
    for mask in away:
        gu_core[mask] = swap_core(after(gu[mask], *(settled if mask != mirror else ())))

    def arrived(parts):
        return [parts[0]] + [swap_place(parts[mask], mask) for mask in range(1, places)]

    def add_up(parts):
        total = parts[0].astype(jnp.float32)
        for part in parts[1:]:
            total += part.astype(jnp.float32)
        return total.astype(jnp.bfloat16)

    def late(key, masks):
        columns = [lax.rem(v, 2 * len(masks)) * depth for v in lines_of(masks)]
        counted = jnp.concatenate([places_of(away), numbers(columns + [here])])
        hidden, parts = [], []
        for chunk, sums in zip(chunks[key], early[key]):
            pieces = both_cores(gu, gu_core, away)
            rows, blocks = late_outputs(chunk, pieces, both_cores(dn, dn_core, masks), counted, sums, experts)
            hidden.append(rows)
            parts += blocks
        return hidden, parts

    far_hidden, far_parts = late("far", near)
    for mask in near[1:]:
        dn[mask ^ mirror] = swap_layer(after(dn[mirror], gu[mask ^ mirror], *[dn_core[other] for other in near]), mask)
    for mask in away:
        dn_core[mask] = swap_core(after(dn[mask], far_hidden[-1]))
    starts = numbers([lax.rem(v, 2 * len(away)) * depth for v in lines_of(away)] + [here])
    more_parts = []
    for chunk, rows in zip(chunks["far"], far_hidden):
        more_parts += outputs_of(rows, chunk, both_cores(dn, dn_core, away), starts, experts)
    sums = [swap_layer(add_up(arrived(parts)), mirror) for parts in (far_parts, more_parts)]
    mine = arrived(late("own", near + away)[1])
    width = model // 2
    bases = numbers([(1 - side) * width, side * width])
    whole = pl.BlockSpec(memory_space=pltpu.VMEM)
    return pl.pallas_call(
        functools.partial(finish_kernel, len(mine)),
        in_specs=[SMEM] + [whole] * (len(mine) + len(sums)),
        out_specs=whole,
        out_shape=jax.ShapeDtypeStruct((tok_rows, model), jnp.bfloat16),
        compiler_params=pltpu.CompilerParams(vmem_limit_bytes=VMEM),
    )(bases, *mine, *sums)


def solution(mesh):
    placed = (
        P(("dp", "expert"), None),
        P(("dp", "expert"), None),
        P(("dp", "expert"), None),
        P(),
        P("expert", "dp", None),
        P("expert", "dp", None),
        P("expert", None, "dp"),
    )
    return jax.shard_map(
        shards, mesh=mesh, in_specs=placed, out_specs=P(("dp", "expert"), None), check_vma=False
    )
```

time: 200 us -> 174 us (0.87)
  waiting for transfers between devices: 131 us -> 67.1 us
  starting transfers between devices: 18.6 us -> 51.3 us
  Pallas kernels: 27.3 us -> 37 us
  other arithmetic: 10.3 us -> 6.24 us
    ppermute x8 -> x9, waiting for transfers between devices: 95.6 us -> 53.4 us  [swap_layer(): return lax.ppermute(array, 'dp', [(i, i ^ 2 * mask) for i in range(lines)])]
    ppermute x8 -> x9, starting transfers between devices: 5.43 us -> 30.1 us  [swap_layer(): return lax.ppermute(array, 'dp', [(i, i ^ 2 * mask) for i in range(lines)])]
    ppermute x10 -> x15, waiting for transfers between devices: 35.8 us -> 13.6 us  [swap_place(): return lax.ppermute(array, 'expert', [(i, i ^ mask) for i in range(places)])]
    pallas_call x4 -> x6, Pallas kernels: 27.3 us -> 37 us  [the longest x2 18 us: late_outputs(): pl.pallas_call(functools.partial(late_kernel, blocks, slices, down_slices...]
    ppermute x10 -> x15, starting transfers between devices: 12.1 us -> 20.1 us  [swap_place(): return lax.ppermute(array, 'expert', [(i, i ^ mask) for i in range(places)])]
    slice x2 -> x0, local copies, waits for them, and re-layouts: 3.05 us -> none  [home(): parts[mask * tok_rows:(mask + 1) * tok_rows]]
    concatenate x3 -> x2, other arithmetic: 3.97 us -> 1.07 us  [shards(): jnp.concatenate([pick(w_gate, which), pick(w_up, which)], axis=1)]
    unnamed x29 -> x50, local copies, waits for them, and re-layouts: 5.33 us -> 4.11 us
  transfers between devices with their start and end apart: 26 -> 32, of which waited for: 10 -> 10; matrix products, arithmetic and copies ran while one was open for 6% -> 5% of each run, Pallas kernels for 11% -> 20%
where the time goes in v2:
time: 174 us; the launch traced here: 172 us
  waiting for transfers between devices  67.1 us (39%)
  starting transfers between devices  51.3 us (29%)
  Pallas kernels  37 us (21%)
  local copies, waits for them, and re-layouts  10.2 us (6%)
  other arithmetic  6.24 us (4%)
    ppermute x9, waiting for transfers between devices, swap_layer(): return lax.ppermute(array, 'dp', [(i, i ^ 2 * mask) for i in range(lines)])  53.4 us
    ppermute x9, starting transfers between devices, swap_layer(): return lax.ppermute(array, 'dp', [(i, i ^ 2 * mask) for i in range(lines)])  30.1 us
    ppermute x15, starting transfers between devices, swap_place(): return lax.ppermute(array, 'expert', [(i, i ^ mask) for i in range(places)])  20.1 us
    pallas_call x2, Pallas kernels, late_outputs(): pl.pallas_call(functools.partial(late_kernel, blocks, slices, down_slices...  18 us
    ppermute x15, waiting for transfers between devices, swap_place(): return lax.ppermute(array, 'expert', [(i, i ^ mask) for i in range(places)])  13.6 us
    pallas_call x2, Pallas kernels, early_sums(): pl.pallas_call(functools.partial(early_kernel, blocks, slices), grid=(til...  11.9 us
    pallas_call x1, Pallas kernels, outputs_of(): pl.pallas_call(functools.partial(down_kernel, blocks, slices, experts, mo...  4.32 us
    unnamed x50, local copies, waits for them, and re-layouts  4.11 us
  transfers between devices with their start and end apart: 32, of which 10 were waited for; matrix products, arithmetic and copies ran while one was open for 5% of the time, Pallas kernels for 20%

profile of v2, /device:TPU:16, one launch (start us, length us, event | category | flops | bytes accessed | tf_op | source)
XLA Modules:
  0.0 172.2 jit_solution(16102095153059582873)
XLA Ops:
  0.0 0.8 select_reduce_fusion
  0.8 0.1 copy.12
  0.9 1.1 fusion.1.refs_0_
  2.1 1.4 dynamic-slice_bitcast_fusion.2
  3.5 0.1 pad_maximum_fusion.1.refs_4_
  3.5 1.6 collective-permute-start.5
  5.2 0.0 collective-permute-start.3
  5.2 0.0 collective-permute-start.10
  5.2 1.5 collective-permute-start
  6.7 1.5 collective-permute-start.1
  8.2 15.8 %collective-permute-done.5.refs_6_ = bf16[256,1536]{1,0:T(8,128)(2,1)S(1)} collective-permute-done((bf16[256,1536]{1,0:T(8,128)(2,1)S(1)}, bf16[256,1536]{1,0:T(8,128)(2,1)S(1)}, u32[]{:S(2)}, u32[]{:S(2)}) %collective-permute-start.5) | collective-permute-done | bytes 786464 | tf_op jit(solution)/shard_map/ppermute | solution.py:266
  24.1 2.5 %collective-permute-start.2 = (bf16[128,2176]{1,0:T(8,128)(2,1)S(1)}, bf16[128,2176]{1,0:T(8,128)(2,1)S(1)}, u32[]{:S(2)}, u32[]{:S(2)}) collective-permute-start(bf16[128,2176]{1,0:T(8,128)(2,1)S(1)} %fusion.1.refs_0_), channel_id=1, source_target_pairs={{0,3},{1,2},{2,1},{3,0},{4,7},{5,6},{6,5},{7,4},{8,11},{9,10},{10,... | collective-permute-start | bytes 1671176 | tf_op jit(solution)/shard_map/ppermute | solution.py:272
  26.6 1.0 pad_maximum_fusion
  27.6 0.5 collective-permute-start.4
  28.1 0.5 collective-permute-start.6
  28.7 11.8 %collective-permute-done.2.refs_3_ = bf16[128,2176]{1,0:T(8,128)(2,1)S(1)} collective-permute-done((bf16[128,2176]{1,0:T(8,128)(2,1)S(1)}, bf16[128,2176]{1,0:T(8,128)(2,1)S(1)}, u32[]{:S(2)}, u32[]{:S(2)}) %collective-permute-start.2) | collective-permute-done | bytes 557088 | tf_op jit(solution)/shard_map/ppermute | solution.py:272
  40.5 1.5 collective-permute-start.7
  42.0 0.9 copy-done.7
  42.9 1.7 collective-permute-start.8
  44.6 2.1 %dynamic-slice_bitcast_fusion = (bf16[768,256]{1,0:T(8,128)(2,1)}, bf16[768,256]{1,0:T(8,128)(2,1)}) fusion(bf16[2,768,256]{2,1,0:T(8,128)(2,1)} %param.12, s32[]{:T(128)S(6)} %select_n.34, s32[]{:T(128)S(6)} %select_n.33), kind=kLoop, calls=%fused_computation.7 | loop fusion | bytes 1572872 | tf_op jit(solution)/shard_map/jit(dynamic_index_in_dim)/squeeze | solution.py:282
  46.7 12.4 %collective-permute-start.9 = (bf16[768,256]{1,0:T(8,128)(2,1)}, bf16[768,256]{1,0:T(8,128)(2,1)S(1)}, u32[]{:S(2)}, u32[]{:S(2)}) collective-permute-start(bf16[768,256]{1,0:T(8,128)(2,1)} %get-tuple-element.39.refs_8_), channel_id=1, source_target_pairs={{0,8},{4,12},{8,0},{12,4},{16,24},{20,28},{24,16},{28,20},{1,9},{5... | collective-permute-start | bytes 1179656 | tf_op jit(solution)/shard_map/ppermute | solution.py:266
  59.1 0.6 stack.115.numbers_ref
  59.7 6.0 %shard_map.64 = (f32[512,768]{1,0:T(8,128)}, f32[512,768]{1,0:T(8,128)}) custom-call(s32[5]{0:T(128)} %stack.115.numbers_ref, bf16[128,2176]{1,0:T(8,128)(2,1)} %copy-done.3, bf16[128,2176]{1,0:T(8,128)(2,1)} %copy-done.8, bf16[128,2176]{1,0:T(8,128)(2,1)} %copy-done.9, bf16[128,2176]{1,0:T(8,128)(2,1)} %copy-done.10, bf16[256,1536]{1,0:T(8,128)(2,1)} %copy-done, ...), custom_call_target="tpu_custom_call" | custom-call | tf_op jit(solution)/shard_map/pallas_call | solution.py:162
  65.7 0.7 collective-permute-done.7.refs_2_
  66.3 1.5 collective-permute-done.9.refs_10_
  67.9 0.7 collective-permute-done.4.refs_6_
  68.6 0.0 copy-done.11
  68.6 10.9 %collective-permute-start.12 = (bf16[256,1536]{1,0:T(8,128)(2,1)}, bf16[256,1536]{1,0:T(8,128)(2,1)S(1)}, u32[]{:S(2)}, u32[]{:S(2)}) collective-permute-start(bf16[256,1536]{1,0:T(8,128)(2,1)} %collective-permute-done.4.refs_6_), channel_id=1, source_target_pairs={{0,8},{4,12},{8,0},{12,4},{16,24},{20,28},{24,16},{28,20},{1,9},{5... | collective-permute-start | bytes 2359304 | tf_op jit(solution)/shard_map/ppermute | solution.py:266
  79.6 0.5 collective-permute-start.14
  80.1 0.0 collective-permute-start.17
  80.1 6.0 %shard_map.65 = (f32[512,768]{1,0:T(8,128)}, f32[512,768]{1,0:T(8,128)}) custom-call(s32[5]{0:T(128)} %stack.115.numbers_ref, bf16[128,2176]{1,0:T(8,128)(2,1)} %copy-done.1, bf16[128,2176]{1,0:T(8,128)(2,1)} %copy-done.2, bf16[128,2176]{1,0:T(8,128)(2,1)} %collective-permute-done.7.refs_2_, bf16[128,2176]{1,0:T(8,128)(2,1)} %collective-permute-done.8.refs_3_, ...), custom_call_target="tpu_custom_call" | custom-call | tf_op jit(solution)/shard_map/pallas_call | solution.py:162
  86.1 8.4 %collective-permute-done.15.refs_14_.refs_6_ = bf16[768,256]{1,0:T(8,128)(2,1)} collective-permute-done((bf16[768,256]{1,0:T(8,128)(2,1)}, bf16[768,256]{1,0:T(8,128)(2,1)}, u32[]{:S(2)}, u32[]{:S(2)}) %collective-permute-start.15) | collective-permute-done | bytes 393248 | tf_op jit(solution)/shard_map/ppermute | solution.py:266
  94.6 9.2 %collective-permute-done.12.refs_4_ = bf16[256,1536]{1,0:T(8,128)(2,1)S(1)} collective-permute-done((bf16[256,1536]{1,0:T(8,128)(2,1)}, bf16[256,1536]{1,0:T(8,128)(2,1)S(1)}, u32[]{:S(2)}, u32[]{:S(2)}) %collective-permute-start.12) | collective-permute-done | bytes 786464 | tf_op jit(solution)/shard_map/ppermute | solution.py:266
  103.8 2.4 %collective-permute-start.18 = (bf16[768,256]{1,0:T(8,128)(2,1)}, bf16[768,256]{1,0:T(8,128)(2,1)}, u32[]{:S(2)}, u32[]{:S(2)}) collective-permute-start(bf16[768,256]{1,0:T(8,128)(2,1)} %collective-permute-done.15.refs_14_.refs_6_), channel_id=1, source_target_pairs={{0,8},{4,12},{8,0},{12,4},{16,24},{20,28},{24,16},{28,20},{1,9},{5... | collective-permute-start | bytes 1179656 | tf_op jit(solution)/shard_map/ppermute | solution.py:266
  106.2 0.7 concatenate.23.numbers_ref
  106.9 0.9 copy-done.5
  107.8 8.3 %shard_map.66 = (bf16[512,768]{1,0:T(8,128)(2,1)}, bf16[128,1024]{1,0:T(8,128)(2,1)}, bf16[128,1024]{1,0:T(8,128)(2,1)}, bf16[128,1024]{1,0:T(8,128)(2,1)}, bf16[128,1024]{1,0:T(8,128)(2,1)}) custom-call(s32[10]{0:T(128)} %concatenate.23.numbers_ref, bf16[128,2176]{1,0:T(8,128)(2,1)} %copy-done.1, bf16[128,2176]{1,0:T(8,128)(2,1)} %copy-done.2, ...), custom_call_target="tpu_custom_call" | custom-call | tf_op jit(solution)/shard_map/pallas_call | solution.py:188
  116.1 0.2 collective-permute-start.20
  116.3 0.4 collective-permute-start.19
  116.7 1.5 collective-permute-start.24
  118.2 0.6 stack.116.numbers_ref
  118.8 1.5 collective-permute-start.25
  120.3 0.5 collective-permute-start.26
  120.8 0.8 copy-done.13
  121.6 0.8 copy-done.14
  122.3 4.3 %shard_map.68 = (bf16[128,1024]{1,0:T(8,128)(2,1)}, bf16[128,1024]{1,0:T(8,128)(2,1)}, bf16[128,1024]{1,0:T(8,128)(2,1)}, bf16[128,1024]{1,0:T(8,128)(2,1)}) custom-call(s32[5]{0:T(128)} %stack.116.numbers_ref, bf16[512,768]{1,0:T(8,128)(2,1)} %get-tuple-element.48.hidden_ref, bf16[128,2176]{1,0:T(8,128)(2,1)} %copy-done.1, bf16[128,2176]{1,0:T(8,128)(2,1)} %copy-done.2, ...), custom_call_target="tpu_custom_call" | custom-call | tf_op jit(solution)/shard_map/pallas_call | solution.py:233
  126.6 1.6 collective-permute-start.28
  128.2 1.5 collective-permute-start.29
  129.7 0.5 collective-permute-start.30
  130.2 0.7 concatenate.18.numbers_ref
  130.9 9.7 %shard_map.67 = (bf16[512,768]{1,0:T(8,128)(2,1)}, bf16[128,2048]{1,0:T(8,128)(2,1)}, bf16[128,2048]{1,0:T(8,128)(2,1)}, bf16[128,2048]{1,0:T(8,128)(2,1)}, bf16[128,2048]{1,0:T(8,128)(2,1)}) custom-call(s32[14]{0:T(128)} %concatenate.18.numbers_ref, bf16[128,2176]{1,0:T(8,128)(2,1)} %copy-done.3, bf16[128,2176]{1,0:T(8,128)(2,1)} %copy-done.8, ...), custom_call_target="tpu_custom_call" | custom-call | tf_op jit(solution)/shard_map/pallas_call | solution.py:188
  140.6 1.6 collective-permute-start.21
  142.2 1.5 collective-permute-start.22
  143.7 0.7 collective-permute-start.23
  144.4 1.3 add_convert_fusion.1
  145.7 1.4 collective-permute-start.27
  147.1 1.4 add_convert_fusion
  148.5 0.7 collective-permute-start.31
  149.2 0.7 pad_add_fusion.bases_ref
  149.8 15.4 %collective-permute-done.27.refs_4_ = bf16[128,1024]{1,0:T(8,128)(2,1)S(1)} collective-permute-done((bf16[128,1024]{1,0:T(8,128)(2,1)S(1)}, bf16[128,1024]{1,0:T(8,128)(2,1)S(1)}, u32[]{:S(2)}, u32[]{:S(2)}) %collective-permute-start.27) | collective-permute-done | bytes 262176 | tf_op jit(solution)/shard_map/ppermute | solution.py:266
  165.3 1.2 collective-permute-done.22.refs_2_
  166.4 2.3 %collective-permute-done.31.refs_5_ = bf16[128,1024]{1,0:T(8,128)(2,1)S(1)} collective-permute-done((bf16[128,1024]{1,0:T(8,128)(2,1)S(1)}, bf16[128,1024]{1,0:T(8,128)(2,1)S(1)}, u32[]{:S(2)}, u32[]{:S(2)}) %collective-permute-start.31) | collective-permute-done | bytes 262176 | tf_op jit(solution)/shard_map/ppermute | solution.py:266
  168.7 0.7 copy-done.24
  169.4 2.8 %shard_map.69 = bf16[128,2048]{1,0:T(8,128)(2,1)} custom-call(s32[2]{0:T(128)} %pad_add_fusion.bases_ref, bf16[128,2048]{1,0:T(8,128)(2,1)} %get-tuple-element.51.refs_0_, bf16[128,2048]{1,0:T(8,128)(2,1)} %copy-done.16, bf16[128,2048]{1,0:T(8,128)(2,1)} %copy-done.17, bf16[128,2048]{1,0:T(8,128)(2,1)} %copy-done.18, bf16[128,1024]{1,0:T(8,128)(2,1)} %copy-done.23, ...), custom_call_target="tpu_custom_call" | custom-call | tf_op jit(solution)/shard_map/pallas_call | solution.py:360
  (72 shorter events, 0.2 us)
Async XLA Ops:
  0.0 2.1 %copy-start.15 = (bf16[2,256,768]{2,1,0:T(8,128)(2,1)S(1)}, bf16[2,256,768]{2,1,0:T(8,128)(2,1)}, u32[]{:S(2)}) copy-start(bf16[2,256,768]{2,1,0:T(8,128)(2,1)} %param.11) | copy-start | bytes 2359300
  2.0 22.0 %copy-start.3 = (bf16[128,2176]{1,0:T(8,128)(2,1)}, bf16[128,2176]{1,0:T(8,128)(2,1)S(1)}, u32[]{:S(2)}) copy-start(bf16[128,2176]{1,0:T(8,128)(2,1)S(1)} %fusion.1.refs_0_) | copy-start | bytes 1671172
  3.5 43.1 %copy-start = (bf16[256,1536]{1,0:T(8,128)(2,1)}, bf16[256,1536]{1,0:T(8,128)(2,1)S(1)}, u32[]{:S(2)}) copy-start(bf16[256,1536]{1,0:T(8,128)(2,1)S(1)} %pad_maximum_fusion.1.refs_4_) | copy-start | bytes 2359300
  3.5 20.5 %collective-permute-start.5 = (bf16[256,1536]{1,0:T(8,128)(2,1)S(1)}, bf16[256,1536]{1,0:T(8,128)(2,1)S(1)}, u32[]{:S(2)}, u32[]{:S(2)}) collective-permute-start(bf16[256,1536]{1,0:T(8,128)(2,1)S(1)} %pad_maximum_fusion.1.refs_4_), channel_id=1, source_target_pairs={{0,8},{4,12},{8,0},{12,4},{16,24},{20,28},{24,16},{28,20},{1,9},{5... | collective-permute-start | bytes 2359304 | tf_op jit(solution)/shard_map/ppermute | solution.py:266
  5.2 18.9 %collective-permute-start.3 = (bf16[128,2176]{1,0:T(8,128)(2,1)S(1)}, bf16[128,2176]{1,0:T(8,128)(2,1)S(1)}, u32[]{:S(2)}, u32[]{:S(2)}) collective-permute-start(bf16[128,2176]{1,0:T(8,128)(2,1)S(1)} %fusion.1.refs_0_), channel_id=1, source_target_pairs={{0,24},{4,28},{8,16},{12,20},{16,8},{20,12},{24,0},{28,4},{1,25},{... | collective-permute-start | bytes 1671176 | tf_op jit(solution)/shard_map/ppermute | solution.py:266
  5.2 36.8 %collective-permute-start.10 = (bf16[256,1536]{1,0:T(8,128)(2,1)S(1)}, bf16[256,1536]{1,0:T(8,128)(2,1)S(1)}, u32[]{:S(2)}, u32[]{:S(2)}) collective-permute-start(bf16[256,1536]{1,0:T(8,128)(2,1)S(1)} %pad_maximum_fusion.1.refs_4_), channel_id=1, source_target_pairs={{0,4},{4,0},{8,12},{12,8},{16,20},{20,16},{24,28},{28,24},{1,5},{5... | collective-permute-start | bytes 2359304 | tf_op jit(solution)/shard_map/ppermute | solution.py:269
  5.2 22.4 %collective-permute-start = (bf16[128,2176]{1,0:T(8,128)(2,1)S(1)}, bf16[128,2176]{1,0:T(8,128)(2,1)S(1)}, u32[]{:S(2)}, u32[]{:S(2)}) collective-permute-start(bf16[128,2176]{1,0:T(8,128)(2,1)S(1)} %fusion.1.refs_0_), channel_id=1, source_target_pairs={{0,1},{1,0},{2,3},{3,2},{4,5},{5,4},{6,7},{7,6},{8,9},{9,8},{10,11... | collective-permute-start | bytes 1671176 | tf_op jit(solution)/shard_map/ppermute | solution.py:272
  6.7 20.9 %collective-permute-start.1 = (bf16[128,2176]{1,0:T(8,128)(2,1)S(1)}, bf16[128,2176]{1,0:T(8,128)(2,1)S(1)}, u32[]{:S(2)}, u32[]{:S(2)}) collective-permute-start(bf16[128,2176]{1,0:T(8,128)(2,1)S(1)} %fusion.1.refs_0_), channel_id=1, source_target_pairs={{0,2},{1,3},{2,0},{3,1},{4,6},{5,7},{6,4},{7,5},{8,10},{9,11},{10,... | collective-permute-start | bytes 1671176 | tf_op jit(solution)/shard_map/ppermute | solution.py:272
  24.0 22.6 %copy-start.6 = (bf16[256,1536]{1,0:T(8,128)(2,1)}, bf16[256,1536]{1,0:T(8,128)(2,1)S(1)}, u32[]{:S(2)}) copy-start(bf16[256,1536]{1,0:T(8,128)(2,1)S(1)} %collective-permute-done.5.refs_6_) | copy-start | bytes 2359300
  24.0 22.6 %collective-permute-start.11 = (bf16[256,1536]{1,0:T(8,128)(2,1)S(1)}, bf16[256,1536]{1,0:T(8,128)(2,1)}, u32[]{:S(2)}, u32[]{:S(2)}) collective-permute-start(bf16[256,1536]{1,0:T(8,128)(2,1)S(1)} %collective-permute-done.5.refs_6_), channel_id=1, source_target_pairs={{0,4},{4,0},{8,12},{12,8},{16,20},{20,16},{24,28},{28,24},{1,5},{5... | collective-permute-start | bytes 2359304 | tf_op jit(solution)/shard_map/ppermute | solution.py:269
  24.1 22.6 %copy-start.1 = (bf16[128,2176]{1,0:T(8,128)(2,1)}, bf16[128,2176]{1,0:T(8,128)(2,1)S(1)}, u32[]{:S(2)}) copy-start(bf16[128,2176]{1,0:T(8,128)(2,1)S(1)} %collective-permute-done.3.refs_0_) | copy-start | bytes 1671172
  24.1 16.4 %collective-permute-start.2 = (bf16[128,2176]{1,0:T(8,128)(2,1)S(1)}, bf16[128,2176]{1,0:T(8,128)(2,1)S(1)}, u32[]{:S(2)}, u32[]{:S(2)}) collective-permute-start(bf16[128,2176]{1,0:T(8,128)(2,1)S(1)} %fusion.1.refs_0_), channel_id=1, source_target_pairs={{0,3},{1,2},{2,1},{3,0},{4,7},{5,6},{6,5},{7,4},{8,11},{9,10},{10,... | collective-permute-start | bytes 1671176 | tf_op jit(solution)/shard_map/ppermute | solution.py:272
  27.6 14.4 %copy-start.8 = (bf16[128,2176]{1,0:T(8,128)(2,1)}, bf16[128,2176]{1,0:T(8,128)(2,1)S(1)}, u32[]{:S(2)}) copy-start(bf16[128,2176]{1,0:T(8,128)(2,1)S(1)} %collective-permute-done.refs_1_) | copy-start | bytes 1671172
  27.6 14.4 %copy-start.9 = (bf16[128,2176]{1,0:T(8,128)(2,1)}, bf16[128,2176]{1,0:T(8,128)(2,1)S(1)}, u32[]{:S(2)}) copy-start(bf16[128,2176]{1,0:T(8,128)(2,1)S(1)} %collective-permute-done.1.refs_2_) | copy-start | bytes 1671172
  27.6 41.0 %collective-permute-start.4 = (bf16[256,1536]{1,0:T(8,128)(2,1)}, bf16[256,1536]{1,0:T(8,128)(2,1)}, u32[]{:S(2)}, u32[]{:S(2)}) collective-permute-start(bf16[256,1536]{1,0:T(8,128)(2,1)} %pad_maximum_fusion), channel_id=1, source_target_pairs={{0,24},{4,28},{8,16},{12,20},{16,8},{20,12},{24,0},{28,4},{1,25},{... | collective-permute-start | bytes 2359304 | tf_op jit(solution)/shard_map/ppermute | solution.py:266
  28.1 37.5 %collective-permute-start.6 = (bf16[128,2176]{1,0:T(8,128)(2,1)S(1)}, bf16[128,2176]{1,0:T(8,128)(2,1)S(1)}, u32[]{:S(2)}, u32[]{:S(2)}) collective-permute-start(bf16[128,2176]{1,0:T(8,128)(2,1)S(1)} %collective-permute-done.3.refs_0_), channel_id=1, source_target_pairs={{0,1},{1,0},{2,3},{3,2},{4,5},{5,4},{6,7},{7,6},{8,9},{9,8},{10,11... | collective-permute-start | bytes 1671176 | tf_op jit(solution)/shard_map/ppermute | solution.py:272
  40.5 1.5 copy-start.10
  40.5 25.9 %collective-permute-start.7 = (bf16[128,2176]{1,0:T(8,128)(2,1)S(1)}, bf16[128,2176]{1,0:T(8,128)(2,1)}, u32[]{:S(2)}, u32[]{:S(2)}) collective-permute-start(bf16[128,2176]{1,0:T(8,128)(2,1)S(1)} %collective-permute-done.3.refs_0_), channel_id=1, source_target_pairs={{0,2},{1,3},{2,0},{3,1},{4,6},{5,7},{6,4},{7,5},{8,10},{9,11},{10,... | collective-permute-start | bytes 1671176 | tf_op jit(solution)/shard_map/ppermute | solution.py:272
  42.0 0.9 copy-start.7
  42.9 23.5 %collective-permute-start.8 = (bf16[128,2176]{1,0:T(8,128)(2,1)S(1)}, bf16[128,2176]{1,0:T(8,128)(2,1)}, u32[]{:S(2)}, u32[]{:S(2)}) collective-permute-start(bf16[128,2176]{1,0:T(8,128)(2,1)S(1)} %collective-permute-done.3.refs_0_), channel_id=1, source_target_pairs={{0,3},{1,2},{2,1},{3,0},{4,7},{5,6},{6,5},{7,4},{8,11},{9,10},{10,... | collective-permute-start | bytes 1671176 | tf_op jit(solution)/shard_map/ppermute | solution.py:272
  46.7 21.2 %collective-permute-start.9 = (bf16[768,256]{1,0:T(8,128)(2,1)}, bf16[768,256]{1,0:T(8,128)(2,1)S(1)}, u32[]{:S(2)}, u32[]{:S(2)}) collective-permute-start(bf16[768,256]{1,0:T(8,128)(2,1)} %get-tuple-element.39.refs_8_), channel_id=1, source_target_pairs={{0,8},{4,12},{8,0},{12,4},{16,24},{20,28},{24,16},{28,20},{1,9},{5... | collective-permute-start | bytes 1179656 | tf_op jit(solution)/shard_map/ppermute | solution.py:266
  65.7 14.4 %copy-start.2 = (bf16[128,2176]{1,0:T(8,128)(2,1)}, bf16[128,2176]{1,0:T(8,128)(2,1)S(1)}, u32[]{:S(2)}) copy-start(bf16[128,2176]{1,0:T(8,128)(2,1)S(1)} %collective-permute-done.6.refs_1_) | copy-start | bytes 1671172
  67.9 0.8 copy-start.11
  68.6 35.1 %collective-permute-start.12 = (bf16[256,1536]{1,0:T(8,128)(2,1)}, bf16[256,1536]{1,0:T(8,128)(2,1)S(1)}, u32[]{:S(2)}, u32[]{:S(2)}) collective-permute-start(bf16[256,1536]{1,0:T(8,128)(2,1)} %collective-permute-done.4.refs_6_), channel_id=1, source_target_pairs={{0,8},{4,12},{8,0},{12,4},{16,24},{20,28},{24,16},{28,20},{1,9},{5... | collective-permute-start | bytes 2359304 | tf_op jit(solution)/shard_map/ppermute | solution.py:266
  79.6 6.5 %collective-permute-start.13 = (bf16[768,256]{1,0:T(8,128)(2,1)}, bf16[768,256]{1,0:T(8,128)(2,1)S(1)}, u32[]{:S(2)}, u32[]{:S(2)}) collective-permute-start(bf16[768,256]{1,0:T(8,128)(2,1)} %get-tuple-element.39.refs_8_), channel_id=1, source_target_pairs={{0,4},{4,0},{8,12},{12,8},{16,20},{20,16},{24,28},{28,24},{1,5},{5... | collective-permute-start | bytes 1179656 | tf_op jit(solution)/shard_map/ppermute | solution.py:269
  79.6 6.5 %collective-permute-start.14 = (bf16[768,256]{1,0:T(8,128)(2,1)}, bf16[768,256]{1,0:T(8,128)(2,1)}, u32[]{:S(2)}, u32[]{:S(2)}) collective-permute-start(bf16[768,256]{1,0:T(8,128)(2,1)} %copy-done.11), channel_id=1, source_target_pairs={{0,4},{4,0},{8,12},{12,8},{16,20},{20,16},{24,28},{28,24},{1,5},{5... | collective-permute-start | bytes 1179656 | tf_op jit(solution)/shard_map/ppermute | solution.py:269
  80.1 14.5 %collective-permute-start.15 = (bf16[768,256]{1,0:T(8,128)(2,1)}, bf16[768,256]{1,0:T(8,128)(2,1)}, u32[]{:S(2)}, u32[]{:S(2)}) collective-permute-start(bf16[768,256]{1,0:T(8,128)(2,1)} %get-tuple-element.45), channel_id=1, source_target_pairs={{0,24},{4,28},{8,16},{12,20},{16,8},{20,12},{24,0},{28,4},{1,25},{... | collective-permute-start | bytes 1179656 | tf_op jit(solution)/shard_map/ppermute | solution.py:266
  80.1 26.8 %collective-permute-start.17 = (bf16[256,1536]{1,0:T(8,128)(2,1)}, bf16[256,1536]{1,0:T(8,128)(2,1)}, u32[]{:S(2)}, u32[]{:S(2)}) collective-permute-start(bf16[256,1536]{1,0:T(8,128)(2,1)} %collective-permute-done.4.refs_6_), channel_id=1, source_target_pairs={{0,4},{4,0},{8,12},{12,8},{16,20},{20,16},{24,28},{28,24},{1,5},{5... | collective-permute-start | bytes 2359304 | tf_op jit(solution)/shard_map/ppermute | solution.py:269
  86.1 17.7 %copy-start.12 = (bf16[768,256]{1,0:T(8,128)(2,1)}, bf16[768,256]{1,0:T(8,128)(2,1)S(1)}, u32[]{:S(2)}) copy-start(bf16[768,256]{1,0:T(8,128)(2,1)S(1)} %collective-permute-done.13.refs_9_) | copy-start | bytes 1179652
  103.8 3.1 %copy-start.4 = (bf16[256,1536]{1,0:T(8,128)(2,1)}, bf16[256,1536]{1,0:T(8,128)(2,1)S(1)}, u32[]{:S(2)}) copy-start(bf16[256,1536]{1,0:T(8,128)(2,1)S(1)} %collective-permute-done.12.refs_4_) | copy-start | bytes 2359300
  103.8 3.1 %collective-permute-start.16 = (bf16[256,1536]{1,0:T(8,128)(2,1)S(1)}, bf16[256,1536]{1,0:T(8,128)(2,1)S(1)}, u32[]{:S(2)}, u32[]{:S(2)}) collective-permute-start(bf16[256,1536]{1,0:T(8,128)(2,1)S(1)} %collective-permute-done.12.refs_4_), channel_id=1, source_target_pairs={{0,4},{4,0},{8,12},{12,8},{16,20},{20,16},{24,28},{28,24},{1,5},{5... | collective-permute-start | bytes 2359304 | tf_op jit(solution)/shard_map/ppermute | solution.py:269
  103.8 12.6 %collective-permute-start.18 = (bf16[768,256]{1,0:T(8,128)(2,1)}, bf16[768,256]{1,0:T(8,128)(2,1)}, u32[]{:S(2)}, u32[]{:S(2)}) collective-permute-start(bf16[768,256]{1,0:T(8,128)(2,1)} %collective-permute-done.15.refs_14_.refs_6_), channel_id=1, source_target_pairs={{0,8},{4,12},{8,0},{12,4},{16,24},{20,28},{24,16},{28,20},{1,9},{5... | collective-permute-start | bytes 1179656 | tf_op jit(solution)/shard_map/ppermute | solution.py:266
  106.9 0.9 copy-start.5
  116.1 4.7 %collective-permute-start.20 = (bf16[768,256]{1,0:T(8,128)(2,1)}, bf16[768,256]{1,0:T(8,128)(2,1)S(1)}, u32[]{:S(2)}, u32[]{:S(2)}) collective-permute-start(bf16[768,256]{1,0:T(8,128)(2,1)} %collective-permute-done.15.refs_14_.refs_6_), channel_id=1, source_target_pairs={{0,4},{4,0},{8,12},{12,8},{16,20},{20,16},{24,28},{28,24},{1,5},{5... | collective-permute-start | bytes 1179656 | tf_op jit(solution)/shard_map/ppermute | solution.py:269
  116.3 4.5 %collective-permute-start.19 = (bf16[768,256]{1,0:T(8,128)(2,1)}, bf16[768,256]{1,0:T(8,128)(2,1)S(1)}, u32[]{:S(2)}, u32[]{:S(2)}) collective-permute-start(bf16[768,256]{1,0:T(8,128)(2,1)} %collective-permute-done.18.refs_12_.refs_4_), channel_id=1, source_target_pairs={{0,4},{4,0},{8,12},{12,8},{16,20},{20,16},{24,28},{28,24},{1,5},{5... | collective-permute-start | bytes 1179656 | tf_op jit(solution)/shard_map/ppermute | solution.py:269
  116.7 13.0 %collective-permute-start.24 = (bf16[128,1024]{1,0:T(8,128)(2,1)}, bf16[128,1024]{1,0:T(8,128)(2,1)S(1)}, u32[]{:S(2)}, u32[]{:S(2)}) collective-permute-start(bf16[128,1024]{1,0:T(8,128)(2,1)} %get-tuple-element.56), channel_id=1, source_target_pairs={{0,1},{1,0},{2,3},{3,2},{4,5},{5,4},{6,7},{7,6},{8,9},{9,8},{10,11... | collective-permute-start | bytes 786440 | tf_op jit(solution)/shard_map/ppermute | solution.py:272
  118.8 21.8 %collective-permute-start.25 = (bf16[128,1024]{1,0:T(8,128)(2,1)}, bf16[128,1024]{1,0:T(8,128)(2,1)S(1)}, u32[]{:S(2)}, u32[]{:S(2)}) collective-permute-start(bf16[128,1024]{1,0:T(8,128)(2,1)} %get-tuple-element.57), channel_id=1, source_target_pairs={{0,2},{1,3},{2,0},{3,1},{4,6},{5,7},{6,4},{7,5},{8,10},{9,11},{10,... | collective-permute-start | bytes 786440 | tf_op jit(solution)/shard_map/ppermute | solution.py:272
  120.3 21.8 %collective-permute-start.26 = (bf16[128,1024]{1,0:T(8,128)(2,1)}, bf16[128,1024]{1,0:T(8,128)(2,1)S(1)}, u32[]{:S(2)}, u32[]{:S(2)}) collective-permute-start(bf16[128,1024]{1,0:T(8,128)(2,1)} %get-tuple-element.58), channel_id=1, source_target_pairs={{0,3},{1,2},{2,1},{3,0},{4,7},{5,6},{6,5},{7,4},{8,11},{9,10},{10,... | collective-permute-start | bytes 786440 | tf_op jit(solution)/shard_map/ppermute | solution.py:272
  120.8 0.8 copy-start.13
  121.6 0.8 copy-start.14
  126.6 17.0 %collective-permute-start.28 = (bf16[128,1024]{1,0:T(8,128)(2,1)}, bf16[128,1024]{1,0:T(8,128)(2,1)}, u32[]{:S(2)}, u32[]{:S(2)}) collective-permute-start(bf16[128,1024]{1,0:T(8,128)(2,1)} %get-tuple-element.60), channel_id=1, source_target_pairs={{0,1},{1,0},{2,3},{3,2},{4,5},{5,4},{6,7},{7,6},{8,9},{9,8},{10,11... | collective-permute-start | bytes 786440 | tf_op jit(solution)/shard_map/ppermute | solution.py:272
  128.2 17.5 %collective-permute-start.29 = (bf16[128,1024]{1,0:T(8,128)(2,1)}, bf16[128,1024]{1,0:T(8,128)(2,1)}, u32[]{:S(2)}, u32[]{:S(2)}) collective-permute-start(bf16[128,1024]{1,0:T(8,128)(2,1)} %get-tuple-element.61), channel_id=1, source_target_pairs={{0,2},{1,3},{2,0},{3,1},{4,6},{5,7},{6,4},{7,5},{8,10},{9,11},{10,... | collective-permute-start | bytes 786440 | tf_op jit(solution)/shard_map/ppermute | solution.py:272
  129.7 10.8 %copy-start.20 = (bf16[128,1024]{1,0:T(8,128)(2,1)}, bf16[128,1024]{1,0:T(8,128)(2,1)S(1)}, u32[]{:S(2)}) copy-start(bf16[128,1024]{1,0:T(8,128)(2,1)S(1)} %collective-permute-done.24) | copy-start | bytes 786436
  129.7 17.4 %collective-permute-start.30 = (bf16[128,1024]{1,0:T(8,128)(2,1)}, bf16[128,1024]{1,0:T(8,128)(2,1)}, u32[]{:S(2)}, u32[]{:S(2)}) collective-permute-start(bf16[128,1024]{1,0:T(8,128)(2,1)} %get-tuple-element.62), channel_id=1, source_target_pairs={{0,3},{1,2},{2,1},{3,0},{4,7},{5,6},{6,5},{7,4},{8,11},{9,10},{10,... | collective-permute-start | bytes 786440 | tf_op jit(solution)/shard_map/ppermute | solution.py:272
  130.9 13.5 %copy-start.19 = (bf16[128,1024]{1,0:T(8,128)(2,1)S(1)}, bf16[128,1024]{1,0:T(8,128)(2,1)}, u32[]{:S(2)}) copy-start(bf16[128,1024]{1,0:T(8,128)(2,1)} %get-tuple-element.55) | copy-start | bytes 786436
  140.6 3.1 %copy-start.21 = (bf16[128,1024]{1,0:T(8,128)(2,1)}, bf16[128,1024]{1,0:T(8,128)(2,1)S(1)}, u32[]{:S(2)}) copy-start(bf16[128,1024]{1,0:T(8,128)(2,1)S(1)} %collective-permute-done.25) | copy-start | bytes 786436
  140.6 24.7 %collective-permute-start.21 = (bf16[128,2048]{1,0:T(8,128)(2,1)}, bf16[128,2048]{1,0:T(8,128)(2,1)S(1)}, u32[]{:S(2)}, u32[]{:S(2)}) collective-permute-start(bf16[128,2048]{1,0:T(8,128)(2,1)} %get-tuple-element.52), channel_id=1, source_target_pairs={{0,1},{1,0},{2,3},{3,2},{4,5},{5,4},{6,7},{7,6},{8,9},{9,8},{10,11... | collective-permute-start | bytes 1572872 | tf_op jit(solution)/shard_map/ppermute | solution.py:272
  142.2 1.5 copy-start.22
  142.2 24.3 %collective-permute-start.22 = (bf16[128,2048]{1,0:T(8,128)(2,1)}, bf16[128,2048]{1,0:T(8,128)(2,1)S(1)}, u32[]{:S(2)}, u32[]{:S(2)}) collective-permute-start(bf16[128,2048]{1,0:T(8,128)(2,1)} %get-tuple-element.53), channel_id=1, source_target_pairs={{0,2},{1,3},{2,0},{3,1},{4,6},{5,7},{6,4},{7,5},{8,10},{9,11},{10,... | collective-permute-start | bytes 1572872 | tf_op jit(solution)/shard_map/ppermute | solution.py:272
  143.7 22.7 %collective-permute-start.23 = (bf16[128,2048]{1,0:T(8,128)(2,1)}, bf16[128,2048]{1,0:T(8,128)(2,1)S(1)}, u32[]{:S(2)}, u32[]{:S(2)}) collective-permute-start(bf16[128,2048]{1,0:T(8,128)(2,1)} %get-tuple-element.54), channel_id=1, source_target_pairs={{0,3},{1,2},{2,1},{3,0},{4,7},{5,6},{6,5},{7,4},{8,11},{9,10},{10,... | collective-permute-start | bytes 1572872 | tf_op jit(solution)/shard_map/ppermute | solution.py:272
  145.7 19.6 %collective-permute-start.27 = (bf16[128,1024]{1,0:T(8,128)(2,1)S(1)}, bf16[128,1024]{1,0:T(8,128)(2,1)S(1)}, u32[]{:S(2)}, u32[]{:S(2)}) collective-permute-start(bf16[128,1024]{1,0:T(8,128)(2,1)S(1)} %add_convert_fusion.1), channel_id=1, source_target_pairs={{0,24},{4,28},{8,16},{12,20},{16,8},{20,12},{24,0},{28,4},{1,25},{... | collective-permute-start | bytes 786440 | tf_op jit(solution)/shard_map/ppermute | solution.py:266
  148.5 20.3 %collective-permute-start.31 = (bf16[128,1024]{1,0:T(8,128)(2,1)S(1)}, bf16[128,1024]{1,0:T(8,128)(2,1)S(1)}, u32[]{:S(2)}, u32[]{:S(2)}) collective-permute-start(bf16[128,1024]{1,0:T(8,128)(2,1)S(1)} %add_convert_fusion), channel_id=1, source_target_pairs={{0,24},{4,28},{8,16},{12,20},{16,8},{20,12},{24,0},{28,4},{1,25},{... | collective-permute-start | bytes 786440 | tf_op jit(solution)/shard_map/ppermute | solution.py:266
  165.2 4.2 %copy-start.23 = (bf16[128,1024]{1,0:T(8,128)(2,1)}, bf16[128,1024]{1,0:T(8,128)(2,1)S(1)}, u32[]{:S(2)}) copy-start(bf16[128,1024]{1,0:T(8,128)(2,1)S(1)} %collective-permute-done.27.refs_4_) | copy-start | bytes 786436
  165.3 4.2 %copy-start.16 = (bf16[128,2048]{1,0:T(8,128)(2,1)}, bf16[128,2048]{1,0:T(8,128)(2,1)S(1)}, u32[]{:S(2)}) copy-start(bf16[128,2048]{1,0:T(8,128)(2,1)S(1)} %collective-permute-done.21.refs_1_) | copy-start | bytes 1572868
  166.4 3.0 %copy-start.17 = (bf16[128,2048]{1,0:T(8,128)(2,1)}, bf16[128,2048]{1,0:T(8,128)(2,1)S(1)}, u32[]{:S(2)}) copy-start(bf16[128,2048]{1,0:T(8,128)(2,1)S(1)} %collective-permute-done.22.refs_2_) | copy-start | bytes 1572868
  166.4 3.0 %copy-start.18 = (bf16[128,2048]{1,0:T(8,128)(2,1)}, bf16[128,2048]{1,0:T(8,128)(2,1)S(1)}, u32[]{:S(2)}) copy-start(bf16[128,2048]{1,0:T(8,128)(2,1)S(1)} %collective-permute-done.23.refs_3_) | copy-start | bytes 1572868
  168.7 0.7 copy-start.24

commit v3 on v2

--- a/solution.py
+++ b/solution.py
@@ -294,34 +294,41 @@
     def both_cores(found, found_core, masks):
         return [piece for mask in masks for piece in (found[mask], found_core[mask])]
 
+    singles = [1 << i for i in range(places.bit_length() - 1)]
+    others = [mask for mask in range(1, places) if mask not in singles]
     block = jnp.concatenate([tokens, gate_columns(expert_ids, gate_weights, experts)], axis=1)
-    far_block = swap_layer(block, mirror)
-    own = [block] + [swap_place(block, mask) for mask in range(1, places)]
-
-    singles = [1 << i for i in range(places.bit_length() - 1)]
-    ready = after(side, block)
-    mine, theirs = [jnp.concatenate([pick(w_gate, which), pick(w_up, which)], axis=1) for which in (ready, 1 - ready)]
-    dn_mine, dn_theirs = pick(w_down, side), pick(w_down, 1 - side)
-    gu, dn = {0: mine}, {0: dn_mine}
-    for mask in near[1:]:
-        gu[mask] = swap_layer(mine, mask)
-    gu[mirror] = swap_layer(after(theirs, far_block, *[own[mask] for mask in singles]), mirror)
-    far = [far_block] + [swap_place(after(far_block, own[mask]), mask) for mask in range(1, places)]
-    for mask in near[1:]:
-        dn[mask] = swap_layer(after(dn_mine, gu[mask]), mask)
-    gu_core = {mask: swap_core(gu[mask]) for mask in near}
+    dn = {0: pick(w_down, side)}
+    far = {0: swap_layer(block, mirror)}
+    own = {0: block, **{mask: swap_place(block, mask) for mask in range(1, places)}}
+    for mask in near[1:]:
+        dn[mask] = swap_layer(dn[0], mask)
+    wave = [far[0], *[own[mask] for mask in singles], *[dn[mask] for mask in near[1:]]]
+
+    mine, theirs = [jnp.concatenate([pick(w_gate, which), pick(w_up, which)], axis=1) for which in (side, 1 - side)]
+    gu = {0: mine, mirror: swap_layer(after(theirs, *wave), mirror)}
+    for mask in near[1:]:
+        gu[mask] = swap_layer(after(mine, *wave), mask)
+    for mask in singles:
+        far[mask] = swap_place(after(far[0], *wave), mask)
+    for mask in others:
+        far[mask] = swap_place(after(far[0], *wave), mask)
+    wave = [gu[mirror], *[gu[mask] for mask in near[1:]], *[far[mask] for mask in range(1, places)], *[own[mask] for mask in others]]
+
+    for mask in near[1:]:
+        gu[mask ^ mirror] = swap_layer(after(gu[mirror], *wave), mask)
+    dn[mirror] = swap_layer(after(pick(w_down, 1 - side), *wave), mirror)
+    gu_core = {mask: swap_core(after(gu[mask], *wave)) for mask in near + [mirror]}
     pieces = both_cores(gu, gu_core, near)
-    chunks = {"far": [far[i : i + 4] for i in range(0, places, 4)], "own": [own[i : i + 4] for i in range(0, places, 4)]}
-    early = {"own": [early_sums(chunk, pieces, places_of(near)) for chunk in chunks["own"]]}
-    settled = [*own[1:], *far[1:], *[dn[mask] for mask in near], *[sums for pair in early["own"] for sums in pair]]
-    for mask in near[1:]:
-        gu[mask ^ mirror] = swap_layer(after(gu[mirror], gu[mask], *settled), mask)
-    dn[mirror] = swap_layer(after(dn_theirs, gu[mirror]), mirror)
-    early["far"] = [early_sums(chunk, pieces, places_of(near)) for chunk in chunks["far"]]
-    dn_core = {mask: swap_core(dn[mask]) for mask in near}
-    settled = [sums for pair in early["far"] for sums in pair] + [dn_core[mask] for mask in near] + [dn[mirror]]
-    for mask in away:
-        gu_core[mask] = swap_core(after(gu[mask], *(settled if mask != mirror else ())))
+    chunks = {}
+    for key, found in (("far", far), ("own", own)):
+        blocks = [found[mask] for mask in range(places)]
+        chunks[key] = [blocks[i : i + 4] for i in range(0, places, 4)]
+    early = {key: [early_sums(chunk, pieces, places_of(near)) for chunk in chunks[key]] for key in ("own", "far")}
+    settled = {key: [sums for pair in early[key] for sums in pair] for key in early}
+    dn_core = {mask: swap_core(after(dn[mask], *settled["own"])) for mask in near}
+    wave = [*settled["far"], *[dn_core[mask] for mask in near], dn[mirror]]
+    for mask in near[1:]:
+        gu_core[mask ^ mirror] = swap_core(after(gu[mask ^ mirror], *wave))
 
     def arrived(parts):
         return [parts[0]] + [swap_place(parts[mask], mask) for mask in range(1, places)]

time: 174 us -> 165 us (0.948)
  starting transfers between devices: 51.3 us -> 38.7 us
  waiting for transfers between devices: 67.1 us -> 73.3 us
    ppermute x9, starting transfers between devices: 30.1 us -> 19.1 us  [swap_layer(): return lax.ppermute(array, 'dp', [(i, i ^ 2 * mask) for i in range(lines)])]
    ppermute x15, waiting for transfers between devices: 13.6 us -> 22.6 us  [swap_place(): return lax.ppermute(array, 'expert', [(i, i ^ mask) for i in range(places)])]
    ppermute x9, waiting for transfers between devices: 53.4 us -> 50.4 us  [swap_layer(): return lax.ppermute(array, 'dp', [(i, i ^ 2 * mask) for i in range(lines)])]
    squeeze x2, local copies, waits for them, and re-layouts: 3.47 us -> 0.9 us  [pick(): return lax.dynamic_index_in_dim(array, which, 0, keepdims=False)]
    ppermute x15, starting transfers between devices: 20.1 us -> 17.8 us  [swap_place(): return lax.ppermute(array, 'expert', [(i, i ^ mask) for i in range(places)])]
    unnamed x50 -> x56, local copies, waits for them, and re-layouts: 4.11 us -> 4.9 us
  transfers between devices with their start and end apart: 32 -> 32, of which waited for: 10 -> 11; matrix products, arithmetic and copies ran while one was open for 5% -> 4% of each run, Pallas kernels for 20% -> 21%
where the time goes in v3:
time: 165 us; the launch traced here: 163 us
  waiting for transfers between devices  73.3 us (44%)
  starting transfers between devices  38.7 us (23%)
  Pallas kernels  37 us (22%)
  local copies, waits for them, and re-layouts  8.57 us (5%)
  other arithmetic  5.29 us (3%)
    ppermute x9, waiting for transfers between devices, swap_layer(): return lax.ppermute(array, 'dp', [(i, i ^ 2 * mask) for i in range(lines)])  50.4 us
    ppermute x15, waiting for transfers between devices, swap_place(): return lax.ppermute(array, 'expert', [(i, i ^ mask) for i in range(places)])  22.6 us
    ppermute x9, starting transfers between devices, swap_layer(): return lax.ppermute(array, 'dp', [(i, i ^ 2 * mask) for i in range(lines)])  19.1 us
    pallas_call x2, Pallas kernels, late_outputs(): pl.pallas_call(functools.partial(late_kernel, blocks, slices, down_slices...  18 us
    ppermute x15, starting transfers between devices, swap_place(): return lax.ppermute(array, 'expert', [(i, i ^ mask) for i in range(places)])  17.8 us
    pallas_call x2, Pallas kernels, early_sums(): pl.pallas_call(functools.partial(early_kernel, blocks, slices), grid=(til...  11.9 us
    unnamed x56, local copies, waits for them, and re-layouts  4.9 us
    pallas_call x1, Pallas kernels, outputs_of(): pl.pallas_call(functools.partial(down_kernel, blocks, slices, experts, mo...  4.34 us
  transfers between devices with their start and end apart: 32, of which 11 were waited for; matrix products, arithmetic and copies ran while one was open for 4% of the time, Pallas kernels for 21%

profile of v3, /device:TPU:16, one launch (start us, length us, event | category | flops | bytes accessed | tf_op | source)
XLA Modules:
  0.0 163.1 jit_solution(4733664388117145952)
XLA Ops:
  0.0 0.8 select_reduce_fusion
  0.8 0.1 copy.12
  0.9 1.1 fusion.1.refs_0_
  2.0 0.5 collective-permute-start.3
  2.5 1.5 collective-permute-start
  4.0 1.5 collective-permute-start.1
  5.6 0.5 collective-permute-start.2
  6.0 0.8 dynamic-slice_bitcast_fusion
  6.8 1.2 collective-permute-start.4
  8.0 0.1 dynamic-slice_bitcast_fusion.1
  8.3 17.6 %collective-permute-done.4.refs_10_ = bf16[768,256]{1,0:T(8,128)(2,1)S(1)} collective-permute-done((bf16[768,256]{1,0:T(8,128)(2,1)S(1)}, bf16[768,256]{1,0:T(8,128)(2,1)S(1)}, u32[]{:S(2)}, u32[]{:S(2)}) %collective-permute-start.4) | collective-permute-done | bytes 393248 | tf_op jit(solution)/shard_map/ppermute | solution.py:266
  25.9 2.5 %collective-permute-done.3.refs_0_ = bf16[128,2176]{1,0:T(8,128)(2,1)S(1)} collective-permute-done((bf16[128,2176]{1,0:T(8,128)(2,1)S(1)}, bf16[128,2176]{1,0:T(8,128)(2,1)S(1)}, u32[]{:S(2)}, u32[]{:S(2)}) %collective-permute-start.3) | collective-permute-done | bytes 557088 | tf_op jit(solution)/shard_map/ppermute | solution.py:266
  28.4 1.4 collective-permute-done.1.refs_2_
  29.8 1.5 collective-permute-start.6
  31.3 2.6 %collective-permute-start.5 = (bf16[256,1536]{1,0:T(8,128)(2,1)S(1)}, bf16[256,1536]{1,0:T(8,128)(2,1)}, u32[]{:S(2)}, u32[]{:S(2)}) collective-permute-start(bf16[256,1536]{1,0:T(8,128)(2,1)S(1)} %pad_maximum_fusion), channel_id=1, source_target_pairs={{0,24},{4,28},{8,16},{12,20},{16,8},{20,12},{24,0},{28,4},{1,25},{... | collective-permute-start | bytes 2359304 | tf_op jit(solution)/shard_map/ppermute | solution.py:266
  33.8 2.1 %collective-permute-start.8 = (bf16[128,2176]{1,0:T(8,128)(2,1)S(1)}, bf16[128,2176]{1,0:T(8,128)(2,1)S(1)}, u32[]{:S(2)}, u32[]{:S(2)}) collective-permute-start(bf16[128,2176]{1,0:T(8,128)(2,1)S(1)} %collective-permute-done.3.refs_0_), channel_id=1, source_target_pairs={{0,2},{1,3},{2,0},{3,1},{4,6},{5,7},{6,4},{7,5},{8,10},{9,11},{10,... | collective-permute-start | bytes 1671176 | tf_op jit(solution)/shard_map/ppermute | solution.py:272
  35.9 1.4 collective-permute-start.9
  37.3 12.0 %collective-permute-done.7.refs_1_ = bf16[128,2176]{1,0:T(8,128)(2,1)S(1)} collective-permute-done((bf16[128,2176]{1,0:T(8,128)(2,1)S(1)}, bf16[128,2176]{1,0:T(8,128)(2,1)S(1)}, u32[]{:S(2)}, u32[]{:S(2)}) %collective-permute-start.7) | collective-permute-done | bytes 557088 | tf_op jit(solution)/shard_map/ppermute | solution.py:272
  49.4 7.2 %collective-permute-done.8.refs_2_ = bf16[128,2176]{1,0:T(8,128)(2,1)S(1)} collective-permute-done((bf16[128,2176]{1,0:T(8,128)(2,1)S(1)}, bf16[128,2176]{1,0:T(8,128)(2,1)S(1)}, u32[]{:S(2)}, u32[]{:S(2)}) %collective-permute-start.8) | collective-permute-done | bytes 557088 | tf_op jit(solution)/shard_map/ppermute | solution.py:272
  56.5 8.4 %collective-permute-done.5.refs_6_ = bf16[256,1536]{1,0:T(8,128)(2,1)} collective-permute-done((bf16[256,1536]{1,0:T(8,128)(2,1)S(1)}, bf16[256,1536]{1,0:T(8,128)(2,1)}, u32[]{:S(2)}, u32[]{:S(2)}) %collective-permute-start.5) | collective-permute-done | bytes 786464 | tf_op jit(solution)/shard_map/ppermute | solution.py:266
  64.9 0.5 collective-permute-start.11
  65.4 0.7 collective-permute-start.10
  66.1 0.6 stack.115.numbers_ref
  66.7 1.4 collective-permute-start.15
  68.1 0.3 collective-permute-done.11.refs_5_
  68.4 6.0 %shard_map.65 = (f32[512,768]{1,0:T(8,128)}, f32[512,768]{1,0:T(8,128)}) custom-call(s32[5]{0:T(128)} %stack.115.numbers_ref, bf16[128,2176]{1,0:T(8,128)(2,1)} %copy-done.5, bf16[128,2176]{1,0:T(8,128)(2,1)} %copy-done.9, bf16[128,2176]{1,0:T(8,128)(2,1)} %copy-done.10, bf16[128,2176]{1,0:T(8,128)(2,1)} %collective-permute-done.2.refs_3_, ...), custom_call_target="tpu_custom_call" | custom-call | tf_op jit(solution)/shard_map/pallas_call | solution.py:162
  74.4 0.2 collective-permute-start.14
  74.6 0.4 collective-permute-start.13
  75.0 0.1 collective-permute-start.17
  75.1 5.9 %shard_map.64 = (f32[512,768]{1,0:T(8,128)}, f32[512,768]{1,0:T(8,128)}) custom-call(s32[5]{0:T(128)} %stack.115.numbers_ref, bf16[128,2176]{1,0:T(8,128)(2,1)} %copy-done.1, bf16[128,2176]{1,0:T(8,128)(2,1)} %copy-done.2, bf16[128,2176]{1,0:T(8,128)(2,1)} %copy-done.3, bf16[128,2176]{1,0:T(8,128)(2,1)} %copy-done.4, bf16[256,1536]{1,0:T(8,128)(2,1)} %copy-done, ...), custom_call_target="tpu_custom_call" | custom-call | tf_op jit(solution)/shard_map/pallas_call | solution.py:162
  81.1 5.0 %collective-permute-done.10.refs_4_ = bf16[256,1536]{1,0:T(8,128)(2,1)} collective-permute-done((bf16[256,1536]{1,0:T(8,128)(2,1)}, bf16[256,1536]{1,0:T(8,128)(2,1)}, u32[]{:S(2)}, u32[]{:S(2)}) %collective-permute-start.10) | collective-permute-done | bytes 786464 | tf_op jit(solution)/shard_map/ppermute | solution.py:266
  86.1 0.8 copy-done.13
  86.9 9.1 %collective-permute-start.18 = (bf16[768,256]{1,0:T(8,128)(2,1)}, bf16[768,256]{1,0:T(8,128)(2,1)}, u32[]{:S(2)}, u32[]{:S(2)}) collective-permute-start(bf16[768,256]{1,0:T(8,128)(2,1)} %collective-permute-done.15.refs_14_.refs_6_), channel_id=1, source_target_pairs={{0,8},{4,12},{8,0},{12,4},{16,24},{20,28},{24,16},{28,20},{1,9},{5... | collective-permute-start | bytes 1179656 | tf_op jit(solution)/shard_map/ppermute | solution.py:266
  96.0 0.7 concatenate.23.numbers_ref
  96.7 0.9 copy-done.7
  97.6 0.9 copy-done.8
  98.5 8.3 %shard_map.66 = (bf16[512,768]{1,0:T(8,128)(2,1)}, bf16[128,1024]{1,0:T(8,128)(2,1)}, bf16[128,1024]{1,0:T(8,128)(2,1)}, bf16[128,1024]{1,0:T(8,128)(2,1)}, bf16[128,1024]{1,0:T(8,128)(2,1)}) custom-call(s32[10]{0:T(128)} %concatenate.23.numbers_ref, bf16[128,2176]{1,0:T(8,128)(2,1)} %copy-done.1, bf16[128,2176]{1,0:T(8,128)(2,1)} %copy-done.2, ...), custom_call_target="tpu_custom_call" | custom-call | tf_op jit(solution)/shard_map/pallas_call | solution.py:188
  106.8 0.3 collective-permute-start.20
  107.1 0.3 collective-permute-start.19
  107.4 1.5 collective-permute-start.24
  108.9 0.7 stack.116.numbers_ref
  109.6 1.5 collective-permute-start.25
  111.1 0.5 collective-permute-start.26
  111.6 0.8 copy-done.14
  112.3 0.7 copy-done.15
  113.1 4.3 %shard_map.68 = (bf16[128,1024]{1,0:T(8,128)(2,1)}, bf16[128,1024]{1,0:T(8,128)(2,1)}, bf16[128,1024]{1,0:T(8,128)(2,1)}, bf16[128,1024]{1,0:T(8,128)(2,1)}) custom-call(s32[5]{0:T(128)} %stack.116.numbers_ref, bf16[512,768]{1,0:T(8,128)(2,1)} %get-tuple-element.50.hidden_ref, bf16[128,2176]{1,0:T(8,128)(2,1)} %copy-done.1, bf16[128,2176]{1,0:T(8,128)(2,1)} %copy-done.2, ...), custom_call_target="tpu_custom_call" | custom-call | tf_op jit(solution)/shard_map/pallas_call | solution.py:233
  117.4 1.6 collective-permute-start.28
  119.0 1.5 collective-permute-start.29
  120.5 0.5 collective-permute-start.30
  121.0 0.7 concatenate.18.numbers_ref
  121.7 9.7 %shard_map.67 = (bf16[512,768]{1,0:T(8,128)(2,1)}, bf16[128,2048]{1,0:T(8,128)(2,1)}, bf16[128,2048]{1,0:T(8,128)(2,1)}, bf16[128,2048]{1,0:T(8,128)(2,1)}, bf16[128,2048]{1,0:T(8,128)(2,1)}) custom-call(s32[14]{0:T(128)} %concatenate.18.numbers_ref, bf16[128,2176]{1,0:T(8,128)(2,1)} %copy-done.5, bf16[128,2176]{1,0:T(8,128)(2,1)} %copy-done.9, ...), custom_call_target="tpu_custom_call" | custom-call | tf_op jit(solution)/shard_map/pallas_call | solution.py:188
  131.4 1.6 collective-permute-start.21
  133.0 1.5 collective-permute-start.22
  134.5 0.7 collective-permute-start.23
  135.1 1.3 add_convert_fusion.1
  136.4 1.5 collective-permute-start.27
  137.9 1.4 add_convert_fusion
  139.3 0.7 collective-permute-start.31
  140.0 0.7 pad_add_fusion.bases_ref
  140.6 14.7 %collective-permute-done.27.refs_4_ = bf16[128,1024]{1,0:T(8,128)(2,1)S(1)} collective-permute-done((bf16[128,1024]{1,0:T(8,128)(2,1)S(1)}, bf16[128,1024]{1,0:T(8,128)(2,1)S(1)}, u32[]{:S(2)}, u32[]{:S(2)}) %collective-permute-start.27) | collective-permute-done | bytes 262176 | tf_op jit(solution)/shard_map/ppermute | solution.py:266
  155.3 2.0 %collective-permute-done.22.refs_2_ = bf16[128,2048]{1,0:T(8,128)(2,1)S(1)} collective-permute-done((bf16[128,2048]{1,0:T(8,128)(2,1)}, bf16[128,2048]{1,0:T(8,128)(2,1)S(1)}, u32[]{:S(2)}, u32[]{:S(2)}) %collective-permute-start.22) | collective-permute-done | bytes 524320 | tf_op jit(solution)/shard_map/ppermute | solution.py:272
  157.3 2.3 %collective-permute-done.31.refs_5_ = bf16[128,1024]{1,0:T(8,128)(2,1)S(1)} collective-permute-done((bf16[128,1024]{1,0:T(8,128)(2,1)S(1)}, bf16[128,1024]{1,0:T(8,128)(2,1)S(1)}, u32[]{:S(2)}, u32[]{:S(2)}) %collective-permute-start.31) | collective-permute-done | bytes 262176 | tf_op jit(solution)/shard_map/ppermute | solution.py:266
  159.6 0.7 copy-done.27
  160.3 2.8 %shard_map.69 = bf16[128,2048]{1,0:T(8,128)(2,1)} custom-call(s32[2]{0:T(128)} %pad_add_fusion.bases_ref, bf16[128,2048]{1,0:T(8,128)(2,1)} %get-tuple-element.53.refs_0_, bf16[128,2048]{1,0:T(8,128)(2,1)} %copy-done.19, bf16[128,2048]{1,0:T(8,128)(2,1)} %copy-done.20, bf16[128,2048]{1,0:T(8,128)(2,1)} %copy-done.21, bf16[128,1024]{1,0:T(8,128)(2,1)} %copy-done.26, ...), custom_call_target="tpu_custom_call" | custom-call | tf_op jit(solution)/shard_map/pallas_call | solution.py:367
  (78 shorter events, 0.3 us)
Async XLA Ops:
  0.0 6.0 %copy-start.16 = (bf16[2,768,256]{2,1,0:T(8,128)(2,1)S(1)}, bf16[2,768,256]{2,1,0:T(8,128)(2,1)}, u32[]{:S(2)}) copy-start(bf16[2,768,256]{2,1,0:T(8,128)(2,1)} %param.12) | copy-start | bytes 2359300
  2.0 6.1 %copy-start.5 = (bf16[128,2176]{1,0:T(8,128)(2,1)}, bf16[128,2176]{1,0:T(8,128)(2,1)S(1)}, u32[]{:S(2)}) copy-start(bf16[128,2176]{1,0:T(8,128)(2,1)S(1)} %fusion.1.refs_0_) | copy-start | bytes 1671172
  2.0 26.4 %collective-permute-start.3 = (bf16[128,2176]{1,0:T(8,128)(2,1)S(1)}, bf16[128,2176]{1,0:T(8,128)(2,1)S(1)}, u32[]{:S(2)}, u32[]{:S(2)}) collective-permute-start(bf16[128,2176]{1,0:T(8,128)(2,1)S(1)} %fusion.1.refs_0_), channel_id=1, source_target_pairs={{0,24},{4,28},{8,16},{12,20},{16,8},{20,12},{24,0},{28,4},{1,25},{... | collective-permute-start | bytes 1671176 | tf_op jit(solution)/shard_map/ppermute | solution.py:266
  2.5 25.9 %collective-permute-start = (bf16[128,2176]{1,0:T(8,128)(2,1)S(1)}, bf16[128,2176]{1,0:T(8,128)(2,1)S(1)}, u32[]{:S(2)}, u32[]{:S(2)}) collective-permute-start(bf16[128,2176]{1,0:T(8,128)(2,1)S(1)} %fusion.1.refs_0_), channel_id=1, source_target_pairs={{0,1},{1,0},{2,3},{3,2},{4,5},{5,4},{6,7},{7,6},{8,9},{9,8},{10,11... | collective-permute-start | bytes 1671176 | tf_op jit(solution)/shard_map/ppermute | solution.py:272
  4.0 25.7 %collective-permute-start.1 = (bf16[128,2176]{1,0:T(8,128)(2,1)S(1)}, bf16[128,2176]{1,0:T(8,128)(2,1)S(1)}, u32[]{:S(2)}, u32[]{:S(2)}) collective-permute-start(bf16[128,2176]{1,0:T(8,128)(2,1)S(1)} %fusion.1.refs_0_), channel_id=1, source_target_pairs={{0,2},{1,3},{2,0},{3,1},{4,6},{5,7},{6,4},{7,5},{8,10},{9,11},{10,... | collective-permute-start | bytes 1671176 | tf_op jit(solution)/shard_map/ppermute | solution.py:272
  5.6 30.3 %collective-permute-start.2 = (bf16[128,2176]{1,0:T(8,128)(2,1)S(1)}, bf16[128,2176]{1,0:T(8,128)(2,1)}, u32[]{:S(2)}, u32[]{:S(2)}) collective-permute-start(bf16[128,2176]{1,0:T(8,128)(2,1)S(1)} %fusion.1.refs_0_), channel_id=1, source_target_pairs={{0,3},{1,2},{2,1},{3,0},{4,7},{5,6},{6,5},{7,4},{8,11},{9,10},{10,... | collective-permute-start | bytes 1671176 | tf_op jit(solution)/shard_map/ppermute | solution.py:272
  6.0 2.0 %copy-start.17 = (bf16[2,256,768]{2,1,0:T(8,128)(2,1)S(1)}, bf16[2,256,768]{2,1,0:T(8,128)(2,1)}, u32[]{:S(2)}) copy-start(bf16[2,256,768]{2,1,0:T(8,128)(2,1)} %param.11) | copy-start | bytes 2359300
  6.0 2.0 %copy-start.18 = (bf16[2,256,768]{2,1,0:T(8,128)(2,1)S(1)}, bf16[2,256,768]{2,1,0:T(8,128)(2,1)}, u32[]{:S(2)}) copy-start(bf16[2,256,768]{2,1,0:T(8,128)(2,1)} %param.10) | copy-start | bytes 2359300
  6.8 1.3 copy-start.6
  6.8 19.0 %collective-permute-start.4 = (bf16[768,256]{1,0:T(8,128)(2,1)S(1)}, bf16[768,256]{1,0:T(8,128)(2,1)S(1)}, u32[]{:S(2)}, u32[]{:S(2)}) collective-permute-start(bf16[768,256]{1,0:T(8,128)(2,1)S(1)} %get-tuple-element.45.refs_8_), channel_id=1, source_target_pairs={{0,8},{4,12},{8,0},{12,4},{16,24},{20,28},{24,16},{28,20},{1,9},{5... | collective-permute-start | bytes 1179656 | tf_op jit(solution)/shard_map/ppermute | solution.py:266
  8.2 60.2 %copy-start = (bf16[256,1536]{1,0:T(8,128)(2,1)}, bf16[256,1536]{1,0:T(8,128)(2,1)S(1)}, u32[]{:S(2)}) copy-start(bf16[256,1536]{1,0:T(8,128)(2,1)S(1)} %pad_maximum_fusion.1.refs_4_) | copy-start | bytes 2359300
  25.9 39.5 %copy-start.11 = (bf16[768,256]{1,0:T(8,128)(2,1)}, bf16[768,256]{1,0:T(8,128)(2,1)S(1)}, u32[]{:S(2)}) copy-start(bf16[768,256]{1,0:T(8,128)(2,1)S(1)} %collective-permute-done.4.refs_10_) | copy-start | bytes 1179652
  28.4 46.0 %copy-start.1 = (bf16[128,2176]{1,0:T(8,128)(2,1)}, bf16[128,2176]{1,0:T(8,128)(2,1)S(1)}, u32[]{:S(2)}) copy-start(bf16[128,2176]{1,0:T(8,128)(2,1)S(1)} %collective-permute-done.3.refs_0_) | copy-start | bytes 1671172
  28.4 5.4 %copy-start.9 = (bf16[128,2176]{1,0:T(8,128)(2,1)}, bf16[128,2176]{1,0:T(8,128)(2,1)S(1)}, u32[]{:S(2)}) copy-start(bf16[128,2176]{1,0:T(8,128)(2,1)S(1)} %collective-permute-done.refs_1_) | copy-start | bytes 1671172
  29.8 1.5 copy-start.10
  29.8 26.8 %collective-permute-start.6 = (bf16[256,1536]{1,0:T(8,128)(2,1)S(1)}, bf16[256,1536]{1,0:T(8,128)(2,1)}, u32[]{:S(2)}, u32[]{:S(2)}) collective-permute-start(bf16[256,1536]{1,0:T(8,128)(2,1)S(1)} %pad_maximum_fusion.1.refs_4_), channel_id=1, source_target_pairs={{0,8},{4,12},{8,0},{12,4},{16,24},{20,28},{24,16},{28,20},{1,9},{5... | collective-permute-start | bytes 2359304 | tf_op jit(solution)/shard_map/ppermute | solution.py:266
  31.3 33.6 %collective-permute-start.5 = (bf16[256,1536]{1,0:T(8,128)(2,1)S(1)}, bf16[256,1536]{1,0:T(8,128)(2,1)}, u32[]{:S(2)}, u32[]{:S(2)}) collective-permute-start(bf16[256,1536]{1,0:T(8,128)(2,1)S(1)} %pad_maximum_fusion), channel_id=1, source_target_pairs={{0,24},{4,28},{8,16},{12,20},{16,8},{20,12},{24,0},{28,4},{1,25},{... | collective-permute-start | bytes 2359304 | tf_op jit(solution)/shard_map/ppermute | solution.py:266
  33.8 15.5 %collective-permute-start.7 = (bf16[128,2176]{1,0:T(8,128)(2,1)S(1)}, bf16[128,2176]{1,0:T(8,128)(2,1)S(1)}, u32[]{:S(2)}, u32[]{:S(2)}) collective-permute-start(bf16[128,2176]{1,0:T(8,128)(2,1)S(1)} %collective-permute-done.3.refs_0_), channel_id=1, source_target_pairs={{0,1},{1,0},{2,3},{3,2},{4,5},{5,4},{6,7},{7,6},{8,9},{9,8},{10,11... | collective-permute-start | bytes 1671176 | tf_op jit(solution)/shard_map/ppermute | solution.py:272
  33.8 22.7 %collective-permute-start.8 = (bf16[128,2176]{1,0:T(8,128)(2,1)S(1)}, bf16[128,2176]{1,0:T(8,128)(2,1)S(1)}, u32[]{:S(2)}, u32[]{:S(2)}) collective-permute-start(bf16[128,2176]{1,0:T(8,128)(2,1)S(1)} %collective-permute-done.3.refs_0_), channel_id=1, source_target_pairs={{0,2},{1,3},{2,0},{3,1},{4,6},{5,7},{6,4},{7,5},{8,10},{9,11},{10,... | collective-permute-start | bytes 1671176 | tf_op jit(solution)/shard_map/ppermute | solution.py:272
  35.9 20.6 %collective-permute-start.9 = (bf16[128,2176]{1,0:T(8,128)(2,1)S(1)}, bf16[128,2176]{1,0:T(8,128)(2,1)S(1)}, u32[]{:S(2)}, u32[]{:S(2)}) collective-permute-start(bf16[128,2176]{1,0:T(8,128)(2,1)S(1)} %collective-permute-done.3.refs_0_), channel_id=1, source_target_pairs={{0,3},{1,2},{2,1},{3,0},{4,7},{5,6},{6,5},{7,4},{8,11},{9,10},{10,... | collective-permute-start | bytes 1671176 | tf_op jit(solution)/shard_map/ppermute | solution.py:272
  49.3 25.1 %copy-start.2 = (bf16[128,2176]{1,0:T(8,128)(2,1)}, bf16[128,2176]{1,0:T(8,128)(2,1)S(1)}, u32[]{:S(2)}) copy-start(bf16[128,2176]{1,0:T(8,128)(2,1)S(1)} %collective-permute-done.7.refs_1_) | copy-start | bytes 1671172
  56.5 8.4 %copy-start.3 = (bf16[128,2176]{1,0:T(8,128)(2,1)}, bf16[128,2176]{1,0:T(8,128)(2,1)S(1)}, u32[]{:S(2)}) copy-start(bf16[128,2176]{1,0:T(8,128)(2,1)S(1)} %collective-permute-done.8.refs_2_) | copy-start | bytes 1671172
  56.5 8.4 %copy-start.4 = (bf16[128,2176]{1,0:T(8,128)(2,1)}, bf16[128,2176]{1,0:T(8,128)(2,1)S(1)}, u32[]{:S(2)}) copy-start(bf16[128,2176]{1,0:T(8,128)(2,1)S(1)} %collective-permute-done.9.refs_3_) | copy-start | bytes 1671172
  64.9 3.2 %collective-permute-start.12 = (bf16[256,1536]{1,0:T(8,128)(2,1)}, bf16[256,1536]{1,0:T(8,128)(2,1)}, u32[]{:S(2)}, u32[]{:S(2)}) collective-permute-start(bf16[256,1536]{1,0:T(8,128)(2,1)} %collective-permute-done.6.refs_6_), channel_id=1, source_target_pairs={{0,4},{4,0},{8,12},{12,8},{16,20},{20,16},{24,28},{28,24},{1,5},{5... | collective-permute-start | bytes 2359304 | tf_op jit(solution)/shard_map/ppermute | solution.py:269
  64.9 3.5 %collective-permute-start.11 = (bf16[256,1536]{1,0:T(8,128)(2,1)S(1)}, bf16[256,1536]{1,0:T(8,128)(2,1)}, u32[]{:S(2)}, u32[]{:S(2)}) collective-permute-start(bf16[256,1536]{1,0:T(8,128)(2,1)S(1)} %pad_maximum_fusion.1.refs_4_), channel_id=1, source_target_pairs={{0,4},{4,0},{8,12},{12,8},{16,20},{20,16},{24,28},{28,24},{1,5},{5... | collective-permute-start | bytes 2359304 | tf_op jit(solution)/shard_map/ppermute | solution.py:269
  65.4 20.7 %collective-permute-start.10 = (bf16[256,1536]{1,0:T(8,128)(2,1)}, bf16[256,1536]{1,0:T(8,128)(2,1)}, u32[]{:S(2)}, u32[]{:S(2)}) collective-permute-start(bf16[256,1536]{1,0:T(8,128)(2,1)} %collective-permute-done.5.refs_6_), channel_id=1, source_target_pairs={{0,8},{4,12},{8,0},{12,4},{16,24},{20,28},{24,16},{28,20},{1,9},{5... | collective-permute-start | bytes 2359304 | tf_op jit(solution)/shard_map/ppermute | solution.py:266
  66.7 14.3 %collective-permute-start.15 = (bf16[768,256]{1,0:T(8,128)(2,1)}, bf16[768,256]{1,0:T(8,128)(2,1)}, u32[]{:S(2)}, u32[]{:S(2)}) collective-permute-start(bf16[768,256]{1,0:T(8,128)(2,1)} %get-tuple-element.47), channel_id=1, source_target_pairs={{0,24},{4,28},{8,16},{12,20},{16,8},{20,12},{24,0},{28,4},{1,25},{... | collective-permute-start | bytes 1179656 | tf_op jit(solution)/shard_map/ppermute | solution.py:266
  74.4 11.7 %collective-permute-start.14 = (bf16[768,256]{1,0:T(8,128)(2,1)}, bf16[768,256]{1,0:T(8,128)(2,1)S(1)}, u32[]{:S(2)}, u32[]{:S(2)}) collective-permute-start(bf16[768,256]{1,0:T(8,128)(2,1)} %copy-done.11), channel_id=1, source_target_pairs={{0,4},{4,0},{8,12},{12,8},{16,20},{20,16},{24,28},{28,24},{1,5},{5... | collective-permute-start | bytes 1179656 | tf_op jit(solution)/shard_map/ppermute | solution.py:269
  74.6 11.5 %collective-permute-start.13 = (bf16[768,256]{1,0:T(8,128)(2,1)}, bf16[768,256]{1,0:T(8,128)(2,1)S(1)}, u32[]{:S(2)}, u32[]{:S(2)}) collective-permute-start(bf16[768,256]{1,0:T(8,128)(2,1)} %copy-done.6), channel_id=1, source_target_pairs={{0,4},{4,0},{8,12},{12,8},{16,20},{20,16},{24,28},{28,24},{1,5},{5... | collective-permute-start | bytes 1179656 | tf_op jit(solution)/shard_map/ppermute | solution.py:269
  75.0 21.7 %collective-permute-start.17 = (bf16[256,1536]{1,0:T(8,128)(2,1)}, bf16[256,1536]{1,0:T(8,128)(2,1)S(1)}, u32[]{:S(2)}, u32[]{:S(2)}) collective-permute-start(bf16[256,1536]{1,0:T(8,128)(2,1)} %collective-permute-done.5.refs_6_), channel_id=1, source_target_pairs={{0,4},{4,0},{8,12},{12,8},{16,20},{20,16},{24,28},{28,24},{1,5},{5... | collective-permute-start | bytes 2359304 | tf_op jit(solution)/shard_map/ppermute | solution.py:269
  86.1 10.6 %copy-start.12 = (bf16[768,256]{1,0:T(8,128)(2,1)}, bf16[768,256]{1,0:T(8,128)(2,1)S(1)}, u32[]{:S(2)}) copy-start(bf16[768,256]{1,0:T(8,128)(2,1)S(1)} %collective-permute-done.14.refs_11_) | copy-start | bytes 1179652
  86.1 0.8 copy-start.13
  86.9 9.8 %collective-permute-start.16 = (bf16[256,1536]{1,0:T(8,128)(2,1)}, bf16[256,1536]{1,0:T(8,128)(2,1)S(1)}, u32[]{:S(2)}, u32[]{:S(2)}) collective-permute-start(bf16[256,1536]{1,0:T(8,128)(2,1)} %collective-permute-done.10.refs_4_), channel_id=1, source_target_pairs={{0,4},{4,0},{8,12},{12,8},{16,20},{20,16},{24,28},{28,24},{1,5},{5... | collective-permute-start | bytes 2359304 | tf_op jit(solution)/shard_map/ppermute | solution.py:269
  86.9 20.2 %collective-permute-start.18 = (bf16[768,256]{1,0:T(8,128)(2,1)}, bf16[768,256]{1,0:T(8,128)(2,1)}, u32[]{:S(2)}, u32[]{:S(2)}) collective-permute-start(bf16[768,256]{1,0:T(8,128)(2,1)} %collective-permute-done.15.refs_14_.refs_6_), channel_id=1, source_target_pairs={{0,8},{4,12},{8,0},{12,4},{16,24},{20,28},{24,16},{28,20},{1,9},{5... | collective-permute-start | bytes 1179656 | tf_op jit(solution)/shard_map/ppermute | solution.py:266
  96.7 0.9 copy-start.7
  97.6 0.9 copy-start.8
  106.8 4.7 %collective-permute-start.20 = (bf16[768,256]{1,0:T(8,128)(2,1)}, bf16[768,256]{1,0:T(8,128)(2,1)S(1)}, u32[]{:S(2)}, u32[]{:S(2)}) collective-permute-start(bf16[768,256]{1,0:T(8,128)(2,1)} %collective-permute-done.15.refs_14_.refs_6_), channel_id=1, source_target_pairs={{0,4},{4,0},{8,12},{12,8},{16,20},{20,16},{24,28},{28,24},{1,5},{5... | collective-permute-start | bytes 1179656 | tf_op jit(solution)/shard_map/ppermute | solution.py:269
  107.1 4.4 %collective-permute-start.19 = (bf16[768,256]{1,0:T(8,128)(2,1)}, bf16[768,256]{1,0:T(8,128)(2,1)S(1)}, u32[]{:S(2)}, u32[]{:S(2)}) collective-permute-start(bf16[768,256]{1,0:T(8,128)(2,1)} %collective-permute-done.18.refs_12_.refs_4_), channel_id=1, source_target_pairs={{0,4},{4,0},{8,12},{12,8},{16,20},{20,16},{24,28},{28,24},{1,5},{5... | collective-permute-start | bytes 1179656 | tf_op jit(solution)/shard_map/ppermute | solution.py:269
  107.4 13.1 %collective-permute-start.24 = (bf16[128,1024]{1,0:T(8,128)(2,1)}, bf16[128,1024]{1,0:T(8,128)(2,1)S(1)}, u32[]{:S(2)}, u32[]{:S(2)}) collective-permute-start(bf16[128,1024]{1,0:T(8,128)(2,1)} %get-tuple-element.58), channel_id=1, source_target_pairs={{0,1},{1,0},{2,3},{3,2},{4,5},{5,4},{6,7},{7,6},{8,9},{9,8},{10,11... | collective-permute-start | bytes 786440 | tf_op jit(solution)/shard_map/ppermute | solution.py:272
  109.6 21.8 %collective-permute-start.25 = (bf16[128,1024]{1,0:T(8,128)(2,1)}, bf16[128,1024]{1,0:T(8,128)(2,1)S(1)}, u32[]{:S(2)}, u32[]{:S(2)}) collective-permute-start(bf16[128,1024]{1,0:T(8,128)(2,1)} %get-tuple-element.59), channel_id=1, source_target_pairs={{0,2},{1,3},{2,0},{3,1},{4,6},{5,7},{6,4},{7,5},{8,10},{9,11},{10,... | collective-permute-start | bytes 786440 | tf_op jit(solution)/shard_map/ppermute | solution.py:272
  111.1 21.9 %collective-permute-start.26 = (bf16[128,1024]{1,0:T(8,128)(2,1)}, bf16[128,1024]{1,0:T(8,128)(2,1)S(1)}, u32[]{:S(2)}, u32[]{:S(2)}) collective-permute-start(bf16[128,1024]{1,0:T(8,128)(2,1)} %get-tuple-element.60), channel_id=1, source_target_pairs={{0,3},{1,2},{2,1},{3,0},{4,7},{5,6},{6,5},{7,4},{8,11},{9,10},{10,... | collective-permute-start | bytes 786440 | tf_op jit(solution)/shard_map/ppermute | solution.py:272
  111.6 0.8 copy-start.14
  112.3 0.7 copy-start.15
  117.4 17.0 %collective-permute-start.28 = (bf16[128,1024]{1,0:T(8,128)(2,1)}, bf16[128,1024]{1,0:T(8,128)(2,1)}, u32[]{:S(2)}, u32[]{:S(2)}) collective-permute-start(bf16[128,1024]{1,0:T(8,128)(2,1)} %get-tuple-element.62), channel_id=1, source_target_pairs={{0,1},{1,0},{2,3},{3,2},{4,5},{5,4},{6,7},{7,6},{8,9},{9,8},{10,11... | collective-permute-start | bytes 786440 | tf_op jit(solution)/shard_map/ppermute | solution.py:272
  119.0 17.4 %collective-permute-start.29 = (bf16[128,1024]{1,0:T(8,128)(2,1)}, bf16[128,1024]{1,0:T(8,128)(2,1)}, u32[]{:S(2)}, u32[]{:S(2)}) collective-permute-start(bf16[128,1024]{1,0:T(8,128)(2,1)} %get-tuple-element.63), channel_id=1, source_target_pairs={{0,2},{1,3},{2,0},{3,1},{4,6},{5,7},{6,4},{7,5},{8,10},{9,11},{10,... | collective-permute-start | bytes 786440 | tf_op jit(solution)/shard_map/ppermute | solution.py:272
  120.5 10.9 %copy-start.23 = (bf16[128,1024]{1,0:T(8,128)(2,1)}, bf16[128,1024]{1,0:T(8,128)(2,1)S(1)}, u32[]{:S(2)}) copy-start(bf16[128,1024]{1,0:T(8,128)(2,1)S(1)} %collective-permute-done.24) | copy-start | bytes 786436
  120.5 17.4 %collective-permute-start.30 = (bf16[128,1024]{1,0:T(8,128)(2,1)}, bf16[128,1024]{1,0:T(8,128)(2,1)}, u32[]{:S(2)}, u32[]{:S(2)}) collective-permute-start(bf16[128,1024]{1,0:T(8,128)(2,1)} %get-tuple-element.64), channel_id=1, source_target_pairs={{0,3},{1,2},{2,1},{3,0},{4,7},{5,6},{6,5},{7,4},{8,11},{9,10},{10,... | collective-permute-start | bytes 786440 | tf_op jit(solution)/shard_map/ppermute | solution.py:272
  121.7 13.5 %copy-start.22 = (bf16[128,1024]{1,0:T(8,128)(2,1)S(1)}, bf16[128,1024]{1,0:T(8,128)(2,1)}, u32[]{:S(2)}) copy-start(bf16[128,1024]{1,0:T(8,128)(2,1)} %get-tuple-element.57) | copy-start | bytes 786436
  131.4 3.1 %copy-start.24 = (bf16[128,1024]{1,0:T(8,128)(2,1)}, bf16[128,1024]{1,0:T(8,128)(2,1)S(1)}, u32[]{:S(2)}) copy-start(bf16[128,1024]{1,0:T(8,128)(2,1)S(1)} %collective-permute-done.25) | copy-start | bytes 786436
  131.4 23.9 %collective-permute-start.21 = (bf16[128,2048]{1,0:T(8,128)(2,1)}, bf16[128,2048]{1,0:T(8,128)(2,1)S(1)}, u32[]{:S(2)}, u32[]{:S(2)}) collective-permute-start(bf16[128,2048]{1,0:T(8,128)(2,1)} %get-tuple-element.54), channel_id=1, source_target_pairs={{0,1},{1,0},{2,3},{3,2},{4,5},{5,4},{6,7},{7,6},{8,9},{9,8},{10,11... | collective-permute-start | bytes 1572872 | tf_op jit(solution)/shard_map/ppermute | solution.py:272
  133.0 1.5 copy-start.25
  133.0 24.3 %collective-permute-start.22 = (bf16[128,2048]{1,0:T(8,128)(2,1)}, bf16[128,2048]{1,0:T(8,128)(2,1)S(1)}, u32[]{:S(2)}, u32[]{:S(2)}) collective-permute-start(bf16[128,2048]{1,0:T(8,128)(2,1)} %get-tuple-element.55), channel_id=1, source_target_pairs={{0,2},{1,3},{2,0},{3,1},{4,6},{5,7},{6,4},{7,5},{8,10},{9,11},{10,... | collective-permute-start | bytes 1572872 | tf_op jit(solution)/shard_map/ppermute | solution.py:272
  134.5 22.8 %collective-permute-start.23 = (bf16[128,2048]{1,0:T(8,128)(2,1)}, bf16[128,2048]{1,0:T(8,128)(2,1)S(1)}, u32[]{:S(2)}, u32[]{:S(2)}) collective-permute-start(bf16[128,2048]{1,0:T(8,128)(2,1)} %get-tuple-element.56), channel_id=1, source_target_pairs={{0,3},{1,2},{2,1},{3,0},{4,7},{5,6},{6,5},{7,4},{8,11},{9,10},{10,... | collective-permute-start | bytes 1572872 | tf_op jit(solution)/shard_map/ppermute | solution.py:272
  136.4 18.8 %collective-permute-start.27 = (bf16[128,1024]{1,0:T(8,128)(2,1)S(1)}, bf16[128,1024]{1,0:T(8,128)(2,1)S(1)}, u32[]{:S(2)}, u32[]{:S(2)}) collective-permute-start(bf16[128,1024]{1,0:T(8,128)(2,1)S(1)} %add_convert_fusion.1), channel_id=1, source_target_pairs={{0,24},{4,28},{8,16},{12,20},{16,8},{20,12},{24,0},{28,4},{1,25},{... | collective-permute-start | bytes 786440 | tf_op jit(solution)/shard_map/ppermute | solution.py:266
  139.3 20.3 %collective-permute-start.31 = (bf16[128,1024]{1,0:T(8,128)(2,1)S(1)}, bf16[128,1024]{1,0:T(8,128)(2,1)S(1)}, u32[]{:S(2)}, u32[]{:S(2)}) collective-permute-start(bf16[128,1024]{1,0:T(8,128)(2,1)S(1)} %add_convert_fusion), channel_id=1, source_target_pairs={{0,24},{4,28},{8,16},{12,20},{16,8},{20,12},{24,0},{28,4},{1,25},{... | collective-permute-start | bytes 786440 | tf_op jit(solution)/shard_map/ppermute | solution.py:266
  155.3 5.0 %copy-start.26 = (bf16[128,1024]{1,0:T(8,128)(2,1)}, bf16[128,1024]{1,0:T(8,128)(2,1)S(1)}, u32[]{:S(2)}) copy-start(bf16[128,1024]{1,0:T(8,128)(2,1)S(1)} %collective-permute-done.27.refs_4_) | copy-start | bytes 786436
  155.3 5.0 %copy-start.19 = (bf16[128,2048]{1,0:T(8,128)(2,1)}, bf16[128,2048]{1,0:T(8,128)(2,1)S(1)}, u32[]{:S(2)}) copy-start(bf16[128,2048]{1,0:T(8,128)(2,1)S(1)} %collective-permute-done.21.refs_1_) | copy-start | bytes 1572868
  157.3 3.0 %copy-start.20 = (bf16[128,2048]{1,0:T(8,128)(2,1)}, bf16[128,2048]{1,0:T(8,128)(2,1)S(1)}, u32[]{:S(2)}) copy-start(bf16[128,2048]{1,0:T(8,128)(2,1)S(1)} %collective-permute-done.22.refs_2_) | copy-start | bytes 1572868
  157.3 3.0 %copy-start.21 = (bf16[128,2048]{1,0:T(8,128)(2,1)}, bf16[128,2048]{1,0:T(8,128)(2,1)S(1)}, u32[]{:S(2)}) copy-start(bf16[128,2048]{1,0:T(8,128)(2,1)S(1)} %collective-permute-done.23.refs_3_) | copy-start | bytes 1572868
  159.6 0.7 copy-start.27

commit v4 on v3

--- a/solution.py
+++ b/solution.py
@@ -42,9 +42,9 @@
 
 
 def row_loads(loads, row_refs, rows, numbers_ref, slices, depth):
-    tok_rows, span = row_refs[0].shape[0], 4 * depth
+    tok_rows, span = row_refs[0].shape[0], 2 * depth
     copies = []
-    for j in range(slices // 4):
+    for j in range(slices // 2):
         columns = pl.ds(pl.multiple_of(numbers_ref[slices + j], LANES), span)
         for b, row_ref in enumerate(row_refs):
             target = rows.at[pl.ds(b * tok_rows, tok_rows), pl.ds(j * span, span)]
@@ -58,7 +58,7 @@
     for t in range(tiles):
         copies.append([])
         for k, weight_ref in enumerate(weight_refs):
-            place = pl.ds(pl.multiple_of((k // 4) * 4 * depth + numbers_ref[k], LANES), depth)
+            place = pl.ds(pl.multiple_of(numbers_ref[k], LANES), depth)
             for part in range(2):
                 source = weight_ref.at[:, pl.ds(part * (both // 2) + t * tile, tile)]
                 target = weights.at[t, place, pl.ds(part * tile, tile)]
@@ -134,7 +134,7 @@
     def _():
         for copy in final:
             copy.wait()
-        first_down = slices + slices // 4
+        first_down = slices + slices // 2
         weigh_out(hidden, [down.at[k] for k in range(down_slices)], gates, out_refs, experts, numbers_ref, first_down)
         hidden_out[...] = hidden[...]
 
@@ -168,9 +168,9 @@
         scratch_shapes=[
             pltpu.VMEM((count, slices * depth), jnp.bfloat16),
             pltpu.VMEM((tiles, slices * depth, 2 * tile), jnp.bfloat16),
-            pltpu.SemaphoreType.DMA((slices // 4 * blocks + 2 * tiles * slices,)),
+            pltpu.SemaphoreType.DMA((slices // 2 * blocks + 2 * tiles * slices,)),
         ],
-        compiler_params=pltpu.CompilerParams(vmem_limit_bytes=VMEM),
+        compiler_params=pltpu.CompilerParams(vmem_limit_bytes=62 * 1024 * 1024),
         cost_estimate=FREE,
     )(numbers, *row_blocks, *gate_up)
 
@@ -197,9 +197,9 @@
             pltpu.VMEM((count, inner), jnp.bfloat16),
             pltpu.VMEM((down_slices, inner, depth), jnp.bfloat16),
             pltpu.VMEM((count, extra), jnp.bfloat16),
-            pltpu.SemaphoreType.DMA((slices // 4 * blocks + 2 * tiles * slices + down_slices + blocks,)),
+            pltpu.SemaphoreType.DMA((slices // 2 * blocks + 2 * tiles * slices + down_slices + blocks,)),
         ],
-        compiler_params=pltpu.CompilerParams(vmem_limit_bytes=VMEM),
+        compiler_params=pltpu.CompilerParams(vmem_limit_bytes=62 * 1024 * 1024),
         cost_estimate=FREE,
     )(numbers, *row_blocks, *gate_up, *down, *early)
     return results[0], results[1:]
@@ -236,7 +236,7 @@
         out_specs=[whole] * blocks,
         out_shape=[jax.ShapeDtypeStruct((tok_rows, slices * depth), jnp.bfloat16)] * blocks,
         scratch_shapes=[pltpu.VMEM((count, extra), jnp.bfloat16), pltpu.SemaphoreType.DMA((blocks,))],
-        compiler_params=pltpu.CompilerParams(vmem_limit_bytes=VMEM),
+        compiler_params=pltpu.CompilerParams(vmem_limit_bytes=24 * 1024 * 1024),
         cost_estimate=FREE,
     )(offsets, hidden, *row_blocks, *down)
 
@@ -277,6 +277,7 @@
     side = line // (lines // 2)
     here = lax.axis_index("expert") * local_count + side
     near, away = list(range(half)), list(range(half, layers))
+    soon, last = near + [mirror], away[:-1]
 
     def pick(array, which):
         return lax.dynamic_index_in_dim(array, which, 0, keepdims=False)
@@ -288,8 +289,8 @@
         return [line ^ (2 * mask + core) for mask in masks for core in range(2)]
 
     def places_of(masks):
-        first = [(layer - parity) ^ mask for mask in masks[::2]]
-        return numbers([lax.rem(v, 4) * depth for v in lines_of(masks)] + [2 * v * depth for v in first])
+        first = [2 * (layer ^ mask) * depth for mask in masks]
+        return numbers([(2 * (k // 2) + lax.rem(v, 2)) * depth for k, v in enumerate(lines_of(masks))] + first)
 
     def both_cores(found, found_core, masks):
         return [piece for mask in masks for piece in (found[mask], found_core[mask])]
@@ -303,11 +304,12 @@
     for mask in near[1:]:
         dn[mask] = swap_layer(dn[0], mask)
     wave = [far[0], *[own[mask] for mask in singles], *[dn[mask] for mask in near[1:]]]
+    first = [far[0], *[dn[mask] for mask in near[1:]]]
 
     mine, theirs = [jnp.concatenate([pick(w_gate, which), pick(w_up, which)], axis=1) for which in (side, 1 - side)]
-    gu = {0: mine, mirror: swap_layer(after(theirs, *wave), mirror)}
-    for mask in near[1:]:
-        gu[mask] = swap_layer(after(mine, *wave), mask)
+    gu = {0: mine, mirror: swap_layer(after(theirs, *first), mirror)}
+    for mask in near[1:]:
+        gu[mask] = swap_layer(after(mine, *first), mask)
     for mask in singles:
         far[mask] = swap_place(after(far[0], *wave), mask)
     for mask in others:
@@ -318,12 +320,12 @@
         gu[mask ^ mirror] = swap_layer(after(gu[mirror], *wave), mask)
     dn[mirror] = swap_layer(after(pick(w_down, 1 - side), *wave), mirror)
     gu_core = {mask: swap_core(after(gu[mask], *wave)) for mask in near + [mirror]}
-    pieces = both_cores(gu, gu_core, near)
+    pieces = both_cores(gu, gu_core, soon)
     chunks = {}
     for key, found in (("far", far), ("own", own)):
         blocks = [found[mask] for mask in range(places)]
         chunks[key] = [blocks[i : i + 4] for i in range(0, places, 4)]
-    early = {key: [early_sums(chunk, pieces, places_of(near)) for chunk in chunks[key]] for key in ("own", "far")}
+    early = {key: [early_sums(chunk, pieces, places_of(soon)) for chunk in chunks[key]] for key in ("own", "far")}
     settled = {key: [sums for pair in early[key] for sums in pair] for key in early}
     dn_core = {mask: swap_core(after(dn[mask], *settled["own"])) for mask in near}
     wave = [*settled["far"], *[dn_core[mask] for mask in near], dn[mirror]]
@@ -341,10 +343,10 @@
 
     def late(key, masks):
         columns = [lax.rem(v, 2 * len(masks)) * depth for v in lines_of(masks)]
-        counted = jnp.concatenate([places_of(away), numbers(columns + [here])])
+        counted = jnp.concatenate([places_of(last), numbers(columns + [here])])
         hidden, parts = [], []
         for chunk, sums in zip(chunks[key], early[key]):
-            pieces = both_cores(gu, gu_core, away)
+            pieces = both_cores(gu, gu_core, last)
             rows, blocks = late_outputs(chunk, pieces, both_cores(dn, dn_core, masks), counted, sums, experts)
             hidden.append(rows)
             parts += blocks
@@ -369,7 +371,7 @@
         in_specs=[SMEM] + [whole] * (len(mine) + len(sums)),
         out_specs=whole,
         out_shape=jax.ShapeDtypeStruct((tok_rows, model), jnp.bfloat16),
-        compiler_params=pltpu.CompilerParams(vmem_limit_bytes=VMEM),
+        compiler_params=pltpu.CompilerParams(vmem_limit_bytes=16 * 1024 * 1024),
     )(bases, *mine, *sums)
 
 

time: 165 us -> 160 us (0.970)
  starting transfers between devices: 38.7 us -> 36.9 us
  Pallas kernels: 37 us -> 35.3 us
    ppermute x9, waiting for transfers between devices: 50.4 us -> 46.3 us  [swap_layer(): return lax.ppermute(array, 'dp', [(i, i ^ 2 * mask) for i in range(lines)])]
    ppermute x15, waiting for transfers between devices: 22.6 us -> 26 us  [swap_place(): return lax.ppermute(array, 'expert', [(i, i ^ mask) for i in range(places)])]
    pallas_call x2, Pallas kernels: 11.9 us -> 14.4 us  [early_sums(): pl.pallas_call(functools.partial(early_kernel, blocks, slices), grid=(til...]
    pallas_call x2, Pallas kernels: 18 us -> 16.1 us  [late_outputs(): pl.pallas_call(functools.partial(late_kernel, blocks, slices, down_slices...]
    unnamed x56 -> x48, local copies, waits for them, and re-layouts: 4.9 us -> 4.96 us
  transfers between devices with their start and end apart: 32 -> 32, of which waited for: 11 -> 14; matrix products, arithmetic and copies ran while one was open for 4% -> 4% of each run, Pallas kernels for 21% -> 21%
where the time goes in v4:
time: 160 us; the launch traced here: 159 us
  waiting for transfers between devices  73.6 us (46%)
  starting transfers between devices  36.9 us (23%)
  Pallas kernels  35.3 us (22%)
  local copies, waits for them, and re-layouts  7.98 us (5%)
  other arithmetic  5.25 us (3%)
    ppermute x9, waiting for transfers between devices, swap_layer(): return lax.ppermute(array, 'dp', [(i, i ^ 2 * mask) for i in range(lines)])  46.3 us
    ppermute x15, waiting for transfers between devices, swap_place(): return lax.ppermute(array, 'expert', [(i, i ^ mask) for i in range(places)])  26 us
    ppermute x9, starting transfers between devices, swap_layer(): return lax.ppermute(array, 'dp', [(i, i ^ 2 * mask) for i in range(lines)])  17.6 us
    ppermute x15, starting transfers between devices, swap_place(): return lax.ppermute(array, 'expert', [(i, i ^ mask) for i in range(places)])  17.6 us
    pallas_call x2, Pallas kernels, late_outputs(): pl.pallas_call(functools.partial(late_kernel, blocks, slices, down_slices...  16.1 us
    pallas_call x2, Pallas kernels, early_sums(): pl.pallas_call(functools.partial(early_kernel, blocks, slices), grid=(til...  14.4 us
    unnamed x48, local copies, waits for them, and re-layouts  4.96 us
  transfers between devices with their start and end apart: 32, of which 14 were waited for; matrix products, arithmetic and copies ran while one was open for 4% of the time, Pallas kernels for 21%

profile of v4, /device:TPU:16, one launch (start us, length us, event | category | flops | bytes accessed | tf_op | source)
XLA Modules:
  0.0 159.3 jit_solution(6413662417389541838)
XLA Ops:
  0.0 0.8 select_reduce_fusion
  0.8 0.1 copy.12
  0.9 1.1 fusion.1.refs_0_
  2.0 0.5 collective-permute-start.3
  2.5 2.4 %collective-permute-start.2 = (bf16[128,2176]{1,0:T(8,128)(2,1)S(1)}, bf16[128,2176]{1,0:T(8,128)(2,1)}, u32[]{:S(2)}, u32[]{:S(2)}) collective-permute-start(bf16[128,2176]{1,0:T(8,128)(2,1)S(1)} %fusion.1.refs_0_), channel_id=1, source_target_pairs={{0,3},{1,2},{2,1},{3,0},{4,7},{5,6},{6,5},{7,4},{8,11},{9,10},{10,... | collective-permute-start | bytes 1671176 | tf_op jit(solution)/shard_map/ppermute | solution.py:272
  5.0 0.5 collective-permute-start.1
  5.5 0.5 collective-permute-start
  6.0 0.8 dynamic-slice_bitcast_fusion
  6.8 1.2 collective-permute-start.4
  8.0 0.1 dynamic-slice_bitcast_fusion.1
  8.3 17.6 %collective-permute-done.4.refs_8_ = bf16[768,256]{1,0:T(8,128)(2,1)S(1)} collective-permute-done((bf16[768,256]{1,0:T(8,128)(2,1)S(1)}, bf16[768,256]{1,0:T(8,128)(2,1)S(1)}, u32[]{:S(2)}, u32[]{:S(2)}) %collective-permute-start.4) | collective-permute-done | bytes 393248 | tf_op jit(solution)/shard_map/ppermute | solution.py:266
  25.9 2.5 %collective-permute-done.3.refs_0_ = bf16[128,2176]{1,0:T(8,128)(2,1)S(1)} collective-permute-done((bf16[128,2176]{1,0:T(8,128)(2,1)S(1)}, bf16[128,2176]{1,0:T(8,128)(2,1)S(1)}, u32[]{:S(2)}, u32[]{:S(2)}) %collective-permute-start.3) | collective-permute-done | bytes 557088 | tf_op jit(solution)/shard_map/ppermute | solution.py:266
  28.4 0.4 collective-permute-start.5
  28.9 0.6 collective-permute-done.1.refs_2_
  29.5 0.8 copy-done.15
  30.3 0.8 copy-done.16
  31.1 1.8 %collective-permute-start.9 = (bf16[128,2176]{1,0:T(8,128)(2,1)S(1)}, bf16[128,2176]{1,0:T(8,128)(2,1)S(1)}, u32[]{:S(2)}, u32[]{:S(2)}) collective-permute-start(bf16[128,2176]{1,0:T(8,128)(2,1)S(1)} %collective-permute-done.3.refs_0_), channel_id=1, source_target_pairs={{0,3},{1,2},{2,1},{3,0},{4,7},{5,6},{6,5},{7,4},{8,11},{9,10},{10,... | collective-permute-start | bytes 1671176 | tf_op jit(solution)/shard_map/ppermute | solution.py:272
  33.0 1.1 collective-permute-start.8
  34.1 0.5 collective-permute-start.7
  34.6 12.9 %collective-permute-done.9.refs_3_ = bf16[128,2176]{1,0:T(8,128)(2,1)S(1)} collective-permute-done((bf16[128,2176]{1,0:T(8,128)(2,1)S(1)}, bf16[128,2176]{1,0:T(8,128)(2,1)S(1)}, u32[]{:S(2)}, u32[]{:S(2)}) %collective-permute-start.9) | collective-permute-done | bytes 557088 | tf_op jit(solution)/shard_map/ppermute | solution.py:272
  47.6 11.0 %collective-permute-done.8.refs_2_ = bf16[128,2176]{1,0:T(8,128)(2,1)S(1)} collective-permute-done((bf16[128,2176]{1,0:T(8,128)(2,1)S(1)}, bf16[128,2176]{1,0:T(8,128)(2,1)S(1)}, u32[]{:S(2)}, u32[]{:S(2)}) %collective-permute-start.8) | collective-permute-done | bytes 557088 | tf_op jit(solution)/shard_map/ppermute | solution.py:272
  58.5 0.1 collective-permute-done.7.refs_1_
  58.6 0.9 copy-done.6
  59.5 4.2 %collective-permute-done.5.refs_8_ = bf16[256,1536]{1,0:T(8,128)(2,1)} collective-permute-done((bf16[256,1536]{1,0:T(8,128)(2,1)S(1)}, bf16[256,1536]{1,0:T(8,128)(2,1)}, u32[]{:S(2)}, u32[]{:S(2)}) %collective-permute-start.5) | collective-permute-done | bytes 786464 | tf_op jit(solution)/shard_map/ppermute | solution.py:266
  63.8 0.5 collective-permute-start.11
  64.4 1.2 collective-permute-start.10
  65.5 0.7 stack.141.numbers_ref
  66.2 1.2 collective-permute-start.16
  67.4 0.7 collective-permute-done.11.refs_5_
  68.1 0.6 collective-permute-done.12.refs_7_
  68.6 7.2 %shard_map.65 = (f32[512,768]{1,0:T(8,128)}, f32[512,768]{1,0:T(8,128)}) custom-call(s32[9]{0:T(128)} %stack.141.numbers_ref, bf16[128,2176]{1,0:T(8,128)(2,1)} %copy-done.13, bf16[128,2176]{1,0:T(8,128)(2,1)} %copy-done.16, bf16[128,2176]{1,0:T(8,128)(2,1)} %copy-done.15, bf16[128,2176]{1,0:T(8,128)(2,1)} %collective-permute-done.2.refs_3_, ...), custom_call_target="tpu_custom_call" | custom-call | tf_op jit(solution)/shard_map/pallas_call | solution.py:162
  75.9 0.2 collective-permute-start.14
  76.1 0.4 collective-permute-start.15
  76.4 7.2 %shard_map.64 = (f32[512,768]{1,0:T(8,128)}, f32[512,768]{1,0:T(8,128)}) custom-call(s32[9]{0:T(128)} %stack.141.numbers_ref, bf16[128,2176]{1,0:T(8,128)(2,1)} %copy-done, bf16[128,2176]{1,0:T(8,128)(2,1)} %copy-done.6, bf16[128,2176]{1,0:T(8,128)(2,1)} %copy-done.4, bf16[128,2176]{1,0:T(8,128)(2,1)} %copy-done.2, bf16[256,1536]{1,0:T(8,128)(2,1)} %copy-done.12, ...), custom_call_target="tpu_custom_call" | custom-call | tf_op jit(solution)/shard_map/pallas_call | solution.py:162
  83.6 1.4 collective-permute-done.10.refs_4_
  85.0 0.1 collective-permute-start.17
  85.1 11.0 %collective-permute-start.18 = (bf16[768,256]{1,0:T(8,128)(2,1)}, bf16[768,256]{1,0:T(8,128)(2,1)}, u32[]{:S(2)}, u32[]{:S(2)}) collective-permute-start(bf16[768,256]{1,0:T(8,128)(2,1)} %collective-permute-done.16.refs_12_.refs_6_), channel_id=1, source_target_pairs={{0,8},{4,12},{8,0},{12,4},{16,24},{20,28},{24,16},{28,20},{1,9},{5... | collective-permute-start | bytes 1179656 | tf_op jit(solution)/shard_map/ppermute | solution.py:266
  96.1 0.6 concatenate.23.numbers_ref
  96.7 7.4 %shard_map.66 = (bf16[512,768]{1,0:T(8,128)(2,1)}, bf16[128,1024]{1,0:T(8,128)(2,1)}, bf16[128,1024]{1,0:T(8,128)(2,1)}, bf16[128,1024]{1,0:T(8,128)(2,1)}, bf16[128,1024]{1,0:T(8,128)(2,1)}) custom-call(s32[8]{0:T(128)} %concatenate.23.numbers_ref, bf16[128,2176]{1,0:T(8,128)(2,1)} %copy-done, bf16[128,2176]{1,0:T(8,128)(2,1)} %copy-done.6, ...), custom_call_target="tpu_custom_call" | custom-call | tf_op jit(solution)/shard_map/pallas_call | solution.py:188
  104.2 1.9 %collective-permute-done.18.refs_10_.refs_4_ = bf16[768,256]{1,0:T(8,128)(2,1)} collective-permute-done((bf16[768,256]{1,0:T(8,128)(2,1)}, bf16[768,256]{1,0:T(8,128)(2,1)}, u32[]{:S(2)}, u32[]{:S(2)}) %collective-permute-start.18) | collective-permute-done | bytes 393248 | tf_op jit(solution)/shard_map/ppermute | solution.py:266
  106.1 0.5 collective-permute-start.20
  106.6 1.5 collective-permute-start.24
  108.1 0.1 stack.150.numbers_ref
  108.2 1.5 collective-permute-start.25
  109.7 0.5 collective-permute-start.26
  110.2 1.2 copy-done.7
  111.4 1.1 copy-done.10
  112.5 3.1 %shard_map.68 = (bf16[128,1024]{1,0:T(8,128)(2,1)S(1)}, bf16[128,1024]{1,0:T(8,128)(2,1)}, bf16[128,1024]{1,0:T(8,128)(2,1)}, bf16[128,1024]{1,0:T(8,128)(2,1)}) custom-call(s32[5]{0:T(128)S(1)} %stack.150.numbers_ref, bf16[512,768]{1,0:T(8,128)(2,1)S(1)} %copy-done.10, bf16[128,2176]{1,0:T(8,128)(2,1)S(1)} %copy-done.1, bf16[128,2176]{1,0:T(8,128)(2,1)S(1)} %copy-done.7, ...), custom_call_target="tpu_custom_call" | custom-call | tf_op jit(solution)/shard_map/pallas_call | solution.py:233
  115.7 1.6 collective-permute-start.28
  117.3 1.5 collective-permute-start.29
  118.8 0.5 collective-permute-start.30
  119.3 0.6 concatenate.18.numbers_ref
  119.9 8.7 %shard_map.67 = (bf16[512,768]{1,0:T(8,128)(2,1)}, bf16[128,2048]{1,0:T(8,128)(2,1)}, bf16[128,2048]{1,0:T(8,128)(2,1)}, bf16[128,2048]{1,0:T(8,128)(2,1)}, bf16[128,2048]{1,0:T(8,128)(2,1)}) custom-call(s32[12]{0:T(128)} %concatenate.18.numbers_ref, bf16[128,2176]{1,0:T(8,128)(2,1)} %copy-done.13, bf16[128,2176]{1,0:T(8,128)(2,1)} %copy-done.16, ...), custom_call_target="tpu_custom_call" | custom-call | tf_op jit(solution)/shard_map/pallas_call | solution.py:188
  128.6 1.6 collective-permute-start.21
  130.2 1.5 collective-permute-start.22
  131.7 0.5 collective-permute-start.23
  132.2 2.0 %add_convert_fusion.1 = bf16[128,1024]{1,0:T(8,128)(2,1)} fusion(bf16[128,1024]{1,0:T(8,128)(2,1)} %collective-permute-done.26, bf16[128,1024]{1,0:T(8,128)(2,1)} %collective-permute-done.25, bf16[128,1024]{1,0:T(8,128)(2,1)} %collective-permute-done.24, bf16[128,1024]{1,0:T(8,128)(2,1)S(1)} %copy-done.23), kind=kLoop, calls=%fused_computation.6 | loop fusion | flops 1048576 | bytes 1310720 | tf_op jit(solution)/shard_map/convert_element_type | solution.py:342
  134.2 1.2 add_convert_fusion
  135.4 2.1 %collective-permute-start.31 = (bf16[128,1024]{1,0:T(8,128)(2,1)S(1)}, bf16[128,1024]{1,0:T(8,128)(2,1)S(1)}, u32[]{:S(2)}, u32[]{:S(2)}) collective-permute-start(bf16[128,1024]{1,0:T(8,128)(2,1)S(1)} %add_convert_fusion), channel_id=1, source_target_pairs={{0,24},{4,28},{8,16},{12,20},{16,8},{20,12},{24,0},{28,4},{1,25},{... | collective-permute-start | bytes 786440 | tf_op jit(solution)/shard_map/ppermute | solution.py:266
  137.5 0.1 pad_add_fusion.bases_ref
  137.5 16.7 %collective-permute-done.27.refs_4_ = bf16[128,1024]{1,0:T(8,128)(2,1)S(1)} collective-permute-done((bf16[128,1024]{1,0:T(8,128)(2,1)}, bf16[128,1024]{1,0:T(8,128)(2,1)S(1)}, u32[]{:S(2)}, u32[]{:S(2)}) %collective-permute-start.27) | collective-permute-done | bytes 262176 | tf_op jit(solution)/shard_map/ppermute | solution.py:266
  154.3 1.4 collective-permute-done.22.refs_2_
  155.7 2.0 %collective-permute-done.31.refs_5_ = bf16[128,1024]{1,0:T(8,128)(2,1)S(1)} collective-permute-done((bf16[128,1024]{1,0:T(8,128)(2,1)S(1)}, bf16[128,1024]{1,0:T(8,128)(2,1)S(1)}, u32[]{:S(2)}, u32[]{:S(2)}) %collective-permute-start.31) | collective-permute-done | bytes 262176 | tf_op jit(solution)/shard_map/ppermute | solution.py:266
  157.6 1.7 %shard_map.69 = bf16[128,2048]{1,0:T(8,128)(2,1)} custom-call(s32[2]{0:T(128)S(1)} %pad_add_fusion.bases_ref, bf16[128,2048]{1,0:T(8,128)(2,1)S(1)} %copy-done.11, bf16[128,2048]{1,0:T(8,128)(2,1)S(1)} %collective-permute-done.21.refs_1_, bf16[128,2048]{1,0:T(8,128)(2,1)S(1)} %collective-permute-done.22.refs_2_, ...), custom_call_target="tpu_custom_call" | custom-call | tf_op jit(solution)/shard_map/pallas_call | solution.py:369
  (70 shorter events, 0.3 us)
Async XLA Ops:
  0.0 6.0 %copy-start.20 = (bf16[2,768,256]{2,1,0:T(8,128)(2,1)S(1)}, bf16[2,768,256]{2,1,0:T(8,128)(2,1)}, u32[]{:S(2)}) copy-start(bf16[2,768,256]{2,1,0:T(8,128)(2,1)} %param.12) | copy-start | bytes 2359300
  2.0 6.1 %copy-start.13 = (bf16[128,2176]{1,0:T(8,128)(2,1)}, bf16[128,2176]{1,0:T(8,128)(2,1)S(1)}, u32[]{:S(2)}) copy-start(bf16[128,2176]{1,0:T(8,128)(2,1)S(1)} %fusion.1.refs_0_) | copy-start | bytes 1671172
  2.0 26.4 %collective-permute-start.3 = (bf16[128,2176]{1,0:T(8,128)(2,1)S(1)}, bf16[128,2176]{1,0:T(8,128)(2,1)S(1)}, u32[]{:S(2)}, u32[]{:S(2)}) collective-permute-start(bf16[128,2176]{1,0:T(8,128)(2,1)S(1)} %fusion.1.refs_0_), channel_id=1, source_target_pairs={{0,24},{4,28},{8,16},{12,20},{16,8},{20,12},{24,0},{28,4},{1,25},{... | collective-permute-start | bytes 1671176 | tf_op jit(solution)/shard_map/ppermute | solution.py:266
  2.5 31.5 %collective-permute-start.2 = (bf16[128,2176]{1,0:T(8,128)(2,1)S(1)}, bf16[128,2176]{1,0:T(8,128)(2,1)}, u32[]{:S(2)}, u32[]{:S(2)}) collective-permute-start(bf16[128,2176]{1,0:T(8,128)(2,1)S(1)} %fusion.1.refs_0_), channel_id=1, source_target_pairs={{0,3},{1,2},{2,1},{3,0},{4,7},{5,6},{6,5},{7,4},{8,11},{9,10},{10,... | collective-permute-start | bytes 1671176 | tf_op jit(solution)/shard_map/ppermute | solution.py:272
  5.0 24.5 %collective-permute-start.1 = (bf16[128,2176]{1,0:T(8,128)(2,1)S(1)}, bf16[128,2176]{1,0:T(8,128)(2,1)S(1)}, u32[]{:S(2)}, u32[]{:S(2)}) collective-permute-start(bf16[128,2176]{1,0:T(8,128)(2,1)S(1)} %fusion.1.refs_0_), channel_id=1, source_target_pairs={{0,2},{1,3},{2,0},{3,1},{4,6},{5,7},{6,4},{7,5},{8,10},{9,11},{10,... | collective-permute-start | bytes 1671176 | tf_op jit(solution)/shard_map/ppermute | solution.py:272
  5.5 24.8 %collective-permute-start = (bf16[128,2176]{1,0:T(8,128)(2,1)S(1)}, bf16[128,2176]{1,0:T(8,128)(2,1)S(1)}, u32[]{:S(2)}, u32[]{:S(2)}) collective-permute-start(bf16[128,2176]{1,0:T(8,128)(2,1)S(1)} %fusion.1.refs_0_), channel_id=1, source_target_pairs={{0,1},{1,0},{2,3},{3,2},{4,5},{5,4},{6,7},{7,6},{8,9},{9,8},{10,11... | collective-permute-start | bytes 1671176 | tf_op jit(solution)/shard_map/ppermute | solution.py:272
  6.0 2.0 %copy-start.21 = (bf16[2,256,768]{2,1,0:T(8,128)(2,1)S(1)}, bf16[2,256,768]{2,1,0:T(8,128)(2,1)}, u32[]{:S(2)}) copy-start(bf16[2,256,768]{2,1,0:T(8,128)(2,1)} %param.11) | copy-start | bytes 2359300
  6.0 2.0 %copy-start.22 = (bf16[2,256,768]{2,1,0:T(8,128)(2,1)S(1)}, bf16[2,256,768]{2,1,0:T(8,128)(2,1)}, u32[]{:S(2)}) copy-start(bf16[2,256,768]{2,1,0:T(8,128)(2,1)} %param.10) | copy-start | bytes 2359300
  6.8 1.3 copy-start.14
  6.8 19.0 %collective-permute-start.4 = (bf16[768,256]{1,0:T(8,128)(2,1)S(1)}, bf16[768,256]{1,0:T(8,128)(2,1)S(1)}, u32[]{:S(2)}, u32[]{:S(2)}) collective-permute-start(bf16[768,256]{1,0:T(8,128)(2,1)S(1)} %get-tuple-element.45.refs_6_), channel_id=1, source_target_pairs={{0,8},{4,12},{8,0},{12,4},{16,24},{20,28},{24,16},{28,20},{1,9},{5... | collective-permute-start | bytes 1179656 | tf_op jit(solution)/shard_map/ppermute | solution.py:266
  8.2 55.5 %copy-start.12 = (bf16[256,1536]{1,0:T(8,128)(2,1)}, bf16[256,1536]{1,0:T(8,128)(2,1)S(1)}, u32[]{:S(2)}) copy-start(bf16[256,1536]{1,0:T(8,128)(2,1)S(1)} %pad_maximum_fusion.1.refs_4_) | copy-start | bytes 2359300
  25.9 38.4 %copy-start.17 = (bf16[768,256]{1,0:T(8,128)(2,1)}, bf16[768,256]{1,0:T(8,128)(2,1)S(1)}, u32[]{:S(2)}) copy-start(bf16[768,256]{1,0:T(8,128)(2,1)S(1)} %collective-permute-done.4.refs_8_) | copy-start | bytes 1179652
  28.4 47.4 %copy-start = (bf16[128,2176]{1,0:T(8,128)(2,1)}, bf16[128,2176]{1,0:T(8,128)(2,1)S(1)}, u32[]{:S(2)}) copy-start(bf16[128,2176]{1,0:T(8,128)(2,1)S(1)} %collective-permute-done.3.refs_0_) | copy-start | bytes 1671172
  28.4 35.4 %collective-permute-start.5 = (bf16[256,1536]{1,0:T(8,128)(2,1)S(1)}, bf16[256,1536]{1,0:T(8,128)(2,1)}, u32[]{:S(2)}, u32[]{:S(2)}) collective-permute-start(bf16[256,1536]{1,0:T(8,128)(2,1)S(1)} %pad_maximum_fusion), channel_id=1, source_target_pairs={{0,24},{4,28},{8,16},{12,20},{16,8},{20,12},{24,0},{28,4},{1,25},{... | collective-permute-start | bytes 2359304 | tf_op jit(solution)/shard_map/ppermute | solution.py:266
  28.8 34.9 %collective-permute-start.6 = (bf16[256,1536]{1,0:T(8,128)(2,1)S(1)}, bf16[256,1536]{1,0:T(8,128)(2,1)}, u32[]{:S(2)}, u32[]{:S(2)}) collective-permute-start(bf16[256,1536]{1,0:T(8,128)(2,1)S(1)} %pad_maximum_fusion.1.refs_4_), channel_id=1, source_target_pairs={{0,8},{4,12},{8,0},{12,4},{16,24},{20,28},{24,16},{28,20},{1,9},{5... | collective-permute-start | bytes 2359304 | tf_op jit(solution)/shard_map/ppermute | solution.py:266
  29.5 0.8 copy-start.15
  30.3 0.8 copy-start.16
  31.1 16.4 %collective-permute-start.9 = (bf16[128,2176]{1,0:T(8,128)(2,1)S(1)}, bf16[128,2176]{1,0:T(8,128)(2,1)S(1)}, u32[]{:S(2)}, u32[]{:S(2)}) collective-permute-start(bf16[128,2176]{1,0:T(8,128)(2,1)S(1)} %collective-permute-done.3.refs_0_), channel_id=1, source_target_pairs={{0,3},{1,2},{2,1},{3,0},{4,7},{5,6},{6,5},{7,4},{8,11},{9,10},{10,... | collective-permute-start | bytes 1671176 | tf_op jit(solution)/shard_map/ppermute | solution.py:272
  33.0 25.5 %collective-permute-start.8 = (bf16[128,2176]{1,0:T(8,128)(2,1)S(1)}, bf16[128,2176]{1,0:T(8,128)(2,1)S(1)}, u32[]{:S(2)}, u32[]{:S(2)}) collective-permute-start(bf16[128,2176]{1,0:T(8,128)(2,1)S(1)} %collective-permute-done.3.refs_0_), channel_id=1, source_target_pairs={{0,2},{1,3},{2,0},{3,1},{4,6},{5,7},{6,4},{7,5},{8,10},{9,11},{10,... | collective-permute-start | bytes 1671176 | tf_op jit(solution)/shard_map/ppermute | solution.py:272
  34.1 24.5 %collective-permute-start.7 = (bf16[128,2176]{1,0:T(8,128)(2,1)S(1)}, bf16[128,2176]{1,0:T(8,128)(2,1)S(1)}, u32[]{:S(2)}, u32[]{:S(2)}) collective-permute-start(bf16[128,2176]{1,0:T(8,128)(2,1)S(1)} %collective-permute-done.3.refs_0_), channel_id=1, source_target_pairs={{0,1},{1,0},{2,3},{3,2},{4,5},{5,4},{6,7},{7,6},{8,9},{9,8},{10,11... | collective-permute-start | bytes 1671176 | tf_op jit(solution)/shard_map/ppermute | solution.py:272
  47.6 28.3 %copy-start.2 = (bf16[128,2176]{1,0:T(8,128)(2,1)}, bf16[128,2176]{1,0:T(8,128)(2,1)S(1)}, u32[]{:S(2)}) copy-start(bf16[128,2176]{1,0:T(8,128)(2,1)S(1)} %collective-permute-done.9.refs_3_) | copy-start | bytes 1671172
  58.5 17.3 %copy-start.4 = (bf16[128,2176]{1,0:T(8,128)(2,1)}, bf16[128,2176]{1,0:T(8,128)(2,1)S(1)}, u32[]{:S(2)}) copy-start(bf16[128,2176]{1,0:T(8,128)(2,1)S(1)} %collective-permute-done.8.refs_2_) | copy-start | bytes 1671172
  58.6 0.9 copy-start.6
  63.8 3.6 %collective-permute-start.13 = (bf16[256,1536]{1,0:T(8,128)(2,1)}, bf16[256,1536]{1,0:T(8,128)(2,1)}, u32[]{:S(2)}, u32[]{:S(2)}) collective-permute-start(bf16[256,1536]{1,0:T(8,128)(2,1)} %collective-permute-done.5.refs_8_), channel_id=1, source_target_pairs={{0,4},{4,0},{8,12},{12,8},{16,20},{20,16},{24,28},{28,24},{1,5},{5... | collective-permute-start | bytes 2359304 | tf_op jit(solution)/shard_map/ppermute | solution.py:269
  63.8 4.3 %collective-permute-start.11 = (bf16[256,1536]{1,0:T(8,128)(2,1)S(1)}, bf16[256,1536]{1,0:T(8,128)(2,1)}, u32[]{:S(2)}, u32[]{:S(2)}) collective-permute-start(bf16[256,1536]{1,0:T(8,128)(2,1)S(1)} %pad_maximum_fusion.1.refs_4_), channel_id=1, source_target_pairs={{0,4},{4,0},{8,12},{12,8},{16,20},{20,16},{24,28},{28,24},{1,5},{5... | collective-permute-start | bytes 2359304 | tf_op jit(solution)/shard_map/ppermute | solution.py:269
  64.3 4.4 %collective-permute-start.12 = (bf16[256,1536]{1,0:T(8,128)(2,1)}, bf16[256,1536]{1,0:T(8,128)(2,1)}, u32[]{:S(2)}, u32[]{:S(2)}) collective-permute-start(bf16[256,1536]{1,0:T(8,128)(2,1)} %collective-permute-done.6.refs_6_), channel_id=1, source_target_pairs={{0,4},{4,0},{8,12},{12,8},{16,20},{20,16},{24,28},{28,24},{1,5},{5... | collective-permute-start | bytes 2359304 | tf_op jit(solution)/shard_map/ppermute | solution.py:269
  64.4 20.7 %collective-permute-start.10 = (bf16[256,1536]{1,0:T(8,128)(2,1)}, bf16[256,1536]{1,0:T(8,128)(2,1)}, u32[]{:S(2)}, u32[]{:S(2)}) collective-permute-start(bf16[256,1536]{1,0:T(8,128)(2,1)} %collective-permute-done.5.refs_8_), channel_id=1, source_target_pairs={{0,8},{4,12},{8,0},{12,4},{16,24},{20,28},{24,16},{28,20},{1,9},{5... | collective-permute-start | bytes 2359304 | tf_op jit(solution)/shard_map/ppermute | solution.py:266
  66.2 17.4 %collective-permute-start.16 = (bf16[768,256]{1,0:T(8,128)(2,1)}, bf16[768,256]{1,0:T(8,128)(2,1)}, u32[]{:S(2)}, u32[]{:S(2)}) collective-permute-start(bf16[768,256]{1,0:T(8,128)(2,1)} %get-tuple-element.47), channel_id=1, source_target_pairs={{0,24},{4,28},{8,16},{12,20},{16,8},{20,12},{24,0},{28,4},{1,25},{... | collective-permute-start | bytes 1179656 | tf_op jit(solution)/shard_map/ppermute | solution.py:266
  75.9 9.2 %collective-permute-start.14 = (bf16[768,256]{1,0:T(8,128)(2,1)}, bf16[768,256]{1,0:T(8,128)(2,1)S(1)}, u32[]{:S(2)}, u32[]{:S(2)}) collective-permute-start(bf16[768,256]{1,0:T(8,128)(2,1)} %copy-done.14), channel_id=1, source_target_pairs={{0,4},{4,0},{8,12},{12,8},{16,20},{20,16},{24,28},{28,24},{1,5},{5... | collective-permute-start | bytes 1179656 | tf_op jit(solution)/shard_map/ppermute | solution.py:269
  76.1 9.0 %collective-permute-start.15 = (bf16[768,256]{1,0:T(8,128)(2,1)}, bf16[768,256]{1,0:T(8,128)(2,1)S(1)}, u32[]{:S(2)}, u32[]{:S(2)}) collective-permute-start(bf16[768,256]{1,0:T(8,128)(2,1)} %copy-done.17), channel_id=1, source_target_pairs={{0,4},{4,0},{8,12},{12,8},{16,20},{20,16},{24,28},{28,24},{1,5},{5... | collective-permute-start | bytes 1179656 | tf_op jit(solution)/shard_map/ppermute | solution.py:269
  85.0 11.1 %copy-start.18 = (bf16[768,256]{1,0:T(8,128)(2,1)}, bf16[768,256]{1,0:T(8,128)(2,1)S(1)}, u32[]{:S(2)}) copy-start(bf16[768,256]{1,0:T(8,128)(2,1)S(1)} %collective-permute-done.14.refs_7_) | copy-start | bytes 1179652
  85.0 11.1 %copy-start.19 = (bf16[768,256]{1,0:T(8,128)(2,1)}, bf16[768,256]{1,0:T(8,128)(2,1)S(1)}, u32[]{:S(2)}) copy-start(bf16[768,256]{1,0:T(8,128)(2,1)S(1)} %collective-permute-done.15.refs_9_) | copy-start | bytes 1179652
  85.0 11.7 %collective-permute-start.17 = (bf16[256,1536]{1,0:T(8,128)(2,1)}, bf16[256,1536]{1,0:T(8,128)(2,1)}, u32[]{:S(2)}, u32[]{:S(2)}) collective-permute-start(bf16[256,1536]{1,0:T(8,128)(2,1)} %collective-permute-done.10.refs_4_), channel_id=1, source_target_pairs={{0,4},{4,0},{8,12},{12,8},{16,20},{20,16},{24,28},{28,24},{1,5},{5... | collective-permute-start | bytes 2359304 | tf_op jit(solution)/shard_map/ppermute | solution.py:269
  85.1 21.0 %collective-permute-start.18 = (bf16[768,256]{1,0:T(8,128)(2,1)}, bf16[768,256]{1,0:T(8,128)(2,1)}, u32[]{:S(2)}, u32[]{:S(2)}) collective-permute-start(bf16[768,256]{1,0:T(8,128)(2,1)} %collective-permute-done.16.refs_12_.refs_6_), channel_id=1, source_target_pairs={{0,8},{4,12},{8,0},{12,4},{16,24},{20,28},{24,16},{28,20},{1,9},{5... | collective-permute-start | bytes 1179656 | tf_op jit(solution)/shard_map/ppermute | solution.py:266
  96.7 13.5 %copy-start.1 = (bf16[128,2176]{1,0:T(8,128)(2,1)S(1)}, bf16[128,2176]{1,0:T(8,128)(2,1)}, u32[]{:S(2)}) copy-start(bf16[128,2176]{1,0:T(8,128)(2,1)} %copy-done) | copy-start | bytes 1671172
  96.7 13.5 %copy-start.3 = (bf16[128,2176]{1,0:T(8,128)(2,1)S(1)}, bf16[128,2176]{1,0:T(8,128)(2,1)}, u32[]{:S(2)}) copy-start(bf16[128,2176]{1,0:T(8,128)(2,1)} %copy-done.2) | copy-start | bytes 1671172
  96.7 13.5 %copy-start.5 = (bf16[128,2176]{1,0:T(8,128)(2,1)S(1)}, bf16[128,2176]{1,0:T(8,128)(2,1)}, u32[]{:S(2)}) copy-start(bf16[128,2176]{1,0:T(8,128)(2,1)} %copy-done.4) | copy-start | bytes 1671172
  106.1 4.1 %collective-permute-start.19 = (bf16[768,256]{1,0:T(8,128)(2,1)}, bf16[768,256]{1,0:T(8,128)(2,1)S(1)}, u32[]{:S(2)}, u32[]{:S(2)}) collective-permute-start(bf16[768,256]{1,0:T(8,128)(2,1)} %collective-permute-done.18.refs_10_.refs_4_), channel_id=1, source_target_pairs={{0,4},{4,0},{8,12},{12,8},{16,20},{20,16},{24,28},{28,24},{1,5},{5... | collective-permute-start | bytes 1179656 | tf_op jit(solution)/shard_map/ppermute | solution.py:269
  106.1 4.1 %collective-permute-start.20 = (bf16[768,256]{1,0:T(8,128)(2,1)}, bf16[768,256]{1,0:T(8,128)(2,1)S(1)}, u32[]{:S(2)}, u32[]{:S(2)}) collective-permute-start(bf16[768,256]{1,0:T(8,128)(2,1)} %collective-permute-done.16.refs_12_.refs_6_), channel_id=1, source_target_pairs={{0,4},{4,0},{8,12},{12,8},{16,20},{20,16},{24,28},{28,24},{1,5},{5... | collective-permute-start | bytes 1179656 | tf_op jit(solution)/shard_map/ppermute | solution.py:269
  106.6 12.2 %collective-permute-start.24 = (bf16[128,1024]{1,0:T(8,128)(2,1)}, bf16[128,1024]{1,0:T(8,128)(2,1)}, u32[]{:S(2)}, u32[]{:S(2)}) collective-permute-start(bf16[128,1024]{1,0:T(8,128)(2,1)} %get-tuple-element.58), channel_id=1, source_target_pairs={{0,1},{1,0},{2,3},{3,2},{4,5},{5,4},{6,7},{7,6},{8,9},{9,8},{10,11... | collective-permute-start | bytes 786440 | tf_op jit(solution)/shard_map/ppermute | solution.py:272
  108.2 20.4 %collective-permute-start.25 = (bf16[128,1024]{1,0:T(8,128)(2,1)}, bf16[128,1024]{1,0:T(8,128)(2,1)}, u32[]{:S(2)}, u32[]{:S(2)}) collective-permute-start(bf16[128,1024]{1,0:T(8,128)(2,1)} %get-tuple-element.59), channel_id=1, source_target_pairs={{0,2},{1,3},{2,0},{3,1},{4,6},{5,7},{6,4},{7,5},{8,10},{9,11},{10,... | collective-permute-start | bytes 786440 | tf_op jit(solution)/shard_map/ppermute | solution.py:272
  109.7 20.5 %collective-permute-start.26 = (bf16[128,1024]{1,0:T(8,128)(2,1)}, bf16[128,1024]{1,0:T(8,128)(2,1)}, u32[]{:S(2)}, u32[]{:S(2)}) collective-permute-start(bf16[128,1024]{1,0:T(8,128)(2,1)} %get-tuple-element.60), channel_id=1, source_target_pairs={{0,3},{1,2},{2,1},{3,0},{4,7},{5,6},{6,5},{7,4},{8,11},{9,10},{10,... | collective-permute-start | bytes 786440 | tf_op jit(solution)/shard_map/ppermute | solution.py:272
  110.2 5.5 %copy-start.8 = (bf16[768,256]{1,0:T(8,128)(2,1)}, bf16[768,256]{1,0:T(8,128)(2,1)S(1)}, u32[]{:S(2)}) copy-start(bf16[768,256]{1,0:T(8,128)(2,1)S(1)} %collective-permute-done.19.refs_11_.refs_5_) | copy-start | bytes 1179652
  110.2 1.2 copy-start.7
  111.4 1.1 copy-start.10
  112.5 3.2 %copy-start.9 = (bf16[768,256]{1,0:T(8,128)(2,1)}, bf16[768,256]{1,0:T(8,128)(2,1)S(1)}, u32[]{:S(2)}) copy-start(bf16[768,256]{1,0:T(8,128)(2,1)S(1)} %collective-permute-done.20.refs_13_.refs_7_) | copy-start | bytes 1179652
  115.7 16.0 %collective-permute-start.28 = (bf16[128,1024]{1,0:T(8,128)(2,1)}, bf16[128,1024]{1,0:T(8,128)(2,1)S(1)}, u32[]{:S(2)}, u32[]{:S(2)}) collective-permute-start(bf16[128,1024]{1,0:T(8,128)(2,1)} %get-tuple-element.62), channel_id=1, source_target_pairs={{0,1},{1,0},{2,3},{3,2},{4,5},{5,4},{6,7},{7,6},{8,9},{9,8},{10,11... | collective-permute-start | bytes 786440 | tf_op jit(solution)/shard_map/ppermute | solution.py:272
  117.3 16.9 %collective-permute-start.29 = (bf16[128,1024]{1,0:T(8,128)(2,1)}, bf16[128,1024]{1,0:T(8,128)(2,1)}, u32[]{:S(2)}, u32[]{:S(2)}) collective-permute-start(bf16[128,1024]{1,0:T(8,128)(2,1)} %get-tuple-element.63), channel_id=1, source_target_pairs={{0,2},{1,3},{2,0},{3,1},{4,6},{5,7},{6,4},{7,5},{8,10},{9,11},{10,... | collective-permute-start | bytes 786440 | tf_op jit(solution)/shard_map/ppermute | solution.py:272
  118.8 15.4 %collective-permute-start.30 = (bf16[128,1024]{1,0:T(8,128)(2,1)}, bf16[128,1024]{1,0:T(8,128)(2,1)}, u32[]{:S(2)}, u32[]{:S(2)}) collective-permute-start(bf16[128,1024]{1,0:T(8,128)(2,1)} %get-tuple-element.64), channel_id=1, source_target_pairs={{0,3},{1,2},{2,1},{3,0},{4,7},{5,6},{6,5},{7,4},{8,11},{9,10},{10,... | collective-permute-start | bytes 786440 | tf_op jit(solution)/shard_map/ppermute | solution.py:272
  119.9 12.3 %copy-start.23 = (bf16[128,1024]{1,0:T(8,128)(2,1)S(1)}, bf16[128,1024]{1,0:T(8,128)(2,1)}, u32[]{:S(2)}) copy-start(bf16[128,1024]{1,0:T(8,128)(2,1)} %get-tuple-element.57) | copy-start | bytes 786436
  128.6 29.0 %copy-start.11 = (bf16[128,2048]{1,0:T(8,128)(2,1)S(1)}, bf16[128,2048]{1,0:T(8,128)(2,1)}, u32[]{:S(2)}) copy-start(bf16[128,2048]{1,0:T(8,128)(2,1)} %get-tuple-element.53.refs_0_) | copy-start | bytes 1572868
  128.6 25.6 %collective-permute-start.21 = (bf16[128,2048]{1,0:T(8,128)(2,1)}, bf16[128,2048]{1,0:T(8,128)(2,1)S(1)}, u32[]{:S(2)}, u32[]{:S(2)}) collective-permute-start(bf16[128,2048]{1,0:T(8,128)(2,1)} %get-tuple-element.54), channel_id=1, source_target_pairs={{0,1},{1,0},{2,3},{3,2},{4,5},{5,4},{6,7},{7,6},{8,9},{9,8},{10,11... | collective-permute-start | bytes 1572872 | tf_op jit(solution)/shard_map/ppermute | solution.py:272
  130.2 25.5 %collective-permute-start.22 = (bf16[128,2048]{1,0:T(8,128)(2,1)}, bf16[128,2048]{1,0:T(8,128)(2,1)S(1)}, u32[]{:S(2)}, u32[]{:S(2)}) collective-permute-start(bf16[128,2048]{1,0:T(8,128)(2,1)} %get-tuple-element.55), channel_id=1, source_target_pairs={{0,2},{1,3},{2,0},{3,1},{4,6},{5,7},{6,4},{7,5},{8,10},{9,11},{10,... | collective-permute-start | bytes 1572872 | tf_op jit(solution)/shard_map/ppermute | solution.py:272
  131.7 24.0 %collective-permute-start.23 = (bf16[128,2048]{1,0:T(8,128)(2,1)}, bf16[128,2048]{1,0:T(8,128)(2,1)S(1)}, u32[]{:S(2)}, u32[]{:S(2)}) collective-permute-start(bf16[128,2048]{1,0:T(8,128)(2,1)} %get-tuple-element.56), channel_id=1, source_target_pairs={{0,3},{1,2},{2,1},{3,0},{4,7},{5,6},{6,5},{7,4},{8,11},{9,10},{10,... | collective-permute-start | bytes 1572872 | tf_op jit(solution)/shard_map/ppermute | solution.py:272
  134.2 20.1 %collective-permute-start.27 = (bf16[128,1024]{1,0:T(8,128)(2,1)}, bf16[128,1024]{1,0:T(8,128)(2,1)S(1)}, u32[]{:S(2)}, u32[]{:S(2)}) collective-permute-start(bf16[128,1024]{1,0:T(8,128)(2,1)} %add_convert_fusion.1), channel_id=1, source_target_pairs={{0,24},{4,28},{8,16},{12,20},{16,8},{20,12},{24,0},{28,4},{1,25},{... | collective-permute-start | bytes 786440 | tf_op jit(solution)/shard_map/ppermute | solution.py:266
  135.4 22.2 %collective-permute-start.31 = (bf16[128,1024]{1,0:T(8,128)(2,1)S(1)}, bf16[128,1024]{1,0:T(8,128)(2,1)S(1)}, u32[]{:S(2)}, u32[]{:S(2)}) collective-permute-start(bf16[128,1024]{1,0:T(8,128)(2,1)S(1)} %add_convert_fusion), channel_id=1, source_target_pairs={{0,24},{4,28},{8,16},{12,20},{16,8},{20,12},{24,0},{28,4},{1,25},{... | collective-permute-start | bytes 786440 | tf_op jit(solution)/shard_map/ppermute | solution.py:266

commit v5 on v4

v5 whole, which is shorter than its diff:
```python
import functools

import jax
import jax.numpy as jnp
from jax import lax
from jax.experimental import pallas as pl
from jax.experimental.pallas import tpu as pltpu
from jax.sharding import PartitionSpec as P

LANES = 128
VMEM = 62 * 1024 * 1024
FREE = pl.CostEstimate(flops=0, bytes_accessed=0, transcendentals=0)
LONG = pl.CostEstimate(flops=20 * 10**9, bytes_accessed=0, transcendentals=0)
ANY = pl.BlockSpec(memory_space=pl.ANY)
SMEM = pl.BlockSpec(memory_space=pltpu.SMEM)


def gate_table(expert_ids, gate_weights, experts):
    named = expert_ids[:, :, None] == jnp.arange(experts, dtype=jnp.int32)
    return jnp.sum(jnp.where(named, gate_weights[:, :, None], 0.0), axis=1)


def pack(table, width):
    parts, rest = [], table
    for _ in range(3):
        part = lax.reduce_precision(rest, 8, 7)
        parts.append(part.astype(jnp.bfloat16))
        rest = rest - part
    flat = jnp.concatenate(parts, axis=0).reshape(-1)
    rows = -(-flat.shape[0] // (16 * width)) * 16
    return jnp.pad(flat, (0, rows * width - flat.shape[0])).reshape(rows, width)


def unpack(packed, count, columns):
    parts = packed.reshape(-1)[: 3 * count * columns].reshape(3, count, columns).astype(jnp.float32)
    return parts[0] + parts[1] + parts[2]


def after(array, *earlier):
    return lax.optimization_barrier((array, *earlier))[0]


class Loads:
    def __init__(self, sems):
        self.sems, self.used = sems, 0

    def add(self, source, target):
        self.used += 1
        return pltpu.make_async_copy(source, target, self.sems.at[self.used - 1])


def row_loads(loads, row_refs, rows, numbers_ref, slices, depth):
    tok_rows, span = row_refs[0].shape[0], 2 * depth
    copies = []
    for j in range(slices // 2):
        columns = pl.ds(pl.multiple_of(numbers_ref[slices + j], LANES), span)
        for b, row_ref in enumerate(row_refs):
            target = rows.at[pl.ds(b * tok_rows, tok_rows), pl.ds(j * span, span)]
            copies.append(loads.add(row_ref.at[:, columns], target))
    return copies


def weight_loads(loads, weight_refs, weights, numbers_ref, tiles, tile):
    depth, both = weight_refs[0].shape
    copies = []
    for t in range(tiles):
        copies.append([])
        for k, weight_ref in enumerate(weight_refs):
            place = pl.ds(pl.multiple_of(numbers_ref[k], LANES), depth)
            for part in range(2):
                source = weight_ref.at[:, pl.ds(part * (both // 2) + t * tile, tile)]
                target = weights.at[t, place, pl.ds(part * tile, tile)]
                copies[t].append(loads.add(source, target))
    return copies


def early_kernel(blocks, slices, numbers_ref, *refs):
    row_refs, refs = refs[:blocks], refs[blocks:]
    weight_refs, (gate_out, up_out, rows, weights, sems) = refs[:slices], refs[slices:]
    tiles, _, twice = weights.shape
    tile = twice // 2
    step = pl.program_id(0)
    loads = Loads(sems)
    first = row_loads(loads, row_refs, rows, numbers_ref, slices, weight_refs[0].shape[0])
    by_tile = weight_loads(loads, weight_refs, weights, numbers_ref, tiles, tile)

    @pl.when(step == 0)
    def _():
        for copy in first + [copy for copies in by_tile for copy in copies]:
            copy.start()
        for copy in first:
            copy.wait()

    for t in range(tiles):

        @pl.when(step == t)
        def _():
            for copy in by_tile[t]:
                copy.wait()
            sums = jnp.dot(rows[...], weights[t], preferred_element_type=jnp.float32)
            gate_out[...] = sums[:, :tile]
            up_out[...] = sums[:, tile:]


def late_kernel(blocks, slices, down_slices, tile, summed, numbers_ref, *refs):
    row_refs, refs = refs[:blocks], refs[blocks:]
    weight_refs, refs = refs[:slices], refs[slices:]
    down_refs, refs = refs[:down_slices], refs[down_slices:]
    sums_in, refs = refs[:summed], refs[summed:]
    hidden, out_refs, refs = refs[0], refs[1 : 1 + blocks], refs[1 + blocks :]
    sums, (rows, weights, down, sems) = refs[:summed], refs[summed:]
    depth, both = weight_refs[0].shape
    loads = Loads(sems)
    first = row_loads(loads, row_refs, rows, numbers_ref, slices, depth)
    for k, weight_ref in enumerate(weight_refs):
        place = pl.ds(pl.multiple_of(numbers_ref[k], LANES), depth)
        first.append(loads.add(weight_ref, weights.at[place]))
    first += [loads.add(source, target) for source, target in zip(sums_in, sums)]
    final = [loads.add(ref.at[pl.ds(0, both // 2)], down.at[k]) for k, ref in enumerate(down_refs)]
    for copy in first + final:
        copy.start()
    for copy in first:
        copy.wait()
    for start in range(0, both // 2, tile):
        columns, up_columns = pl.ds(start, tile), pl.ds(both // 2 + start, tile)
        gate_sum = jnp.dot(rows[...], weights[:, columns], preferred_element_type=jnp.float32)
        up_sum = jnp.dot(rows[...], weights[:, up_columns], preferred_element_type=jnp.float32)
        if summed:
            gate_sum, up_sum = gate_sum + sums[0][:, columns], up_sum + sums[1][:, columns]
        hidden[:, columns] = (gate_sum / (1.0 + jnp.exp(-gate_sum)) * up_sum).astype(jnp.bfloat16)
    for copy in final:
        copy.wait()
    first_down = slices + slices // 2
    write_out(hidden, [down.at[k] for k in range(down_slices)], out_refs, numbers_ref, first_down)


def write_out(hidden, down, out_refs, numbers_ref, at):
    tok_rows = out_refs[0].shape[0]
    for k, weights in enumerate(down):
        part = jnp.dot(hidden[...], weights[: hidden.shape[1]], preferred_element_type=jnp.float32).astype(jnp.bfloat16)
        columns = pl.ds(pl.multiple_of(numbers_ref[at + k], LANES), part.shape[1])
        for b, out_ref in enumerate(out_refs):
            out_ref[:, columns] = part[b * tok_rows : (b + 1) * tok_rows]


def early_sums(row_blocks, gate_up, numbers):
    blocks, slices = len(row_blocks), len(gate_up)
    depth, both = gate_up[0].shape
    count, inner = blocks * row_blocks[0].shape[0], both // 2
    tile = 256 if inner % 256 == 0 else inner
    tiles = inner // tile
    spec = pl.BlockSpec((count, tile), lambda i: (0, i))
    return pl.pallas_call(
        functools.partial(early_kernel, blocks, slices),
        grid=(tiles,),
        in_specs=[SMEM] + [ANY] * (blocks + slices),
        out_specs=[spec, spec],
        out_shape=[jax.ShapeDtypeStruct((count, inner), jnp.float32)] * 2,
        scratch_shapes=[
            pltpu.VMEM((count, slices * depth), jnp.bfloat16),
            pltpu.VMEM((tiles, slices * depth, 2 * tile), jnp.bfloat16),
            pltpu.SemaphoreType.DMA((slices // 2 * blocks + 2 * tiles * slices,)),
        ],
        compiler_params=pltpu.CompilerParams(vmem_limit_bytes=62 * 1024 * 1024),
        cost_estimate=FREE,
    )(numbers, *row_blocks, *gate_up)


def late_outputs(row_blocks, gate_up, down, numbers, early):
    blocks, slices, down_slices = len(row_blocks), len(gate_up), len(down)
    depth, both = gate_up[0].shape
    tok_rows = row_blocks[0].shape[0]
    count, inner = blocks * tok_rows, both // 2
    tile = 256 if inner % 256 == 0 else inner
    whole = pl.BlockSpec(memory_space=pltpu.VMEM)
    out = jax.ShapeDtypeStruct((tok_rows, down_slices * depth), jnp.bfloat16)
    results = pl.pallas_call(
        functools.partial(late_kernel, blocks, slices, down_slices, tile, len(early)),
        in_specs=[SMEM] + [ANY] * (blocks + slices + down_slices + len(early)),
        out_specs=[whole] * (1 + blocks),
        out_shape=[jax.ShapeDtypeStruct((count, inner), jnp.bfloat16)] + [out] * blocks,
        scratch_shapes=[pltpu.VMEM((count, inner), jnp.float32)] * len(early)
        + [
            pltpu.VMEM((count, slices * depth), jnp.bfloat16),
            pltpu.VMEM((slices * depth, both), jnp.bfloat16),
            pltpu.VMEM((down_slices, inner, down[0].shape[1]), jnp.bfloat16),
            pltpu.SemaphoreType.DMA((slices // 2 * blocks + slices + 2 + down_slices,)),
        ],
        compiler_params=pltpu.CompilerParams(vmem_limit_bytes=62 * 1024 * 1024),
        cost_estimate=FREE,
    )(numbers, *row_blocks, *gate_up, *down, *early)
    return results[0], results[1:]


def down_kernel(blocks, slices, numbers_ref, hidden_ref, *refs):
    write_out(hidden_ref, refs[:slices], refs[slices:], numbers_ref, 0)


def outputs_of(hidden, blocks, down, numbers):
    count, inner = hidden.shape
    slices, depth = len(down), down[0].shape[1]
    whole = pl.BlockSpec(memory_space=pltpu.VMEM)
    return pl.pallas_call(
        functools.partial(down_kernel, blocks, slices),
        in_specs=[SMEM] + [whole] * (1 + slices),
        out_specs=[whole] * blocks,
        out_shape=[jax.ShapeDtypeStruct((count // blocks, slices * depth), jnp.bfloat16)] * blocks,
        compiler_params=pltpu.CompilerParams(vmem_limit_bytes=24 * 1024 * 1024),
        cost_estimate=FREE,
    )(numbers, hidden, *down)


def finish_kernel(mine, bases_ref, gates_ref, *refs):
    parts, sums, out_ref = refs[:mine], refs[mine:-1], refs[-1]
    for group, ref in enumerate(sums):
        columns = pl.ds(pl.multiple_of(bases_ref[group], LANES), ref.shape[1])
        total = ref[...].astype(jnp.float32)
        for k, part in enumerate(parts):
            total += part[:, columns].astype(jnp.float32) * gates_ref[:, k : k + 1]
        out_ref[:, columns] = total.astype(jnp.bfloat16)


def shards(tokens, expert_ids, gate_weights, hot_ids, w_gate, w_up, w_down):
    del hot_ids
    tok_rows, model = tokens.shape
    places, lines = lax.axis_size("expert"), lax.axis_size("dp")
    layers = lines // 2
    half = layers // 2
    mirror = layers - 1
    local_count, depth = w_gate.shape[:2]
    experts = places * local_count
    assert local_count == 2 and half % 2 == 0

    def swap_layer(array, mask):
        return lax.ppermute(array, "dp", [(i, i ^ (2 * mask)) for i in range(lines)])

    def swap_core(array):
        return lax.ppermute(array, "dp", [(i, i ^ 1) for i in range(lines)])

    def swap_place(array, mask):
        return lax.ppermute(array, "expert", [(i, i ^ mask) for i in range(places)])

    line = lax.axis_index("dp")
    layer = line // 2
    parity = lax.rem(layer, 2)
    side = line // (lines // 2)
    near, away = list(range(half)), list(range(half, layers))
    soon, last = near + [mirror], away[:-1]

    def pick(array, which):
        return lax.dynamic_index_in_dim(array, which, 0, keepdims=False)

    def numbers(values):
        return jnp.stack([jnp.asarray(v, jnp.int32) for v in values])

    def lines_of(masks):
        return [line ^ (2 * mask + core) for mask in masks for core in range(2)]

    def places_of(masks):
        first = [2 * (layer ^ mask) * depth for mask in masks]
        return numbers([(2 * (k // 2) + lax.rem(v, 2)) * depth for k, v in enumerate(lines_of(masks))] + first)

    def both_cores(found, found_core, masks):
        return [piece for mask in masks for piece in (found[mask], found_core[mask])]

    singles = [1 << i for i in range(places.bit_length() - 1)]
    others = [mask for mask in range(1, places) if mask not in singles]
    block = tokens
    dn = {0: pick(w_down, side)}
    far = {0: swap_layer(block, mirror)}
    own = {0: block, **{mask: swap_place(block, mask) for mask in range(1, places)}}
    for mask in near[1:]:
        dn[mask] = swap_layer(dn[0], mask)
    wave = [far[0], *[own[mask] for mask in singles], *[dn[mask] for mask in near[1:]]]
    first = [far[0], *[dn[mask] for mask in near[1:]]]

    table = gate_table(expert_ids, gate_weights, experts)
    carried = jnp.concatenate([pick(w_down, 1 - side), pack(table, depth)], axis=0)
    mine, theirs = [jnp.concatenate([pick(w_gate, which), pick(w_up, which)], axis=1) for which in (side, 1 - side)]
    gu = {0: mine, mirror: swap_layer(after(theirs, carried, *first), mirror)}
    for mask in near[1:]:
        gu[mask] = swap_layer(after(mine, *first), mask)
    for mask in singles:
        far[mask] = swap_place(after(far[0], *wave), mask)
    for mask in others:
        far[mask] = swap_place(after(far[0], *wave), mask)
    wave = [gu[mirror], *[gu[mask] for mask in near[1:]], *[far[mask] for mask in range(1, places)], *[own[mask] for mask in others]]


    def gates_of(table):
        place = lax.axis_index("expert")
        wanted = jnp.stack([(place ^ mask) * local_count + side for mask in range(places)])
        chosen = jnp.arange(experts, dtype=jnp.int32)[:, None] == wanted
        return jnp.sum(jnp.where(chosen, table[:, :, None], 0.0), axis=1)

    own_gates = gates_of(table)

    for mask in near[1:]:
        gu[mask ^ mirror] = swap_layer(after(gu[mirror], *wave), mask)
    dn[mirror] = swap_layer(after(carried, *wave), mirror)
    gu_core = {mask: swap_core(after(gu[mask], *wave)) for mask in near + [mirror]}
    pieces = both_cores(gu, gu_core, soon)
    chunks = {}
    for key, found in (("far", far), ("own", own)):
        blocks = [found[mask] for mask in range(places)]
        chunks[key] = [blocks[i : i + 4] for i in range(0, places, 4)]
    counted = after(places_of(soon), dn[mirror])
    early = [early_sums(chunk, pieces, counted) for chunk in chunks["far"]]
    settled = [sums for pair in early for sums in pair]
    dn_core = {mask: swap_core(after(dn[mask], dn[mirror])) for mask in near}
    wave = [*settled, *[dn_core[mask] for mask in near]]
    for mask in near[1:]:
        gu_core[mask ^ mirror] = swap_core(after(gu[mask ^ mirror], *wave))

    far_gates = gates_of(unpack(dn[mirror][w_down.shape[1] :], tok_rows, experts))

    def arrived(parts):
        return [parts[0]] + [swap_place(parts[mask], mask) for mask in range(1, places)]

    def add_up(parts, gates):
        total = parts[0].astype(jnp.float32) * gates[:, :1]
        for k, part in enumerate(parts[1:], 1):
            total += part.astype(jnp.float32) * gates[:, k : k + 1]
        return total.astype(jnp.bfloat16)

    def late(chunks, gate_masks, down_masks, early):
        columns = [lax.rem(v, 2 * len(down_masks)) * depth for v in lines_of(down_masks)]
        counted = jnp.concatenate([places_of(gate_masks), numbers(columns)])
        hidden, parts = [], []
        for chunk, sums in zip(chunks, early):
            pieces = both_cores(gu, gu_core, gate_masks)
            rows, blocks = late_outputs(chunk, pieces, both_cores(dn, dn_core, down_masks), counted, sums)
            hidden.append(rows)
            parts += blocks
        return hidden, parts

    far_hidden, far_parts = late(chunks["far"], last, near, early)
    for mask in near[1:]:
        dn[mask ^ mirror] = swap_layer(after(dn[mirror], *settled), mask)
    for mask in away:
        dn_core[mask] = swap_core(after(dn[mask], far_hidden[-1]))
    starts = numbers([lax.rem(v, 2 * len(away)) * depth for v in lines_of(away)])
    more_parts = []
    for chunk, rows in zip(chunks["far"], far_hidden):
        more_parts += outputs_of(rows, len(chunk), both_cores(dn, dn_core, away), starts)
    arrived_near = arrived(far_parts)
    near_total = add_up(arrived_near, far_gates)
    arrived_away = arrived(more_parts)
    away_total = add_up([after(part, near_total, *arrived_near) for part in arrived_away], far_gates)
    sums = [swap_layer(total, mirror) for total in (near_total, away_total)]
    mine = arrived(late(chunks["own"], soon + last, near + away, [()] * len(chunks["own"]))[1])
    width = model // 2
    bases = numbers([(1 - side) * width, side * width])
    whole = pl.BlockSpec(memory_space=pltpu.VMEM)
    return pl.pallas_call(
        functools.partial(finish_kernel, len(mine)),
        in_specs=[SMEM] + [whole] * (1 + len(mine) + len(sums)),
        out_specs=whole,
        out_shape=jax.ShapeDtypeStruct((tok_rows, model), jnp.bfloat16),
        compiler_params=pltpu.CompilerParams(vmem_limit_bytes=16 * 1024 * 1024),
    )(bases, own_gates, *mine, *sums)


def solution(mesh):
    placed = (
        P(("dp", "expert"), None),
        P(("dp", "expert"), None),
        P(("dp", "expert"), None),
        P(),
        P("expert", "dp", None),
        P("expert", "dp", None),
        P("expert", None, "dp"),
    )
    return jax.shard_map(
        shards, mesh=mesh, in_specs=placed, out_specs=P(("dp", "expert"), None), check_vma=False
    )
```

time: 160 us -> 160 us (level)
  waiting for transfers between devices: 73.6 us -> 89.5 us
  starting transfers between devices: 36.9 us -> 28.5 us
  Pallas kernels: 35.3 us -> 28.8 us
    ppermute x9, waiting for transfers between devices: 46.3 us -> 65.4 us  [swap_layer(): return lax.ppermute(array, 'dp', [(i, i ^ 2 * mask) for i in range(lines)])]
    ppermute x9, starting transfers between devices: 17.6 us -> 8.64 us  [swap_layer(): return lax.ppermute(array, 'dp', [(i, i ^ 2 * mask) for i in range(lines)])]
    pallas_call x2 -> x1, Pallas kernels: 14.4 us -> 7.22 us  [early_sums(): pl.pallas_call(functools.partial(early_kernel, blocks, slices), grid=(til...]
    unnamed x48 -> x38, local copies, waits for them, and re-layouts: 4.96 us -> 2.84 us
    ppermute x15, waiting for transfers between devices: 26 us -> 24.1 us  [swap_place(): return lax.ppermute(array, 'expert', [(i, i ^ mask) for i in range(places)])]
  transfers between devices with their start and end apart: 32 -> 32, of which waited for: 14 -> 12; matrix products, arithmetic and copies ran while one was open for 4% -> 5% of each run, Pallas kernels for 21% -> 17%
where the time goes in v5:
time: 160 us; the launch traced here: 158 us
  waiting for transfers between devices  89.5 us (56%)
  Pallas kernels  28.8 us (18%)
  starting transfers between devices  28.5 us (18%)
  local copies, waits for them, and re-layouts  6.73 us (4%)
  other arithmetic  4.1 us (3%)
    ppermute x9, waiting for transfers between devices, swap_layer(): return lax.ppermute(array, 'dp', [(i, i ^ 2 * mask) for i in range(lines)])  65.4 us
    ppermute x15, waiting for transfers between devices, swap_place(): return lax.ppermute(array, 'expert', [(i, i ^ mask) for i in range(places)])  24.1 us
    ppermute x15, starting transfers between devices, swap_place(): return lax.ppermute(array, 'expert', [(i, i ^ mask) for i in range(places)])  18.6 us
    pallas_call x2, Pallas kernels, late_outputs(): pl.pallas_call(functools.partial(late_kernel, blocks, slices, down_slices...  17.3 us
    ppermute x9, starting transfers between devices, swap_layer(): return lax.ppermute(array, 'dp', [(i, i ^ 2 * mask) for i in range(lines)])  8.64 us
    pallas_call x1, Pallas kernels, early_sums(): pl.pallas_call(functools.partial(early_kernel, blocks, slices), grid=(til...  7.22 us
    convert_element_type x2, other arithmetic, add_up(): return total.astype(jnp.bfloat16)  3.54 us
  transfers between devices with their start and end apart: 32, of which 12 were waited for; matrix products, arithmetic and copies ran while one was open for 5% of the time, Pallas kernels for 17%

profile of v5, /device:TPU:16, one launch (start us, length us, event | category | flops | bytes accessed | tf_op | source)
XLA Modules:
  0.0 158.0 jit_solution(1849910010588940743)
XLA Ops:
  0.0 0.4 collective-permute-start.3
  0.5 1.5 collective-permute-start
  1.9 1.5 collective-permute-start.1
  3.5 0.5 collective-permute-start.2
  3.9 1.2 dynamic-slice_bitcast_fusion
  5.2 1.3 collective-permute-start.4
  6.5 0.1 dynamic-slice_bitcast_fusion.4
  6.7 0.6 copy-done.17
  7.3 0.2 copy.15
  7.5 0.1 reshape.37
  7.8 15.5 %collective-permute-done.4.refs_8_.refs_14_ = bf16[768,256]{1,0:T(8,128)(2,1)S(1)} collective-permute-done((bf16[768,256]{1,0:T(8,128)(2,1)S(1)}, bf16[768,256]{1,0:T(8,128)(2,1)S(1)}, u32[]{:S(2)}, u32[]{:S(2)}) %collective-permute-start.4) | collective-permute-done | bytes 393248 | tf_op jit(solution)/shard_map/ppermute | solution.py:235
  23.3 1.8 %collective-permute-done.3.refs_0_ = bf16[128,2048]{1,0:T(8,128)(2,1)S(1)} collective-permute-done((bf16[128,2048]{1,0:T(8,128)(2,1)}, bf16[128,2048]{1,0:T(8,128)(2,1)S(1)}, u32[]{:S(2)}, u32[]{:S(2)}) %collective-permute-start.3) | collective-permute-done | bytes 524320 | tf_op jit(solution)/shard_map/ppermute | solution.py:235
  25.1 0.7 collective-permute-start.6
  25.9 0.7 collective-permute-done.1.refs_2_
  26.6 0.8 collective-permute-start.7
  27.4 1.5 collective-permute-start.8
  28.9 1.2 collective-permute-start.9
  30.1 11.4 %collective-permute-done.7.refs_1_ = bf16[128,2048]{1,0:T(8,128)(2,1)S(1)} collective-permute-done((bf16[128,2048]{1,0:T(8,128)(2,1)S(1)}, bf16[128,2048]{1,0:T(8,128)(2,1)S(1)}, u32[]{:S(2)}, u32[]{:S(2)}) %collective-permute-start.7) | collective-permute-done | bytes 524320 | tf_op jit(solution)/shard_map/ppermute | solution.py:241
  41.5 10.6 %collective-permute-done.8.refs_2_ = bf16[128,2048]{1,0:T(8,128)(2,1)S(1)} collective-permute-done((bf16[128,2048]{1,0:T(8,128)(2,1)S(1)}, bf16[128,2048]{1,0:T(8,128)(2,1)S(1)}, u32[]{:S(2)}, u32[]{:S(2)}) %collective-permute-start.8) | collective-permute-done | bytes 524320 | tf_op jit(solution)/shard_map/ppermute | solution.py:241
  52.1 10.0 %collective-permute-done.5.refs_8_ = bf16[256,1536]{1,0:T(8,128)(2,1)} collective-permute-done((bf16[256,1536]{1,0:T(8,128)(2,1)S(1)}, bf16[256,1536]{1,0:T(8,128)(2,1)}, u32[]{:S(2)}, u32[]{:S(2)}) %collective-permute-start.5) | collective-permute-done | bytes 786464 | tf_op jit(solution)/shard_map/ppermute | solution.py:235
  62.1 0.3 collective-permute-start.14
  62.4 0.2 collective-permute-start.11
  62.6 0.3 collective-permute-start.10
  62.9 2.2 %collective-permute-start.13 = (bf16[256,1536]{1,0:T(8,128)(2,1)}, bf16[256,1536]{1,0:T(8,128)(2,1)}, u32[]{:S(2)}, u32[]{:S(2)}) collective-permute-start(bf16[256,1536]{1,0:T(8,128)(2,1)} %collective-permute-done.5.refs_8_), channel_id=1, source_target_pairs={{0,8},{4,12},{8,0},{12,4},{16,24},{20,28},{24,16},{28,20},{1,9},{5... | collective-permute-start | bytes 2359304 | tf_op jit(solution)/shard_map/ppermute | solution.py:235
  65.1 17.3 %collective-permute-done.14.refs_18_.refs_2_ = bf16[784,256]{1,0:T(8,128)(2,1)S(1)} collective-permute-done((bf16[784,256]{1,0:T(8,128)(2,1)S(1)}, bf16[784,256]{1,0:T(8,128)(2,1)S(1)}, u32[]{:S(2)}, u32[]{:S(2)}) %collective-permute-start.14) | collective-permute-done | bytes 401440 | tf_op jit(solution)/shard_map/ppermute | solution.py:235
  82.4 0.6 collective-permute-start.15
  83.0 0.7 stack.163.numbers_ref
  83.7 7.2 %shard_map.64 = (f32[512,768]{1,0:T(8,128)}, f32[512,768]{1,0:T(8,128)}) custom-call(s32[9]{0:T(128)} %stack.163.numbers_ref, bf16[128,2048]{1,0:T(8,128)(2,1)} %copy-done.10, bf16[128,2048]{1,0:T(8,128)(2,1)} %copy-done.11, bf16[128,2048]{1,0:T(8,128)(2,1)} %copy-done.12, bf16[128,2048]{1,0:T(8,128)(2,1)} %copy-done.13, bf16[256,1536]{1,0:T(8,128)(2,1)} %copy-done.6, ...), custom_call_target="tpu_custom_call" | custom-call | tf_op jit(solution)/shard_map/pallas_call | solution.py:153
  90.9 0.4 collective-permute-done.13.refs_4_.refs_10_
  91.3 0.1 collective-permute-start.17
  91.5 0.6 concatenate.23.numbers_ref
  92.1 0.6 concatenate.18.numbers_ref
  92.8 1.6 %collective-permute-start.18 = (bf16[784,256]{1,0:T(8,128)(2,1)S(1)}, bf16[784,256]{1,0:T(8,128)(2,1)S(1)}, u32[]{:S(2)}, u32[]{:S(2)}) collective-permute-start(bf16[784,256]{1,0:T(8,128)(2,1)S(1)} %collective-permute-done.14.refs_18_.refs_2_), channel_id=1, source_target_pairs={{0,8},{4,12},{8,0},{12,4},{16,24},{20,28},{24,16},{28,20},{1,9},{5... | collective-permute-start | bytes 1204232 | tf_op jit(solution)/shard_map/ppermute | solution.py:235
  94.4 0.1 pad_add_fusion.2.numbers_ref
  94.5 0.1 pad_add_fusion.1
  94.6 0.1 iota_compare_fusion.1
  94.6 0.9 copy-done.8
  95.5 6.3 %shard_map.65 = (bf16[512,768]{1,0:T(8,128)(2,1)}, bf16[128,1024]{1,0:T(8,128)(2,1)}, bf16[128,1024]{1,0:T(8,128)(2,1)}, bf16[128,1024]{1,0:T(8,128)(2,1)}, bf16[128,1024]{1,0:T(8,128)(2,1)}) custom-call(s32[7]{0:T(128)} %concatenate.23.numbers_ref, bf16[128,2048]{1,0:T(8,128)(2,1)} %copy-done.10, bf16[128,2048]{1,0:T(8,128)(2,1)} %copy-done.11, ...), custom_call_target="tpu_custom_call" | custom-call | tf_op jit(solution)/shard_map/pallas_call | solution.py:177
  101.9 0.1 collective-permute-start.20
  102.0 2.3 %collective-permute-done.18.refs_16_.refs_0_ = bf16[784,256]{1,0:T(8,128)(2,1)S(1)} collective-permute-done((bf16[784,256]{1,0:T(8,128)(2,1)S(1)}, bf16[784,256]{1,0:T(8,128)(2,1)S(1)}, u32[]{:S(2)}, u32[]{:S(2)}) %collective-permute-start.18) | collective-permute-done | bytes 401440 | tf_op jit(solution)/shard_map/ppermute | solution.py:235
  104.3 1.6 collective-permute-start.24
  105.9 0.1 add.106
  106.1 1.6 collective-permute-start.25
  107.6 0.5 collective-permute-start.26
  108.1 1.3 copy-done.4
  109.4 2.3 %shard_map.67 = (bf16[128,1024]{1,0:T(8,128)(2,1)S(1)}, bf16[128,1024]{1,0:T(8,128)(2,1)}, bf16[128,1024]{1,0:T(8,128)(2,1)}, bf16[128,1024]{1,0:T(8,128)(2,1)}) custom-call(s32[4]{0:T(128)S(1)} %pad_add_fusion.2.numbers_ref, bf16[512,768]{1,0:T(8,128)(2,1)S(1)} %copy-done.4, bf16[784,256]{1,0:T(8,128)(2,1)S(1)} %collective-permute-done.18.refs_16_.refs_0_, ...), custom_call_target="tpu_custom_call" | custom-call | tf_op jit(solution)/shard_map/pallas_call | solution.py:203
  111.7 1.5 collective-permute-start.28
  113.2 0.1 select_reduce_fusion
  113.3 1.6 %collective-permute-start.29 = (bf16[128,1024]{1,0:T(8,128)(2,1)}, bf16[128,1024]{1,0:T(8,128)(2,1)}, u32[]{:S(2)}, u32[]{:S(2)}) collective-permute-start(bf16[128,1024]{1,0:T(8,128)(2,1)} %get-tuple-element.67), channel_id=1, source_target_pairs={{0,2},{1,3},{2,0},{3,1},{4,6},{5,7},{6,4},{7,5},{8,10},{9,11},{10,... | collective-permute-start | bytes 786440 | tf_op jit(solution)/shard_map/ppermute | solution.py:241
  114.9 1.4 collective-permute-start.30
  116.3 11.0 %shard_map.66 = (bf16[512,768]{1,0:T(8,128)(2,1)}, bf16[128,2048]{1,0:T(8,128)(2,1)}, bf16[128,2048]{1,0:T(8,128)(2,1)}, bf16[128,2048]{1,0:T(8,128)(2,1)}, bf16[128,2048]{1,0:T(8,128)(2,1)}) custom-call(s32[20]{0:T(128)} %concatenate.18.numbers_ref, bf16[128,2048]{1,0:T(8,128)(2,1)} %refs_0_.1, bf16[128,2048]{1,0:T(8,128)(2,1)} %collective-permute-done.refs_1_, ...), custom_call_target="tpu_custom_call" | custom-call | tf_op jit(solution)/shard_map/pallas_call | solution.py:177
  127.3 0.7 collective-permute-start.21
  128.0 1.5 collective-permute-start.22
  129.5 1.4 collective-permute-start.23
  130.9 1.5 add_convert_fusion.1
  132.4 1.3 collective-permute-start.27
  133.6 2.1 %add_convert_fusion = bf16[128,1024]{1,0:T(8,128)(2,1)} fusion(bf16[128,1024]{1,0:T(8,128)(2,1)} %collective-permute-done.30, bf16[128,1024]{1,0:T(8,128)(2,1)} %collective-permute-done.29, bf16[128,1024]{1,0:T(8,128)(2,1)} %collective-permute-done.28, bf16[128,1024]{1,0:T(8,128)(2,1)S(1)} %get-tuple-element.64, f32[128]{0:T(128)S(1)} %get-tuple-element.83, ...), kind=kLoop, calls=%fused_computation.2 | loop fusion | flops 1572864 | bytes 1312768 | tf_op jit(solution)/shard_map/convert_element_type | solution.py:324
  135.7 0.8 collective-permute-start.31
  136.5 0.1 pad_add_fusion.bases_ref
  136.6 0.1 copy.17.gates_ref
  136.7 15.9 %collective-permute-done.27.refs_4_ = bf16[128,1024]{1,0:T(8,128)(2,1)S(1)} collective-permute-done((bf16[128,1024]{1,0:T(8,128)(2,1)S(1)}, bf16[128,1024]{1,0:T(8,128)(2,1)S(1)}, u32[]{:S(2)}, u32[]{:S(2)}) %collective-permute-start.27) | collective-permute-done | bytes 262176 | tf_op jit(solution)/shard_map/ppermute | solution.py:235
  152.6 1.4 collective-permute-done.22.refs_2_
  154.0 2.1 %collective-permute-done.31.refs_5_ = bf16[128,1024]{1,0:T(8,128)(2,1)S(1)} collective-permute-done((bf16[128,1024]{1,0:T(8,128)(2,1)}, bf16[128,1024]{1,0:T(8,128)(2,1)S(1)}, u32[]{:S(2)}, u32[]{:S(2)}) %collective-permute-start.31) | collective-permute-done | bytes 262176 | tf_op jit(solution)/shard_map/ppermute | solution.py:235
  156.1 1.9 %shard_map.68 = bf16[128,2048]{1,0:T(8,128)(2,1)} custom-call(s32[2]{0:T(128)S(1)} %pad_add_fusion.bases_ref, f32[128,4]{1,0:T(8,128)S(1)} %copy.17.gates_ref, bf16[128,2048]{1,0:T(8,128)(2,1)S(1)} %copy-done.5, bf16[128,2048]{1,0:T(8,128)(2,1)S(1)} %collective-permute-done.21.refs_1_, bf16[128,2048]{1,0:T(8,128)(2,1)S(1)} %collective-permute-done.22.refs_2_, ...), custom_call_target="tpu_custom_call" | custom-call | tf_op jit(solution)/shard_map/pallas_call | solution.py:355
  (71 shorter events, 0.4 us)
Async XLA Ops:
  0.0 6.5 %copy-start.15 = (bf16[2,256,768]{2,1,0:T(8,128)(2,1)S(1)}, bf16[2,256,768]{2,1,0:T(8,128)(2,1)}, u32[]{:S(2)}) copy-start(bf16[2,256,768]{2,1,0:T(8,128)(2,1)} %param.11) | copy-start | bytes 2359300
  0.0 25.1 %collective-permute-start.3 = (bf16[128,2048]{1,0:T(8,128)(2,1)}, bf16[128,2048]{1,0:T(8,128)(2,1)S(1)}, u32[]{:S(2)}, u32[]{:S(2)}) collective-permute-start(bf16[128,2048]{1,0:T(8,128)(2,1)} %refs_0_.1), channel_id=1, source_target_pairs={{0,24},{4,28},{8,16},{12,20},{16,8},{20,12},{24,0},{28,4},{1,25},{... | collective-permute-start | bytes 1572872 | tf_op jit(solution)/shard_map/ppermute | solution.py:235
  0.5 25.4 %collective-permute-start = (bf16[128,2048]{1,0:T(8,128)(2,1)}, bf16[128,2048]{1,0:T(8,128)(2,1)}, u32[]{:S(2)}, u32[]{:S(2)}) collective-permute-start(bf16[128,2048]{1,0:T(8,128)(2,1)} %refs_0_.1), channel_id=1, source_target_pairs={{0,1},{1,0},{2,3},{3,2},{4,5},{5,4},{6,7},{7,6},{8,9},{9,8},{10,11... | collective-permute-start | bytes 1572872 | tf_op jit(solution)/shard_map/ppermute | solution.py:241
  1.9 24.7 %collective-permute-start.1 = (bf16[128,2048]{1,0:T(8,128)(2,1)}, bf16[128,2048]{1,0:T(8,128)(2,1)}, u32[]{:S(2)}, u32[]{:S(2)}) collective-permute-start(bf16[128,2048]{1,0:T(8,128)(2,1)} %refs_0_.1), channel_id=1, source_target_pairs={{0,2},{1,3},{2,0},{3,1},{4,6},{5,7},{6,4},{7,5},{8,10},{9,11},{10,... | collective-permute-start | bytes 1572872 | tf_op jit(solution)/shard_map/ppermute | solution.py:241
  3.5 25.5 %collective-permute-start.2 = (bf16[128,2048]{1,0:T(8,128)(2,1)}, bf16[128,2048]{1,0:T(8,128)(2,1)}, u32[]{:S(2)}, u32[]{:S(2)}) collective-permute-start(bf16[128,2048]{1,0:T(8,128)(2,1)} %refs_0_.1), channel_id=1, source_target_pairs={{0,3},{1,2},{2,1},{3,0},{4,7},{5,6},{6,5},{7,4},{8,11},{9,10},{10,... | collective-permute-start | bytes 1572872 | tf_op jit(solution)/shard_map/ppermute | solution.py:241
  3.9 2.5 %copy-start.16 = (bf16[2,256,768]{2,1,0:T(8,128)(2,1)S(1)}, bf16[2,256,768]{2,1,0:T(8,128)(2,1)}, u32[]{:S(2)}) copy-start(bf16[2,256,768]{2,1,0:T(8,128)(2,1)} %param.10) | copy-start | bytes 2359300
  5.2 77.2 %copy-start.7 = (bf16[768,256]{1,0:T(8,128)(2,1)}, bf16[768,256]{1,0:T(8,128)(2,1)S(1)}, u32[]{:S(2)}) copy-start(bf16[768,256]{1,0:T(8,128)(2,1)S(1)} %get-tuple-element.48.refs_6_.refs_12_) | copy-start | bytes 1179652
  5.2 18.1 %collective-permute-start.4 = (bf16[768,256]{1,0:T(8,128)(2,1)S(1)}, bf16[768,256]{1,0:T(8,128)(2,1)S(1)}, u32[]{:S(2)}, u32[]{:S(2)}) collective-permute-start(bf16[768,256]{1,0:T(8,128)(2,1)S(1)} %get-tuple-element.48.refs_6_.refs_12_), channel_id=1, source_target_pairs={{0,8},{4,12},{8,0},{12,4},{16,24},{20,28},{24,16},{28,20},{1,9},{5... | collective-permute-start | bytes 1179656 | tf_op jit(solution)/shard_map/ppermute | solution.py:235
  6.6 0.7 copy-start.17
  6.6 0.7 copy-start.18
  7.3 76.4 %copy-start.6 = (bf16[256,1536]{1,0:T(8,128)(2,1)}, bf16[256,1536]{1,0:T(8,128)(2,1)S(1)}, u32[]{:S(2)}) copy-start(bf16[256,1536]{1,0:T(8,128)(2,1)S(1)} %pad_maximum_fusion.refs_4_) | copy-start | bytes 2359300
  23.3 68.0 %copy-start.14 = (bf16[768,256]{1,0:T(8,128)(2,1)}, bf16[768,256]{1,0:T(8,128)(2,1)S(1)}, u32[]{:S(2)}) copy-start(bf16[768,256]{1,0:T(8,128)(2,1)S(1)} %collective-permute-done.4.refs_8_.refs_14_) | copy-start | bytes 1179652
  25.1 58.6 %copy-start.10 = (bf16[128,2048]{1,0:T(8,128)(2,1)}, bf16[128,2048]{1,0:T(8,128)(2,1)S(1)}, u32[]{:S(2)}) copy-start(bf16[128,2048]{1,0:T(8,128)(2,1)S(1)} %collective-permute-done.3.refs_0_) | copy-start | bytes 1572868
  25.1 26.9 %collective-permute-start.6 = (bf16[256,1536]{1,0:T(8,128)(2,1)S(1)}, bf16[256,1536]{1,0:T(8,128)(2,1)S(1)}, u32[]{:S(2)}, u32[]{:S(2)}) collective-permute-start(bf16[256,1536]{1,0:T(8,128)(2,1)S(1)} %pad_maximum_fusion.refs_4_), channel_id=1, source_target_pairs={{0,8},{4,12},{8,0},{12,4},{16,24},{20,28},{24,16},{28,20},{1,9},{5... | collective-permute-start | bytes 2359304 | tf_op jit(solution)/shard_map/ppermute | solution.py:235
  25.8 36.2 %collective-permute-start.5 = (bf16[256,1536]{1,0:T(8,128)(2,1)S(1)}, bf16[256,1536]{1,0:T(8,128)(2,1)}, u32[]{:S(2)}, u32[]{:S(2)}) collective-permute-start(bf16[256,1536]{1,0:T(8,128)(2,1)S(1)} %pad_maximum_fusion.1), channel_id=1, source_target_pairs={{0,24},{4,28},{8,16},{12,20},{16,8},{20,12},{24,0},{28,4},{1,25},{... | collective-permute-start | bytes 2359304 | tf_op jit(solution)/shard_map/ppermute | solution.py:235
  26.6 14.9 %collective-permute-start.7 = (bf16[128,2048]{1,0:T(8,128)(2,1)S(1)}, bf16[128,2048]{1,0:T(8,128)(2,1)S(1)}, u32[]{:S(2)}, u32[]{:S(2)}) collective-permute-start(bf16[128,2048]{1,0:T(8,128)(2,1)S(1)} %collective-permute-done.3.refs_0_), channel_id=1, source_target_pairs={{0,1},{1,0},{2,3},{3,2},{4,5},{5,4},{6,7},{7,6},{8,9},{9,8},{10,11... | collective-permute-start | bytes 1572872 | tf_op jit(solution)/shard_map/ppermute | solution.py:241
  27.4 24.6 %collective-permute-start.8 = (bf16[128,2048]{1,0:T(8,128)(2,1)S(1)}, bf16[128,2048]{1,0:T(8,128)(2,1)S(1)}, u32[]{:S(2)}, u32[]{:S(2)}) collective-permute-start(bf16[128,2048]{1,0:T(8,128)(2,1)S(1)} %collective-permute-done.3.refs_0_), channel_id=1, source_target_pairs={{0,2},{1,3},{2,0},{3,1},{4,6},{5,7},{6,4},{7,5},{8,10},{9,11},{10,... | collective-permute-start | bytes 1572872 | tf_op jit(solution)/shard_map/ppermute | solution.py:241
  28.9 23.1 %collective-permute-start.9 = (bf16[128,2048]{1,0:T(8,128)(2,1)S(1)}, bf16[128,2048]{1,0:T(8,128)(2,1)S(1)}, u32[]{:S(2)}, u32[]{:S(2)}) collective-permute-start(bf16[128,2048]{1,0:T(8,128)(2,1)S(1)} %collective-permute-done.3.refs_0_), channel_id=1, source_target_pairs={{0,3},{1,2},{2,1},{3,0},{4,7},{5,6},{6,5},{7,4},{8,11},{9,10},{10,... | collective-permute-start | bytes 1572872 | tf_op jit(solution)/shard_map/ppermute | solution.py:241
  41.5 20.6 %copy-start.11 = (bf16[128,2048]{1,0:T(8,128)(2,1)}, bf16[128,2048]{1,0:T(8,128)(2,1)S(1)}, u32[]{:S(2)}) copy-start(bf16[128,2048]{1,0:T(8,128)(2,1)S(1)} %collective-permute-done.7.refs_1_) | copy-start | bytes 1572868
  52.0 30.4 %copy-start.12 = (bf16[128,2048]{1,0:T(8,128)(2,1)}, bf16[128,2048]{1,0:T(8,128)(2,1)S(1)}, u32[]{:S(2)}) copy-start(bf16[128,2048]{1,0:T(8,128)(2,1)S(1)} %collective-permute-done.8.refs_2_) | copy-start | bytes 1572868
  52.0 30.4 %copy-start.13 = (bf16[128,2048]{1,0:T(8,128)(2,1)}, bf16[128,2048]{1,0:T(8,128)(2,1)S(1)}, u32[]{:S(2)}) copy-start(bf16[128,2048]{1,0:T(8,128)(2,1)S(1)} %collective-permute-done.9.refs_3_) | copy-start | bytes 1572868
  52.1 31.0 %copy-start.9 = (bf16[256,1536]{1,0:T(8,128)(2,1)}, bf16[256,1536]{1,0:T(8,128)(2,1)S(1)}, u32[]{:S(2)}) copy-start(bf16[256,1536]{1,0:T(8,128)(2,1)S(1)} %collective-permute-done.6.refs_6_) | copy-start | bytes 2359300
  62.1 20.3 %collective-permute-start.12 = (bf16[256,1536]{1,0:T(8,128)(2,1)}, bf16[256,1536]{1,0:T(8,128)(2,1)}, u32[]{:S(2)}, u32[]{:S(2)}) collective-permute-start(bf16[256,1536]{1,0:T(8,128)(2,1)} %collective-permute-done.5.refs_8_), channel_id=1, source_target_pairs={{0,4},{4,0},{8,12},{12,8},{16,20},{20,16},{24,28},{28,24},{1,5},{5... | collective-permute-start | bytes 2359304 | tf_op jit(solution)/shard_map/ppermute | solution.py:238
  62.1 20.3 %collective-permute-start.14 = (bf16[784,256]{1,0:T(8,128)(2,1)S(1)}, bf16[784,256]{1,0:T(8,128)(2,1)S(1)}, u32[]{:S(2)}, u32[]{:S(2)}) collective-permute-start(bf16[784,256]{1,0:T(8,128)(2,1)S(1)} %pad_maximum_fusion.2), channel_id=1, source_target_pairs={{0,24},{4,28},{8,16},{12,20},{16,8},{20,12},{24,0},{28,4},{1,25},{... | collective-permute-start | bytes 1204232 | tf_op jit(solution)/shard_map/ppermute | solution.py:235
  62.4 21.3 %collective-permute-start.11 = (bf16[256,1536]{1,0:T(8,128)(2,1)S(1)}, bf16[256,1536]{1,0:T(8,128)(2,1)}, u32[]{:S(2)}, u32[]{:S(2)}) collective-permute-start(bf16[256,1536]{1,0:T(8,128)(2,1)S(1)} %collective-permute-done.6.refs_6_), channel_id=1, source_target_pairs={{0,4},{4,0},{8,12},{12,8},{16,20},{20,16},{24,28},{28,24},{1,5},{5... | collective-permute-start | bytes 2359304 | tf_op jit(solution)/shard_map/ppermute | solution.py:238
  62.6 21.1 %collective-permute-start.10 = (bf16[256,1536]{1,0:T(8,128)(2,1)S(1)}, bf16[256,1536]{1,0:T(8,128)(2,1)}, u32[]{:S(2)}, u32[]{:S(2)}) collective-permute-start(bf16[256,1536]{1,0:T(8,128)(2,1)S(1)} %pad_maximum_fusion.refs_4_), channel_id=1, source_target_pairs={{0,4},{4,0},{8,12},{12,8},{16,20},{20,16},{24,28},{28,24},{1,5},{5... | collective-permute-start | bytes 2359304 | tf_op jit(solution)/shard_map/ppermute | solution.py:238
  62.9 28.4 %collective-permute-start.13 = (bf16[256,1536]{1,0:T(8,128)(2,1)}, bf16[256,1536]{1,0:T(8,128)(2,1)}, u32[]{:S(2)}, u32[]{:S(2)}) collective-permute-start(bf16[256,1536]{1,0:T(8,128)(2,1)} %collective-permute-done.5.refs_8_), channel_id=1, source_target_pairs={{0,8},{4,12},{8,0},{12,4},{16,24},{20,28},{24,16},{28,20},{1,9},{5... | collective-permute-start | bytes 2359304 | tf_op jit(solution)/shard_map/ppermute | solution.py:235
  82.4 25.7 %copy-start = (bf16[784,256]{1,0:T(8,128)(2,1)}, bf16[784,256]{1,0:T(8,128)(2,1)S(1)}, u32[]{:S(2)}) copy-start(bf16[784,256]{1,0:T(8,128)(2,1)S(1)} %collective-permute-done.14.refs_18_.refs_2_) | copy-start | bytes 1204228
  82.4 8.9 %collective-permute-start.16 = (bf16[768,256]{1,0:T(8,128)(2,1)S(1)}, bf16[768,256]{1,0:T(8,128)(2,1)}, u32[]{:S(2)}, u32[]{:S(2)}) collective-permute-start(bf16[768,256]{1,0:T(8,128)(2,1)S(1)} %collective-permute-done.4.refs_8_.refs_14_), channel_id=1, source_target_pairs={{0,4},{4,0},{8,12},{12,8},{16,20},{20,16},{24,28},{28,24},{1,5},{5... | collective-permute-start | bytes 1179656 | tf_op jit(solution)/shard_map/ppermute | solution.py:238
  82.4 8.9 %collective-permute-start.15 = (bf16[768,256]{1,0:T(8,128)(2,1)S(1)}, bf16[768,256]{1,0:T(8,128)(2,1)}, u32[]{:S(2)}, u32[]{:S(2)}) collective-permute-start(bf16[768,256]{1,0:T(8,128)(2,1)S(1)} %get-tuple-element.48.refs_6_.refs_12_), channel_id=1, source_target_pairs={{0,4},{4,0},{8,12},{12,8},{16,20},{20,16},{24,28},{28,24},{1,5},{5... | collective-permute-start | bytes 1179656 | tf_op jit(solution)/shard_map/ppermute | solution.py:238
  91.3 3.3 %collective-permute-start.17 = (bf16[256,1536]{1,0:T(8,128)(2,1)}, bf16[256,1536]{1,0:T(8,128)(2,1)S(1)}, u32[]{:S(2)}, u32[]{:S(2)}) collective-permute-start(bf16[256,1536]{1,0:T(8,128)(2,1)} %collective-permute-done.13.refs_4_.refs_10_), channel_id=1, source_target_pairs={{0,4},{4,0},{8,12},{12,8},{16,20},{20,16},{24,28},{28,24},{1,5},{5... | collective-permute-start | bytes 2359304 | tf_op jit(solution)/shard_map/ppermute | solution.py:238
  92.8 11.6 %collective-permute-start.18 = (bf16[784,256]{1,0:T(8,128)(2,1)S(1)}, bf16[784,256]{1,0:T(8,128)(2,1)S(1)}, u32[]{:S(2)}, u32[]{:S(2)}) collective-permute-start(bf16[784,256]{1,0:T(8,128)(2,1)S(1)} %collective-permute-done.14.refs_18_.refs_2_), channel_id=1, source_target_pairs={{0,8},{4,12},{8,0},{12,4},{16,24},{20,28},{24,16},{28,20},{1,9},{5... | collective-permute-start | bytes 1204232 | tf_op jit(solution)/shard_map/ppermute | solution.py:235
  94.6 0.9 copy-start.8
  101.9 6.2 %collective-permute-start.20 = (bf16[784,256]{1,0:T(8,128)(2,1)S(1)}, bf16[784,256]{1,0:T(8,128)(2,1)S(1)}, u32[]{:S(2)}, u32[]{:S(2)}) collective-permute-start(bf16[784,256]{1,0:T(8,128)(2,1)S(1)} %collective-permute-done.14.refs_18_.refs_2_), channel_id=1, source_target_pairs={{0,4},{4,0},{8,12},{12,8},{16,20},{20,16},{24,28},{28,24},{1,5},{5... | collective-permute-start | bytes 1204232 | tf_op jit(solution)/shard_map/ppermute | solution.py:238
  104.3 12.0 %copy-start.1 = (bf16[784,256]{1,0:T(8,128)(2,1)}, bf16[784,256]{1,0:T(8,128)(2,1)S(1)}, u32[]{:S(2)}) copy-start(bf16[784,256]{1,0:T(8,128)(2,1)S(1)} %collective-permute-done.18.refs_16_.refs_0_) | copy-start | bytes 1204228
  104.3 3.8 %collective-permute-start.19 = (bf16[784,256]{1,0:T(8,128)(2,1)S(1)}, bf16[784,256]{1,0:T(8,128)(2,1)S(1)}, u32[]{:S(2)}, u32[]{:S(2)}) collective-permute-start(bf16[784,256]{1,0:T(8,128)(2,1)S(1)} %collective-permute-done.18.refs_16_.refs_0_), channel_id=1, source_target_pairs={{0,4},{4,0},{8,12},{12,8},{16,20},{20,16},{24,28},{28,24},{1,5},{5... | collective-permute-start | bytes 1204232 | tf_op jit(solution)/shard_map/ppermute | solution.py:238
  104.3 10.6 %collective-permute-start.24 = (bf16[128,1024]{1,0:T(8,128)(2,1)}, bf16[128,1024]{1,0:T(8,128)(2,1)}, u32[]{:S(2)}, u32[]{:S(2)}) collective-permute-start(bf16[128,1024]{1,0:T(8,128)(2,1)} %get-tuple-element.60), channel_id=1, source_target_pairs={{0,1},{1,0},{2,3},{3,2},{4,5},{5,4},{6,7},{7,6},{8,9},{9,8},{10,11... | collective-permute-start | bytes 786440 | tf_op jit(solution)/shard_map/ppermute | solution.py:241
  106.1 21.3 %collective-permute-start.25 = (bf16[128,1024]{1,0:T(8,128)(2,1)}, bf16[128,1024]{1,0:T(8,128)(2,1)}, u32[]{:S(2)}, u32[]{:S(2)}) collective-permute-start(bf16[128,1024]{1,0:T(8,128)(2,1)} %get-tuple-element.61), channel_id=1, source_target_pairs={{0,2},{1,3},{2,0},{3,1},{4,6},{5,7},{6,4},{7,5},{8,10},{9,11},{10,... | collective-permute-start | bytes 786440 | tf_op jit(solution)/shard_map/ppermute | solution.py:241
  107.6 20.4 %collective-permute-start.26 = (bf16[128,1024]{1,0:T(8,128)(2,1)}, bf16[128,1024]{1,0:T(8,128)(2,1)}, u32[]{:S(2)}, u32[]{:S(2)}) collective-permute-start(bf16[128,1024]{1,0:T(8,128)(2,1)} %get-tuple-element.62), channel_id=1, source_target_pairs={{0,3},{1,2},{2,1},{3,0},{4,7},{5,6},{6,5},{7,4},{8,11},{9,10},{10,... | collective-permute-start | bytes 786440 | tf_op jit(solution)/shard_map/ppermute | solution.py:241
  108.1 8.2 %copy-start.2 = (bf16[784,256]{1,0:T(8,128)(2,1)}, bf16[784,256]{1,0:T(8,128)(2,1)S(1)}, u32[]{:S(2)}) copy-start(bf16[784,256]{1,0:T(8,128)(2,1)S(1)} %collective-permute-done.20.refs_19_.refs_3_) | copy-start | bytes 1204228
  108.1 1.3 copy-start.4
  109.4 6.9 %copy-start.3 = (bf16[784,256]{1,0:T(8,128)(2,1)}, bf16[784,256]{1,0:T(8,128)(2,1)S(1)}, u32[]{:S(2)}) copy-start(bf16[784,256]{1,0:T(8,128)(2,1)S(1)} %collective-permute-done.19.refs_17_.refs_1_) | copy-start | bytes 1204228
  111.7 17.8 %collective-permute-start.28 = (bf16[128,1024]{1,0:T(8,128)(2,1)}, bf16[128,1024]{1,0:T(8,128)(2,1)}, u32[]{:S(2)}, u32[]{:S(2)}) collective-permute-start(bf16[128,1024]{1,0:T(8,128)(2,1)} %get-tuple-element.65), channel_id=1, source_target_pairs={{0,1},{1,0},{2,3},{3,2},{4,5},{5,4},{6,7},{7,6},{8,9},{9,8},{10,11... | collective-permute-start | bytes 786440 | tf_op jit(solution)/shard_map/ppermute | solution.py:241
  113.3 19.0 %collective-permute-start.29 = (bf16[128,1024]{1,0:T(8,128)(2,1)}, bf16[128,1024]{1,0:T(8,128)(2,1)}, u32[]{:S(2)}, u32[]{:S(2)}) collective-permute-start(bf16[128,1024]{1,0:T(8,128)(2,1)} %get-tuple-element.67), channel_id=1, source_target_pairs={{0,2},{1,3},{2,0},{3,1},{4,6},{5,7},{6,4},{7,5},{8,10},{9,11},{10,... | collective-permute-start | bytes 786440 | tf_op jit(solution)/shard_map/ppermute | solution.py:241
  114.9 18.7 %collective-permute-start.30 = (bf16[128,1024]{1,0:T(8,128)(2,1)}, bf16[128,1024]{1,0:T(8,128)(2,1)}, u32[]{:S(2)}, u32[]{:S(2)}) collective-permute-start(bf16[128,1024]{1,0:T(8,128)(2,1)} %get-tuple-element.69), channel_id=1, source_target_pairs={{0,3},{1,2},{2,1},{3,0},{4,7},{5,6},{6,5},{7,4},{8,11},{9,10},{10,... | collective-permute-start | bytes 786440 | tf_op jit(solution)/shard_map/ppermute | solution.py:241
  127.3 28.8 %copy-start.5 = (bf16[128,2048]{1,0:T(8,128)(2,1)S(1)}, bf16[128,2048]{1,0:T(8,128)(2,1)}, u32[]{:S(2)}) copy-start(bf16[128,2048]{1,0:T(8,128)(2,1)} %get-tuple-element.55.refs_0_) | copy-start | bytes 1572868
  127.3 25.3 %collective-permute-start.21 = (bf16[128,2048]{1,0:T(8,128)(2,1)}, bf16[128,2048]{1,0:T(8,128)(2,1)S(1)}, u32[]{:S(2)}, u32[]{:S(2)}) collective-permute-start(bf16[128,2048]{1,0:T(8,128)(2,1)} %get-tuple-element.56), channel_id=1, source_target_pairs={{0,1},{1,0},{2,3},{3,2},{4,5},{5,4},{6,7},{7,6},{8,9},{9,8},{10,11... | collective-permute-start | bytes 1572872 | tf_op jit(solution)/shard_map/ppermute | solution.py:241
  128.0 26.0 %collective-permute-start.22 = (bf16[128,2048]{1,0:T(8,128)(2,1)}, bf16[128,2048]{1,0:T(8,128)(2,1)S(1)}, u32[]{:S(2)}, u32[]{:S(2)}) collective-permute-start(bf16[128,2048]{1,0:T(8,128)(2,1)} %get-tuple-element.57), channel_id=1, source_target_pairs={{0,2},{1,3},{2,0},{3,1},{4,6},{5,7},{6,4},{7,5},{8,10},{9,11},{10,... | collective-permute-start | bytes 1572872 | tf_op jit(solution)/shard_map/ppermute | solution.py:241
  129.5 24.5 %collective-permute-start.23 = (bf16[128,2048]{1,0:T(8,128)(2,1)}, bf16[128,2048]{1,0:T(8,128)(2,1)S(1)}, u32[]{:S(2)}, u32[]{:S(2)}) collective-permute-start(bf16[128,2048]{1,0:T(8,128)(2,1)} %get-tuple-element.58), channel_id=1, source_target_pairs={{0,3},{1,2},{2,1},{3,0},{4,7},{5,6},{6,5},{7,4},{8,11},{9,10},{10,... | collective-permute-start | bytes 1572872 | tf_op jit(solution)/shard_map/ppermute | solution.py:241
  132.4 20.3 %collective-permute-start.27 = (bf16[128,1024]{1,0:T(8,128)(2,1)S(1)}, bf16[128,1024]{1,0:T(8,128)(2,1)S(1)}, u32[]{:S(2)}, u32[]{:S(2)}) collective-permute-start(bf16[128,1024]{1,0:T(8,128)(2,1)S(1)} %add_convert_fusion.1), channel_id=1, source_target_pairs={{0,24},{4,28},{8,16},{12,20},{16,8},{20,12},{24,0},{28,4},{1,25},{... | collective-permute-start | bytes 786440 | tf_op jit(solution)/shard_map/ppermute | solution.py:235
  135.7 20.4 %collective-permute-start.31 = (bf16[128,1024]{1,0:T(8,128)(2,1)}, bf16[128,1024]{1,0:T(8,128)(2,1)S(1)}, u32[]{:S(2)}, u32[]{:S(2)}) collective-permute-start(bf16[128,1024]{1,0:T(8,128)(2,1)} %add_convert_fusion), channel_id=1, source_target_pairs={{0,24},{4,28},{8,16},{12,20},{16,8},{20,12},{24,0},{28,4},{1,25},{... | collective-permute-start | bytes 786440 | tf_op jit(solution)/shard_map/ppermute | solution.py:235

commit v6 on v5

--- a/solution.py
+++ b/solution.py
@@ -102,19 +102,22 @@
             up_out[...] = sums[:, tile:]
 
 
-def late_kernel(blocks, slices, down_slices, tile, summed, numbers_ref, *refs):
+def late_kernel(blocks, pieces, down_slices, tile, summed, numbers_ref, *refs):
     row_refs, refs = refs[:blocks], refs[blocks:]
-    weight_refs, refs = refs[:slices], refs[slices:]
+    slices = len(pieces)
+    weight_refs, refs = refs[: sum(pieces)], refs[sum(pieces) :]
     down_refs, refs = refs[:down_slices], refs[down_slices:]
     sums_in, refs = refs[:summed], refs[summed:]
     hidden, out_refs, refs = refs[0], refs[1 : 1 + blocks], refs[1 + blocks :]
     sums, (rows, weights, down, sems) = refs[:summed], refs[summed:]
-    depth, both = weight_refs[0].shape
+    depth, both = weight_refs[0].shape[0], weights.shape[1]
     loads = Loads(sems)
     first = row_loads(loads, row_refs, rows, numbers_ref, slices, depth)
-    for k, weight_ref in enumerate(weight_refs):
-        place = pl.ds(pl.multiple_of(numbers_ref[k], LANES), depth)
-        first.append(loads.add(weight_ref, weights.at[place]))
+    left = list(weight_refs)
+    for k, number in enumerate(pieces):
+        place, width = pl.ds(pl.multiple_of(numbers_ref[k], LANES), depth), both // number
+        for part in range(number):
+            first.append(loads.add(left.pop(0), weights.at[place, pl.ds(part * width, width)]))
     first += [loads.add(source, target) for source, target in zip(sums_in, sums)]
     final = [loads.add(ref.at[pl.ds(0, both // 2)], down.at[k]) for k, ref in enumerate(down_refs)]
     for copy in first + final:
@@ -168,15 +171,17 @@
 
 def late_outputs(row_blocks, gate_up, down, numbers, early):
     blocks, slices, down_slices = len(row_blocks), len(gate_up), len(down)
-    depth, both = gate_up[0].shape
+    depth, both = gate_up[0][0].shape[0], sum(piece.shape[1] for piece in gate_up[0])
+    pieces = tuple(len(parts) for parts in gate_up)
+    gate_up = [piece for parts in gate_up for piece in parts]
     tok_rows = row_blocks[0].shape[0]
     count, inner = blocks * tok_rows, both // 2
     tile = 256 if inner % 256 == 0 else inner
     whole = pl.BlockSpec(memory_space=pltpu.VMEM)
     out = jax.ShapeDtypeStruct((tok_rows, down_slices * depth), jnp.bfloat16)
     results = pl.pallas_call(
-        functools.partial(late_kernel, blocks, slices, down_slices, tile, len(early)),
-        in_specs=[SMEM] + [ANY] * (blocks + slices + down_slices + len(early)),
+        functools.partial(late_kernel, blocks, pieces, down_slices, tile, len(early)),
+        in_specs=[SMEM] + [ANY] * (blocks + len(gate_up) + down_slices + len(early)),
         out_specs=[whole] * (1 + blocks),
         out_shape=[jax.ShapeDtypeStruct((count, inner), jnp.bfloat16)] + [out] * blocks,
         scratch_shapes=[pltpu.VMEM((count, inner), jnp.float32)] * len(early)
@@ -184,7 +189,7 @@
             pltpu.VMEM((count, slices * depth), jnp.bfloat16),
             pltpu.VMEM((slices * depth, both), jnp.bfloat16),
             pltpu.VMEM((down_slices, inner, down[0].shape[1]), jnp.bfloat16),
-            pltpu.SemaphoreType.DMA((slices // 2 * blocks + slices + 2 + down_slices,)),
+            pltpu.SemaphoreType.DMA((slices // 2 * blocks + len(gate_up) + 2 + down_slices,)),
         ],
         compiler_params=pltpu.CompilerParams(vmem_limit_bytes=62 * 1024 * 1024),
         cost_estimate=FREE,
@@ -310,7 +315,9 @@
     dn_core = {mask: swap_core(after(dn[mask], dn[mirror])) for mask in near}
     wave = [*settled, *[dn_core[mask] for mask in near]]
     for mask in near[1:]:
-        gu_core[mask ^ mirror] = swap_core(after(gu[mask ^ mirror], *wave))
+        held = after(gu[mask ^ mirror], *wave)
+        parts = (held[:, : held.shape[1] // 2], held[:, held.shape[1] // 2 :])
+        gu_core[mask ^ mirror] = [swap_core(part) for part in parts]
 
     far_gates = gates_of(unpack(dn[mirror][w_down.shape[1] :], tok_rows, experts))
 
@@ -328,7 +335,7 @@
         counted = jnp.concatenate([places_of(gate_masks), numbers(columns)])
         hidden, parts = [], []
         for chunk, sums in zip(chunks, early):
-            pieces = both_cores(gu, gu_core, gate_masks)
+            pieces = [found if isinstance(found, list) else [found] for found in both_cores(gu, gu_core, gate_masks)]
             rows, blocks = late_outputs(chunk, pieces, both_cores(dn, dn_core, down_masks), counted, sums)
             hidden.append(rows)
             parts += blocks

time: 160 us -> 158 us (0.988)
    ppermute x8 -> x9, waiting for transfers between devices: 0.02 us -> 1.69 us  [swap_core(): return lax.ppermute(array, 'dp', [(i, i ^ 1) for i in range(lines)])]
  transfers between devices with their start and end apart: 32 -> 33, of which waited for: 12 -> 12; matrix products, arithmetic and copies ran while one was open for 5% -> 5% of each run, Pallas kernels for 17% -> 17%
where the time goes in v6:
time: 158 us; the launch traced here: 157 us
  waiting for transfers between devices  90.5 us (57%)
  Pallas kernels  29 us (18%)
  starting transfers between devices  27.5 us (17%)
  local copies, waits for them, and re-layouts  5.89 us (4%)
  other arithmetic  4.1 us (3%)
    ppermute x9, waiting for transfers between devices, swap_layer(): return lax.ppermute(array, 'dp', [(i, i ^ 2 * mask) for i in range(lines)])  66.2 us
    ppermute x15, waiting for transfers between devices, swap_place(): return lax.ppermute(array, 'expert', [(i, i ^ mask) for i in range(places)])  22.6 us
    ppermute x15, starting transfers between devices, swap_place(): return lax.ppermute(array, 'expert', [(i, i ^ mask) for i in range(places)])  18.5 us
    pallas_call x2, Pallas kernels, late_outputs(): pl.pallas_call(functools.partial(late_kernel, blocks, pieces, down_slices...  17.3 us
    pallas_call x1, Pallas kernels, early_sums(): pl.pallas_call(functools.partial(early_kernel, blocks, slices), grid=(til...  7.39 us
    ppermute x9, starting transfers between devices, swap_layer(): return lax.ppermute(array, 'dp', [(i, i ^ 2 * mask) for i in range(lines)])  7.2 us
    convert_element_type x2, other arithmetic, add_up(): return total.astype(jnp.bfloat16)  3.54 us
  transfers between devices with their start and end apart: 33, of which 12 were waited for; matrix products, arithmetic and copies ran while one was open for 5% of the time, Pallas kernels for 17%

profile of v6, /device:TPU:16, one launch (start us, length us, event | category | flops | bytes accessed | tf_op | source)
XLA Modules:
  0.0 157.3 jit_solution(14638076028939830868)
XLA Ops:
  0.0 0.4 collective-permute-start.3
  0.5 1.5 collective-permute-start
  1.9 1.5 collective-permute-start.1
  3.5 0.5 collective-permute-start.2
  3.9 1.2 dynamic-slice_bitcast_fusion
  5.2 1.3 collective-permute-start.4
  6.5 0.1 dynamic-slice_bitcast_fusion.4
  6.7 0.6 copy-done.15
  7.3 0.2 copy.15
  7.5 0.1 reshape.37
  7.8 15.5 %collective-permute-done.4.refs_9_.refs_15_ = bf16[768,256]{1,0:T(8,128)(2,1)} collective-permute-done((bf16[768,256]{1,0:T(8,128)(2,1)S(1)}, bf16[768,256]{1,0:T(8,128)(2,1)}, u32[]{:S(2)}, u32[]{:S(2)}) %collective-permute-start.4) | collective-permute-done | bytes 393248 | tf_op jit(solution)/shard_map/ppermute | solution.py:240
  23.3 1.8 %collective-permute-done.3.refs_0_ = bf16[128,2048]{1,0:T(8,128)(2,1)S(1)} collective-permute-done((bf16[128,2048]{1,0:T(8,128)(2,1)}, bf16[128,2048]{1,0:T(8,128)(2,1)S(1)}, u32[]{:S(2)}, u32[]{:S(2)}) %collective-permute-start.3) | collective-permute-done | bytes 524320 | tf_op jit(solution)/shard_map/ppermute | solution.py:240
  25.1 0.8 collective-permute-start.6
  25.9 0.7 collective-permute-done.1.refs_2_
  26.6 0.9 collective-permute-start.7
  27.5 1.5 collective-permute-start.8
  29.0 1.1 collective-permute-start.9
  30.1 11.4 %collective-permute-done.7.refs_1_ = bf16[128,2048]{1,0:T(8,128)(2,1)S(1)} collective-permute-done((bf16[128,2048]{1,0:T(8,128)(2,1)S(1)}, bf16[128,2048]{1,0:T(8,128)(2,1)S(1)}, u32[]{:S(2)}, u32[]{:S(2)}) %collective-permute-start.7) | collective-permute-done | bytes 524320 | tf_op jit(solution)/shard_map/ppermute | solution.py:246
  41.5 10.5 %collective-permute-done.8.refs_2_ = bf16[128,2048]{1,0:T(8,128)(2,1)S(1)} collective-permute-done((bf16[128,2048]{1,0:T(8,128)(2,1)S(1)}, bf16[128,2048]{1,0:T(8,128)(2,1)S(1)}, u32[]{:S(2)}, u32[]{:S(2)}) %collective-permute-start.8) | collective-permute-done | bytes 524320 | tf_op jit(solution)/shard_map/ppermute | solution.py:246
  52.0 10.0 %collective-permute-done.5.refs_8_ = bf16[256,1536]{1,0:T(8,128)(2,1)} collective-permute-done((bf16[256,1536]{1,0:T(8,128)(2,1)S(1)}, bf16[256,1536]{1,0:T(8,128)(2,1)}, u32[]{:S(2)}, u32[]{:S(2)}) %collective-permute-start.5) | collective-permute-done | bytes 786464 | tf_op jit(solution)/shard_map/ppermute | solution.py:240
  62.0 0.3 collective-permute-start.14
  62.4 0.2 collective-permute-start.11
  62.6 0.3 collective-permute-start.10
  62.9 2.2 %collective-permute-start.13 = (bf16[256,1536]{1,0:T(8,128)(2,1)}, bf16[256,1536]{1,0:T(8,128)(2,1)S(1)}, u32[]{:S(2)}, u32[]{:S(2)}) collective-permute-start(bf16[256,1536]{1,0:T(8,128)(2,1)} %collective-permute-done.5.refs_8_), channel_id=1, source_target_pairs={{0,8},{4,12},{8,0},{12,4},{16,24},{20,28},{24,16},{28,20},{1,9},{5... | collective-permute-start | bytes 2359304 | tf_op jit(solution)/shard_map/ppermute | solution.py:240
  65.1 17.2 %collective-permute-done.14.refs_19_.refs_2_ = bf16[784,256]{1,0:T(8,128)(2,1)S(1)} collective-permute-done((bf16[784,256]{1,0:T(8,128)(2,1)S(1)}, bf16[784,256]{1,0:T(8,128)(2,1)S(1)}, u32[]{:S(2)}, u32[]{:S(2)}) %collective-permute-start.14) | collective-permute-done | bytes 401440 | tf_op jit(solution)/shard_map/ppermute | solution.py:240
  82.4 0.5 collective-permute-start.15
  82.9 0.6 concatenate.23.numbers_ref
  83.5 0.7 stack.163.numbers_ref
  84.2 0.6 concatenate.18.numbers_ref
  84.8 7.4 %shard_map.64 = (f32[512,768]{1,0:T(8,128)}, f32[512,768]{1,0:T(8,128)}) custom-call(s32[9]{0:T(128)} %stack.163.numbers_ref, bf16[128,2048]{1,0:T(8,128)(2,1)} %copy-done.9, bf16[128,2048]{1,0:T(8,128)(2,1)} %copy-done.10, bf16[128,2048]{1,0:T(8,128)(2,1)} %copy-done.11, bf16[128,2048]{1,0:T(8,128)(2,1)} %copy-done.12, bf16[256,1536]{1,0:T(8,128)(2,1)} %copy-done.7, ...), custom_call_target="tpu_custom_call" | custom-call | tf_op jit(solution)/shard_map/pallas_call | solution.py:156
  92.2 0.1 collective-permute-start.19
  92.4 0.2 collective-permute-start.17
  92.6 0.3 collective-permute-start.18
  93.0 0.1 pad_add_fusion.2.numbers_ref
  93.0 0.1 pad_add_fusion.1
  93.1 0.1 iota_compare_fusion.1
  93.2 1.1 collective-permute-done.17.refs_5_.refs_11_
  94.3 0.6 collective-permute-done.18.refs_6_.refs_12_
  94.9 6.3 %shard_map.65 = (bf16[512,768]{1,0:T(8,128)(2,1)}, bf16[128,1024]{1,0:T(8,128)(2,1)}, bf16[128,1024]{1,0:T(8,128)(2,1)}, bf16[128,1024]{1,0:T(8,128)(2,1)}, bf16[128,1024]{1,0:T(8,128)(2,1)}) custom-call(s32[7]{0:T(128)} %concatenate.23.numbers_ref, bf16[128,2048]{1,0:T(8,128)(2,1)} %copy-done.9, bf16[128,2048]{1,0:T(8,128)(2,1)} %copy-done.10, ...), custom_call_target="tpu_custom_call" | custom-call | tf_op jit(solution)/shard_map/pallas_call | solution.py:182
  101.2 0.2 collective-permute-start.21
  101.4 2.2 %collective-permute-done.19.refs_17_.refs_0_ = bf16[784,256]{1,0:T(8,128)(2,1)S(1)} collective-permute-done((bf16[784,256]{1,0:T(8,128)(2,1)S(1)}, bf16[784,256]{1,0:T(8,128)(2,1)S(1)}, u32[]{:S(2)}, u32[]{:S(2)}) %collective-permute-start.19) | collective-permute-done | bytes 401440 | tf_op jit(solution)/shard_map/ppermute | solution.py:240
  103.6 1.6 collective-permute-start.25
  105.2 0.1 add.106
  105.4 1.6 collective-permute-start.26
  106.9 0.5 collective-permute-start.27
  107.4 1.3 copy-done.4
  108.7 2.4 %shard_map.67 = (bf16[128,1024]{1,0:T(8,128)(2,1)S(1)}, bf16[128,1024]{1,0:T(8,128)(2,1)}, bf16[128,1024]{1,0:T(8,128)(2,1)}, bf16[128,1024]{1,0:T(8,128)(2,1)}) custom-call(s32[4]{0:T(128)S(1)} %pad_add_fusion.2.numbers_ref, bf16[512,768]{1,0:T(8,128)(2,1)S(1)} %copy-done.4, bf16[784,256]{1,0:T(8,128)(2,1)S(1)} %collective-permute-done.19.refs_17_.refs_0_, ...), custom_call_target="tpu_custom_call" | custom-call | tf_op jit(solution)/shard_map/pallas_call | solution.py:208
  111.1 1.5 collective-permute-start.29
  112.6 0.1 select_reduce_fusion
  112.7 1.6 %collective-permute-start.30 = (bf16[128,1024]{1,0:T(8,128)(2,1)}, bf16[128,1024]{1,0:T(8,128)(2,1)}, u32[]{:S(2)}, u32[]{:S(2)}) collective-permute-start(bf16[128,1024]{1,0:T(8,128)(2,1)} %get-tuple-element.67), channel_id=1, source_target_pairs={{0,2},{1,3},{2,0},{3,1},{4,6},{5,7},{6,4},{7,5},{8,10},{9,11},{10,... | collective-permute-start | bytes 786440 | tf_op jit(solution)/shard_map/ppermute | solution.py:246
  114.3 1.3 collective-permute-start.31
  115.6 11.0 %shard_map.66 = (bf16[512,768]{1,0:T(8,128)(2,1)}, bf16[128,2048]{1,0:T(8,128)(2,1)}, bf16[128,2048]{1,0:T(8,128)(2,1)}, bf16[128,2048]{1,0:T(8,128)(2,1)}, bf16[128,2048]{1,0:T(8,128)(2,1)}) custom-call(s32[20]{0:T(128)} %concatenate.18.numbers_ref, bf16[128,2048]{1,0:T(8,128)(2,1)} %refs_0_.1, bf16[128,2048]{1,0:T(8,128)(2,1)} %collective-permute-done.refs_1_, ...), custom_call_target="tpu_custom_call" | custom-call | tf_op jit(solution)/shard_map/pallas_call | solution.py:182
  126.6 0.7 collective-permute-start.22
  127.3 1.5 collective-permute-start.23
  128.9 1.3 collective-permute-start.24
  130.2 1.5 add_convert_fusion.1
  131.6 0.3 collective-permute-start.28
  132.0 2.1 %add_convert_fusion = bf16[128,1024]{1,0:T(8,128)(2,1)} fusion(bf16[128,1024]{1,0:T(8,128)(2,1)} %collective-permute-done.31, bf16[128,1024]{1,0:T(8,128)(2,1)} %collective-permute-done.30, bf16[128,1024]{1,0:T(8,128)(2,1)} %collective-permute-done.29, bf16[128,1024]{1,0:T(8,128)(2,1)S(1)} %get-tuple-element.64, f32[128]{0:T(128)S(1)} %get-tuple-element.85, ...), kind=kLoop, calls=%fused_computation.2 | loop fusion | flops 1572864 | bytes 1312768 | tf_op jit(solution)/shard_map/convert_element_type | solution.py:331
  134.1 1.7 %collective-permute-start.32 = (bf16[128,1024]{1,0:T(8,128)(2,1)}, bf16[128,1024]{1,0:T(8,128)(2,1)S(1)}, u32[]{:S(2)}, u32[]{:S(2)}) collective-permute-start(bf16[128,1024]{1,0:T(8,128)(2,1)} %add_convert_fusion), channel_id=1, source_target_pairs={{0,24},{4,28},{8,16},{12,20},{16,8},{20,12},{24,0},{28,4},{1,25},{... | collective-permute-start | bytes 786440 | tf_op jit(solution)/shard_map/ppermute | solution.py:240
  135.8 0.1 pad_add_fusion.bases_ref
  135.9 0.1 copy.17.gates_ref
  136.0 14.6 %collective-permute-done.28.refs_4_ = bf16[128,1024]{1,0:T(8,128)(2,1)S(1)} collective-permute-done((bf16[128,1024]{1,0:T(8,128)(2,1)S(1)}, bf16[128,1024]{1,0:T(8,128)(2,1)S(1)}, u32[]{:S(2)}, u32[]{:S(2)}) %collective-permute-start.28) | collective-permute-done | bytes 262176 | tf_op jit(solution)/shard_map/ppermute | solution.py:240
  150.6 4.8 %collective-permute-done.32.refs_5_ = bf16[128,1024]{1,0:T(8,128)(2,1)S(1)} collective-permute-done((bf16[128,1024]{1,0:T(8,128)(2,1)}, bf16[128,1024]{1,0:T(8,128)(2,1)S(1)}, u32[]{:S(2)}, u32[]{:S(2)}) %collective-permute-start.32) | collective-permute-done | bytes 262176 | tf_op jit(solution)/shard_map/ppermute | solution.py:240
  155.5 1.9 %shard_map.68 = bf16[128,2048]{1,0:T(8,128)(2,1)} custom-call(s32[2]{0:T(128)S(1)} %pad_add_fusion.bases_ref, f32[128,4]{1,0:T(8,128)S(1)} %copy.17.gates_ref, bf16[128,2048]{1,0:T(8,128)(2,1)S(1)} %copy-done.5, bf16[128,2048]{1,0:T(8,128)(2,1)S(1)} %collective-permute-done.22.refs_1_, bf16[128,2048]{1,0:T(8,128)(2,1)S(1)} %collective-permute-done.23.refs_2_, ...), custom_call_target="tpu_custom_call" | custom-call | tf_op jit(solution)/shard_map/pallas_call | solution.py:362
  (70 shorter events, 0.4 us)
Async XLA Ops:
  0.0 6.5 %copy-start.13 = (bf16[2,256,768]{2,1,0:T(8,128)(2,1)S(1)}, bf16[2,256,768]{2,1,0:T(8,128)(2,1)}, u32[]{:S(2)}) copy-start(bf16[2,256,768]{2,1,0:T(8,128)(2,1)} %param.11) | copy-start | bytes 2359300
  0.0 25.1 %collective-permute-start.3 = (bf16[128,2048]{1,0:T(8,128)(2,1)}, bf16[128,2048]{1,0:T(8,128)(2,1)S(1)}, u32[]{:S(2)}, u32[]{:S(2)}) collective-permute-start(bf16[128,2048]{1,0:T(8,128)(2,1)} %refs_0_.1), channel_id=1, source_target_pairs={{0,24},{4,28},{8,16},{12,20},{16,8},{20,12},{24,0},{28,4},{1,25},{... | collective-permute-start | bytes 1572872 | tf_op jit(solution)/shard_map/ppermute | solution.py:240
  0.5 25.4 %collective-permute-start = (bf16[128,2048]{1,0:T(8,128)(2,1)}, bf16[128,2048]{1,0:T(8,128)(2,1)}, u32[]{:S(2)}, u32[]{:S(2)}) collective-permute-start(bf16[128,2048]{1,0:T(8,128)(2,1)} %refs_0_.1), channel_id=1, source_target_pairs={{0,1},{1,0},{2,3},{3,2},{4,5},{5,4},{6,7},{7,6},{8,9},{9,8},{10,11... | collective-permute-start | bytes 1572872 | tf_op jit(solution)/shard_map/ppermute | solution.py:246
  1.9 24.7 %collective-permute-start.1 = (bf16[128,2048]{1,0:T(8,128)(2,1)}, bf16[128,2048]{1,0:T(8,128)(2,1)}, u32[]{:S(2)}, u32[]{:S(2)}) collective-permute-start(bf16[128,2048]{1,0:T(8,128)(2,1)} %refs_0_.1), channel_id=1, source_target_pairs={{0,2},{1,3},{2,0},{3,1},{4,6},{5,7},{6,4},{7,5},{8,10},{9,11},{10,... | collective-permute-start | bytes 1572872 | tf_op jit(solution)/shard_map/ppermute | solution.py:246
  3.5 25.5 %collective-permute-start.2 = (bf16[128,2048]{1,0:T(8,128)(2,1)}, bf16[128,2048]{1,0:T(8,128)(2,1)}, u32[]{:S(2)}, u32[]{:S(2)}) collective-permute-start(bf16[128,2048]{1,0:T(8,128)(2,1)} %refs_0_.1), channel_id=1, source_target_pairs={{0,3},{1,2},{2,1},{3,0},{4,7},{5,6},{6,5},{7,4},{8,11},{9,10},{10,... | collective-permute-start | bytes 1572872 | tf_op jit(solution)/shard_map/ppermute | solution.py:246
  3.9 2.5 %copy-start.14 = (bf16[2,256,768]{2,1,0:T(8,128)(2,1)S(1)}, bf16[2,256,768]{2,1,0:T(8,128)(2,1)}, u32[]{:S(2)}) copy-start(bf16[2,256,768]{2,1,0:T(8,128)(2,1)} %param.10) | copy-start | bytes 2359300
  5.2 77.2 %copy-start.8 = (bf16[768,256]{1,0:T(8,128)(2,1)}, bf16[768,256]{1,0:T(8,128)(2,1)S(1)}, u32[]{:S(2)}) copy-start(bf16[768,256]{1,0:T(8,128)(2,1)S(1)} %get-tuple-element.48.refs_7_.refs_13_) | copy-start | bytes 1179652
  5.2 18.1 %collective-permute-start.4 = (bf16[768,256]{1,0:T(8,128)(2,1)S(1)}, bf16[768,256]{1,0:T(8,128)(2,1)}, u32[]{:S(2)}, u32[]{:S(2)}) collective-permute-start(bf16[768,256]{1,0:T(8,128)(2,1)S(1)} %get-tuple-element.48.refs_7_.refs_13_), channel_id=1, source_target_pairs={{0,8},{4,12},{8,0},{12,4},{16,24},{20,28},{24,16},{28,20},{1,9},{5... | collective-permute-start | bytes 1179656 | tf_op jit(solution)/shard_map/ppermute | solution.py:240
  6.6 0.7 copy-start.15
  6.6 0.7 copy-start.16
  7.3 75.0 %copy-start.7 = (bf16[256,1536]{1,0:T(8,128)(2,1)}, bf16[256,1536]{1,0:T(8,128)(2,1)S(1)}, u32[]{:S(2)}) copy-start(bf16[256,1536]{1,0:T(8,128)(2,1)S(1)} %pad_maximum_fusion.refs_4_) | copy-start | bytes 2359300
  25.1 57.8 %copy-start.9 = (bf16[128,2048]{1,0:T(8,128)(2,1)}, bf16[128,2048]{1,0:T(8,128)(2,1)S(1)}, u32[]{:S(2)}) copy-start(bf16[128,2048]{1,0:T(8,128)(2,1)S(1)} %collective-permute-done.3.refs_0_) | copy-start | bytes 1572868
  25.1 26.9 %collective-permute-start.6 = (bf16[256,1536]{1,0:T(8,128)(2,1)S(1)}, bf16[256,1536]{1,0:T(8,128)(2,1)}, u32[]{:S(2)}, u32[]{:S(2)}) collective-permute-start(bf16[256,1536]{1,0:T(8,128)(2,1)S(1)} %pad_maximum_fusion.refs_4_), channel_id=1, source_target_pairs={{0,8},{4,12},{8,0},{12,4},{16,24},{20,28},{24,16},{28,20},{1,9},{5... | collective-permute-start | bytes 2359304 | tf_op jit(solution)/shard_map/ppermute | solution.py:240
  25.9 36.1 %collective-permute-start.5 = (bf16[256,1536]{1,0:T(8,128)(2,1)S(1)}, bf16[256,1536]{1,0:T(8,128)(2,1)}, u32[]{:S(2)}, u32[]{:S(2)}) collective-permute-start(bf16[256,1536]{1,0:T(8,128)(2,1)S(1)} %pad_maximum_fusion.1), channel_id=1, source_target_pairs={{0,24},{4,28},{8,16},{12,20},{16,8},{20,12},{24,0},{28,4},{1,25},{... | collective-permute-start | bytes 2359304 | tf_op jit(solution)/shard_map/ppermute | solution.py:240
  26.6 14.9 %collective-permute-start.7 = (bf16[128,2048]{1,0:T(8,128)(2,1)S(1)}, bf16[128,2048]{1,0:T(8,128)(2,1)S(1)}, u32[]{:S(2)}, u32[]{:S(2)}) collective-permute-start(bf16[128,2048]{1,0:T(8,128)(2,1)S(1)} %collective-permute-done.3.refs_0_), channel_id=1, source_target_pairs={{0,1},{1,0},{2,3},{3,2},{4,5},{5,4},{6,7},{7,6},{8,9},{9,8},{10,11... | collective-permute-start | bytes 1572872 | tf_op jit(solution)/shard_map/ppermute | solution.py:246
  27.5 24.5 %collective-permute-start.8 = (bf16[128,2048]{1,0:T(8,128)(2,1)S(1)}, bf16[128,2048]{1,0:T(8,128)(2,1)S(1)}, u32[]{:S(2)}, u32[]{:S(2)}) collective-permute-start(bf16[128,2048]{1,0:T(8,128)(2,1)S(1)} %collective-permute-done.3.refs_0_), channel_id=1, source_target_pairs={{0,2},{1,3},{2,0},{3,1},{4,6},{5,7},{6,4},{7,5},{8,10},{9,11},{10,... | collective-permute-start | bytes 1572872 | tf_op jit(solution)/shard_map/ppermute | solution.py:246
  29.0 23.0 %collective-permute-start.9 = (bf16[128,2048]{1,0:T(8,128)(2,1)S(1)}, bf16[128,2048]{1,0:T(8,128)(2,1)S(1)}, u32[]{:S(2)}, u32[]{:S(2)}) collective-permute-start(bf16[128,2048]{1,0:T(8,128)(2,1)S(1)} %collective-permute-done.3.refs_0_), channel_id=1, source_target_pairs={{0,3},{1,2},{2,1},{3,0},{4,7},{5,6},{6,5},{7,4},{8,11},{9,10},{10,... | collective-permute-start | bytes 1572872 | tf_op jit(solution)/shard_map/ppermute | solution.py:246
  41.5 20.6 %copy-start.10 = (bf16[128,2048]{1,0:T(8,128)(2,1)}, bf16[128,2048]{1,0:T(8,128)(2,1)S(1)}, u32[]{:S(2)}) copy-start(bf16[128,2048]{1,0:T(8,128)(2,1)S(1)} %collective-permute-done.7.refs_1_) | copy-start | bytes 1572868
  52.0 10.1 %copy-start.11 = (bf16[128,2048]{1,0:T(8,128)(2,1)}, bf16[128,2048]{1,0:T(8,128)(2,1)S(1)}, u32[]{:S(2)}) copy-start(bf16[128,2048]{1,0:T(8,128)(2,1)S(1)} %collective-permute-done.8.refs_2_) | copy-start | bytes 1572868
  52.0 10.6 %copy-start.12 = (bf16[128,2048]{1,0:T(8,128)(2,1)}, bf16[128,2048]{1,0:T(8,128)(2,1)S(1)}, u32[]{:S(2)}) copy-start(bf16[128,2048]{1,0:T(8,128)(2,1)S(1)} %collective-permute-done.9.refs_3_) | copy-start | bytes 1572868
  62.0 20.3 %collective-permute-start.12 = (bf16[256,1536]{1,0:T(8,128)(2,1)}, bf16[256,1536]{1,0:T(8,128)(2,1)}, u32[]{:S(2)}, u32[]{:S(2)}) collective-permute-start(bf16[256,1536]{1,0:T(8,128)(2,1)} %collective-permute-done.5.refs_8_), channel_id=1, source_target_pairs={{0,4},{4,0},{8,12},{12,8},{16,20},{20,16},{24,28},{28,24},{1,5},{5... | collective-permute-start | bytes 2359304 | tf_op jit(solution)/shard_map/ppermute | solution.py:243
  62.0 20.3 %collective-permute-start.14 = (bf16[784,256]{1,0:T(8,128)(2,1)S(1)}, bf16[784,256]{1,0:T(8,128)(2,1)S(1)}, u32[]{:S(2)}, u32[]{:S(2)}) collective-permute-start(bf16[784,256]{1,0:T(8,128)(2,1)S(1)} %pad_maximum_fusion.2), channel_id=1, source_target_pairs={{0,24},{4,28},{8,16},{12,20},{16,8},{20,12},{24,0},{28,4},{1,25},{... | collective-permute-start | bytes 1204232 | tf_op jit(solution)/shard_map/ppermute | solution.py:240
  62.4 22.4 %collective-permute-start.11 = (bf16[256,1536]{1,0:T(8,128)(2,1)}, bf16[256,1536]{1,0:T(8,128)(2,1)}, u32[]{:S(2)}, u32[]{:S(2)}) collective-permute-start(bf16[256,1536]{1,0:T(8,128)(2,1)} %collective-permute-done.6.refs_6_), channel_id=1, source_target_pairs={{0,4},{4,0},{8,12},{12,8},{16,20},{20,16},{24,28},{28,24},{1,5},{5... | collective-permute-start | bytes 2359304 | tf_op jit(solution)/shard_map/ppermute | solution.py:243
  62.6 22.2 %collective-permute-start.10 = (bf16[256,1536]{1,0:T(8,128)(2,1)S(1)}, bf16[256,1536]{1,0:T(8,128)(2,1)}, u32[]{:S(2)}, u32[]{:S(2)}) collective-permute-start(bf16[256,1536]{1,0:T(8,128)(2,1)S(1)} %pad_maximum_fusion.refs_4_), channel_id=1, source_target_pairs={{0,4},{4,0},{8,12},{12,8},{16,20},{20,16},{24,28},{28,24},{1,5},{5... | collective-permute-start | bytes 2359304 | tf_op jit(solution)/shard_map/ppermute | solution.py:243
  62.9 29.4 %collective-permute-start.13 = (bf16[256,1536]{1,0:T(8,128)(2,1)}, bf16[256,1536]{1,0:T(8,128)(2,1)S(1)}, u32[]{:S(2)}, u32[]{:S(2)}) collective-permute-start(bf16[256,1536]{1,0:T(8,128)(2,1)} %collective-permute-done.5.refs_8_), channel_id=1, source_target_pairs={{0,8},{4,12},{8,0},{12,4},{16,24},{20,28},{24,16},{28,20},{1,9},{5... | collective-permute-start | bytes 2359304 | tf_op jit(solution)/shard_map/ppermute | solution.py:240
  82.4 25.1 %copy-start = (bf16[784,256]{1,0:T(8,128)(2,1)}, bf16[784,256]{1,0:T(8,128)(2,1)S(1)}, u32[]{:S(2)}) copy-start(bf16[784,256]{1,0:T(8,128)(2,1)S(1)} %collective-permute-done.14.refs_19_.refs_2_) | copy-start | bytes 1204228
  82.4 10.0 %collective-permute-start.16 = (bf16[768,256]{1,0:T(8,128)(2,1)}, bf16[768,256]{1,0:T(8,128)(2,1)}, u32[]{:S(2)}, u32[]{:S(2)}) collective-permute-start(bf16[768,256]{1,0:T(8,128)(2,1)} %collective-permute-done.4.refs_9_.refs_15_), channel_id=1, source_target_pairs={{0,4},{4,0},{8,12},{12,8},{16,20},{20,16},{24,28},{28,24},{1,5},{5... | collective-permute-start | bytes 1179656 | tf_op jit(solution)/shard_map/ppermute | solution.py:243
  82.4 9.9 %collective-permute-start.15 = (bf16[768,256]{1,0:T(8,128)(2,1)S(1)}, bf16[768,256]{1,0:T(8,128)(2,1)}, u32[]{:S(2)}, u32[]{:S(2)}) collective-permute-start(bf16[768,256]{1,0:T(8,128)(2,1)S(1)} %get-tuple-element.48.refs_7_.refs_13_), channel_id=1, source_target_pairs={{0,4},{4,0},{8,12},{12,8},{16,20},{20,16},{24,28},{28,24},{1,5},{5... | collective-permute-start | bytes 1179656 | tf_op jit(solution)/shard_map/ppermute | solution.py:243
  92.2 11.4 %collective-permute-start.19 = (bf16[784,256]{1,0:T(8,128)(2,1)S(1)}, bf16[784,256]{1,0:T(8,128)(2,1)S(1)}, u32[]{:S(2)}, u32[]{:S(2)}) collective-permute-start(bf16[784,256]{1,0:T(8,128)(2,1)S(1)} %collective-permute-done.14.refs_19_.refs_2_), channel_id=1, source_target_pairs={{0,8},{4,12},{8,0},{12,4},{16,24},{20,28},{24,16},{28,20},{1,9},{5... | collective-permute-start | bytes 1204232 | tf_op jit(solution)/shard_map/ppermute | solution.py:240
  92.3 2.6 %copy-start.6 = (bf16[256,1536]{1,0:T(8,128)(2,1)}, bf16[256,1536]{1,0:T(8,128)(2,1)S(1)}, u32[]{:S(2)}) copy-start(bf16[256,1536]{1,0:T(8,128)(2,1)S(1)} %collective-permute-done.13.refs_4_.refs_10_) | copy-start | bytes 2359300
  92.4 1.9 %collective-permute-start.17 = (bf16[256,768]{1,0:T(8,128)(2,1)S(1)}, bf16[256,768]{1,0:T(8,128)(2,1)}, u32[]{:S(2)}, u32[]{:S(2)}) collective-permute-start(bf16[256,768]{1,0:T(8,128)(2,1)S(1)} %get-tuple-element.74), channel_id=1, source_target_pairs={{0,4},{4,0},{8,12},{12,8},{16,20},{20,16},{24,28},{28,24},{1,5},{5... | collective-permute-start | bytes 1179656 | tf_op jit(solution)/shard_map/ppermute | solution.py:243
  92.6 2.3 %collective-permute-start.18 = (bf16[256,768]{1,0:T(8,128)(2,1)S(1)}, bf16[256,768]{1,0:T(8,128)(2,1)}, u32[]{:S(2)}, u32[]{:S(2)}) collective-permute-start(bf16[256,768]{1,0:T(8,128)(2,1)S(1)} %get-tuple-element.73), channel_id=1, source_target_pairs={{0,4},{4,0},{8,12},{12,8},{16,20},{20,16},{24,28},{28,24},{1,5},{5... | collective-permute-start | bytes 1179656 | tf_op jit(solution)/shard_map/ppermute | solution.py:243
  101.2 6.2 %collective-permute-start.21 = (bf16[784,256]{1,0:T(8,128)(2,1)S(1)}, bf16[784,256]{1,0:T(8,128)(2,1)S(1)}, u32[]{:S(2)}, u32[]{:S(2)}) collective-permute-start(bf16[784,256]{1,0:T(8,128)(2,1)S(1)} %collective-permute-done.14.refs_19_.refs_2_), channel_id=1, source_target_pairs={{0,4},{4,0},{8,12},{12,8},{16,20},{20,16},{24,28},{28,24},{1,5},{5... | collective-permute-start | bytes 1204232 | tf_op jit(solution)/shard_map/ppermute | solution.py:243
  103.6 12.0 %copy-start.1 = (bf16[784,256]{1,0:T(8,128)(2,1)}, bf16[784,256]{1,0:T(8,128)(2,1)S(1)}, u32[]{:S(2)}) copy-start(bf16[784,256]{1,0:T(8,128)(2,1)S(1)} %collective-permute-done.19.refs_17_.refs_0_) | copy-start | bytes 1204228
  103.6 3.8 %collective-permute-start.20 = (bf16[784,256]{1,0:T(8,128)(2,1)S(1)}, bf16[784,256]{1,0:T(8,128)(2,1)S(1)}, u32[]{:S(2)}, u32[]{:S(2)}) collective-permute-start(bf16[784,256]{1,0:T(8,128)(2,1)S(1)} %collective-permute-done.19.refs_17_.refs_0_), channel_id=1, source_target_pairs={{0,4},{4,0},{8,12},{12,8},{16,20},{20,16},{24,28},{28,24},{1,5},{5... | collective-permute-start | bytes 1204232 | tf_op jit(solution)/shard_map/ppermute | solution.py:243
  103.6 10.6 %collective-permute-start.25 = (bf16[128,1024]{1,0:T(8,128)(2,1)}, bf16[128,1024]{1,0:T(8,128)(2,1)}, u32[]{:S(2)}, u32[]{:S(2)}) collective-permute-start(bf16[128,1024]{1,0:T(8,128)(2,1)} %get-tuple-element.60), channel_id=1, source_target_pairs={{0,1},{1,0},{2,3},{3,2},{4,5},{5,4},{6,7},{7,6},{8,9},{9,8},{10,11... | collective-permute-start | bytes 786440 | tf_op jit(solution)/shard_map/ppermute | solution.py:246
  105.4 21.2 %collective-permute-start.26 = (bf16[128,1024]{1,0:T(8,128)(2,1)}, bf16[128,1024]{1,0:T(8,128)(2,1)}, u32[]{:S(2)}, u32[]{:S(2)}) collective-permute-start(bf16[128,1024]{1,0:T(8,128)(2,1)} %get-tuple-element.61), channel_id=1, source_target_pairs={{0,2},{1,3},{2,0},{3,1},{4,6},{5,7},{6,4},{7,5},{8,10},{9,11},{10,... | collective-permute-start | bytes 786440 | tf_op jit(solution)/shard_map/ppermute | solution.py:246
  106.9 20.4 %collective-permute-start.27 = (bf16[128,1024]{1,0:T(8,128)(2,1)}, bf16[128,1024]{1,0:T(8,128)(2,1)}, u32[]{:S(2)}, u32[]{:S(2)}) collective-permute-start(bf16[128,1024]{1,0:T(8,128)(2,1)} %get-tuple-element.62), channel_id=1, source_target_pairs={{0,3},{1,2},{2,1},{3,0},{4,7},{5,6},{6,5},{7,4},{8,11},{9,10},{10,... | collective-permute-start | bytes 786440 | tf_op jit(solution)/shard_map/ppermute | solution.py:246
  107.4 8.2 %copy-start.2 = (bf16[784,256]{1,0:T(8,128)(2,1)}, bf16[784,256]{1,0:T(8,128)(2,1)S(1)}, u32[]{:S(2)}) copy-start(bf16[784,256]{1,0:T(8,128)(2,1)S(1)} %collective-permute-done.21.refs_20_.refs_3_) | copy-start | bytes 1204228
  107.4 1.3 copy-start.4
  108.7 6.9 %copy-start.3 = (bf16[784,256]{1,0:T(8,128)(2,1)}, bf16[784,256]{1,0:T(8,128)(2,1)S(1)}, u32[]{:S(2)}) copy-start(bf16[784,256]{1,0:T(8,128)(2,1)S(1)} %collective-permute-done.20.refs_18_.refs_1_) | copy-start | bytes 1204228
  111.1 17.7 %collective-permute-start.29 = (bf16[128,1024]{1,0:T(8,128)(2,1)}, bf16[128,1024]{1,0:T(8,128)(2,1)}, u32[]{:S(2)}, u32[]{:S(2)}) collective-permute-start(bf16[128,1024]{1,0:T(8,128)(2,1)} %get-tuple-element.65), channel_id=1, source_target_pairs={{0,1},{1,0},{2,3},{3,2},{4,5},{5,4},{6,7},{7,6},{8,9},{9,8},{10,11... | collective-permute-start | bytes 786440 | tf_op jit(solution)/shard_map/ppermute | solution.py:246
  112.7 18.9 %collective-permute-start.30 = (bf16[128,1024]{1,0:T(8,128)(2,1)}, bf16[128,1024]{1,0:T(8,128)(2,1)}, u32[]{:S(2)}, u32[]{:S(2)}) collective-permute-start(bf16[128,1024]{1,0:T(8,128)(2,1)} %get-tuple-element.67), channel_id=1, source_target_pairs={{0,2},{1,3},{2,0},{3,1},{4,6},{5,7},{6,4},{7,5},{8,10},{9,11},{10,... | collective-permute-start | bytes 786440 | tf_op jit(solution)/shard_map/ppermute | solution.py:246
  114.3 17.7 %collective-permute-start.31 = (bf16[128,1024]{1,0:T(8,128)(2,1)}, bf16[128,1024]{1,0:T(8,128)(2,1)}, u32[]{:S(2)}, u32[]{:S(2)}) collective-permute-start(bf16[128,1024]{1,0:T(8,128)(2,1)} %get-tuple-element.69), channel_id=1, source_target_pairs={{0,3},{1,2},{2,1},{3,0},{4,7},{5,6},{6,5},{7,4},{8,11},{9,10},{10,... | collective-permute-start | bytes 786440 | tf_op jit(solution)/shard_map/ppermute | solution.py:246
  126.6 28.9 %copy-start.5 = (bf16[128,2048]{1,0:T(8,128)(2,1)S(1)}, bf16[128,2048]{1,0:T(8,128)(2,1)}, u32[]{:S(2)}) copy-start(bf16[128,2048]{1,0:T(8,128)(2,1)} %get-tuple-element.55.refs_0_) | copy-start | bytes 1572868
  126.6 28.8 %collective-permute-start.22 = (bf16[128,2048]{1,0:T(8,128)(2,1)}, bf16[128,2048]{1,0:T(8,128)(2,1)S(1)}, u32[]{:S(2)}, u32[]{:S(2)}) collective-permute-start(bf16[128,2048]{1,0:T(8,128)(2,1)} %get-tuple-element.56), channel_id=1, source_target_pairs={{0,1},{1,0},{2,3},{3,2},{4,5},{5,4},{6,7},{7,6},{8,9},{9,8},{10,11... | collective-permute-start | bytes 1572872 | tf_op jit(solution)/shard_map/ppermute | solution.py:246
  127.3 28.1 %collective-permute-start.23 = (bf16[128,2048]{1,0:T(8,128)(2,1)}, bf16[128,2048]{1,0:T(8,128)(2,1)S(1)}, u32[]{:S(2)}, u32[]{:S(2)}) collective-permute-start(bf16[128,2048]{1,0:T(8,128)(2,1)} %get-tuple-element.57), channel_id=1, source_target_pairs={{0,2},{1,3},{2,0},{3,1},{4,6},{5,7},{6,4},{7,5},{8,10},{9,11},{10,... | collective-permute-start | bytes 1572872 | tf_op jit(solution)/shard_map/ppermute | solution.py:246
  128.9 26.6 %collective-permute-start.24 = (bf16[128,2048]{1,0:T(8,128)(2,1)}, bf16[128,2048]{1,0:T(8,128)(2,1)S(1)}, u32[]{:S(2)}, u32[]{:S(2)}) collective-permute-start(bf16[128,2048]{1,0:T(8,128)(2,1)} %get-tuple-element.58), channel_id=1, source_target_pairs={{0,3},{1,2},{2,1},{3,0},{4,7},{5,6},{6,5},{7,4},{8,11},{9,10},{10,... | collective-permute-start | bytes 1572872 | tf_op jit(solution)/shard_map/ppermute | solution.py:246
  131.6 19.0 %collective-permute-start.28 = (bf16[128,1024]{1,0:T(8,128)(2,1)S(1)}, bf16[128,1024]{1,0:T(8,128)(2,1)S(1)}, u32[]{:S(2)}, u32[]{:S(2)}) collective-permute-start(bf16[128,1024]{1,0:T(8,128)(2,1)S(1)} %add_convert_fusion.1), channel_id=1, source_target_pairs={{0,24},{4,28},{8,16},{12,20},{16,8},{20,12},{24,0},{28,4},{1,25},{... | collective-permute-start | bytes 786440 | tf_op jit(solution)/shard_map/ppermute | solution.py:240
  134.1 21.4 %collective-permute-start.32 = (bf16[128,1024]{1,0:T(8,128)(2,1)}, bf16[128,1024]{1,0:T(8,128)(2,1)S(1)}, u32[]{:S(2)}, u32[]{:S(2)}) collective-permute-start(bf16[128,1024]{1,0:T(8,128)(2,1)} %add_convert_fusion), channel_id=1, source_target_pairs={{0,24},{4,28},{8,16},{12,20},{16,8},{20,12},{24,0},{28,4},{1,25},{... | collective-permute-start | bytes 786440 | tf_op jit(solution)/shard_map/ppermute | solution.py:240

commit v7 on v6

--- a/solution.py
+++ b/solution.py
@@ -108,7 +108,10 @@
     weight_refs, refs = refs[: sum(pieces)], refs[sum(pieces) :]
     down_refs, refs = refs[:down_slices], refs[down_slices:]
     sums_in, refs = refs[:summed], refs[summed:]
-    hidden, out_refs, refs = refs[0], refs[1 : 1 + blocks], refs[1 + blocks :]
+    if summed:
+        hidden, out_refs, refs = refs[0], refs[1 : 1 + blocks], refs[1 + blocks :]
+    else:
+        hidden, out_refs, refs = refs[blocks], refs[:blocks], refs[blocks + 1 :]
     sums, (rows, weights, down, sems) = refs[:summed], refs[summed:]
     depth, both = weight_refs[0].shape[0], weights.shape[1]
     loads = Loads(sems)
@@ -179,12 +182,13 @@
     tile = 256 if inner % 256 == 0 else inner
     whole = pl.BlockSpec(memory_space=pltpu.VMEM)
     out = jax.ShapeDtypeStruct((tok_rows, down_slices * depth), jnp.bfloat16)
+    kept = [jax.ShapeDtypeStruct((count, inner), jnp.bfloat16)] if early else []
     results = pl.pallas_call(
         functools.partial(late_kernel, blocks, pieces, down_slices, tile, len(early)),
         in_specs=[SMEM] + [ANY] * (blocks + len(gate_up) + down_slices + len(early)),
-        out_specs=[whole] * (1 + blocks),
-        out_shape=[jax.ShapeDtypeStruct((count, inner), jnp.bfloat16)] + [out] * blocks,
-        scratch_shapes=[pltpu.VMEM((count, inner), jnp.float32)] * len(early)
+        out_specs=[whole] * (len(kept) + blocks),
+        out_shape=kept + [out] * blocks,
+        scratch_shapes=([pltpu.VMEM((count, inner), jnp.float32)] * len(early) or [pltpu.VMEM((count, inner), jnp.bfloat16)])
         + [
             pltpu.VMEM((count, slices * depth), jnp.bfloat16),
             pltpu.VMEM((slices * depth, both), jnp.bfloat16),
@@ -194,7 +198,7 @@
         compiler_params=pltpu.CompilerParams(vmem_limit_bytes=62 * 1024 * 1024),
         cost_estimate=FREE,
     )(numbers, *row_blocks, *gate_up, *down, *early)
-    return results[0], results[1:]
+    return results[: len(kept)], results[len(kept) :]
 
 
 def down_kernel(blocks, slices, numbers_ref, hidden_ref, *refs):
@@ -337,7 +341,7 @@
         for chunk, sums in zip(chunks, early):
             pieces = [found if isinstance(found, list) else [found] for found in both_cores(gu, gu_core, gate_masks)]
             rows, blocks = late_outputs(chunk, pieces, both_cores(dn, dn_core, down_masks), counted, sums)
-            hidden.append(rows)
+            hidden += rows
             parts += blocks
         return hidden, parts
 
@@ -345,7 +349,7 @@
     for mask in near[1:]:
         dn[mask ^ mirror] = swap_layer(after(dn[mirror], *settled), mask)
     for mask in away:
-        dn_core[mask] = swap_core(after(dn[mask], far_hidden[-1]))
+        dn_core[mask] = swap_core(after(dn[mask], *((far_hidden[-1],) if mask != mirror else settled)))
     starts = numbers([lax.rem(v, 2 * len(away)) * depth for v in lines_of(away)])
     more_parts = []
     for chunk, rows in zip(chunks["far"], far_hidden):

time: 158 us -> 158 us (level)
  no operation moved by 1% of the time
where the time goes in v7:
time: 158 us; the launch traced here: 157 us
  waiting for transfers between devices  90.4 us (57%)
  Pallas kernels  29 us (18%)
  starting transfers between devices  27.5 us (17%)
  local copies, waits for them, and re-layouts  6 us (4%)
  other arithmetic  4.1 us (3%)
    ppermute x9, waiting for transfers between devices, swap_layer(): return lax.ppermute(array, 'dp', [(i, i ^ 2 * mask) for i in range(lines)])  66.4 us
    ppermute x15, waiting for transfers between devices, swap_place(): return lax.ppermute(array, 'expert', [(i, i ^ mask) for i in range(places)])  22.6 us
    ppermute x15, starting transfers between devices, swap_place(): return lax.ppermute(array, 'expert', [(i, i ^ mask) for i in range(places)])  18.5 us
    pallas_call x2, Pallas kernels, late_outputs(): pl.pallas_call(functools.partial(late_kernel, blocks, pieces, down_slices...  17.3 us
    pallas_call x1, Pallas kernels, early_sums(): pl.pallas_call(functools.partial(early_kernel, blocks, slices), grid=(til...  7.39 us
    ppermute x9, starting transfers between devices, swap_layer(): return lax.ppermute(array, 'dp', [(i, i ^ 2 * mask) for i in range(lines)])  7.2 us
    convert_element_type x2, other arithmetic, add_up(): return total.astype(jnp.bfloat16)  3.55 us
  transfers between devices with their start and end apart: 33, of which 12 were waited for; matrix products, arithmetic and copies ran while one was open for 5% of the time, Pallas kernels for 17%

profile of v7, /device:TPU:16, one launch (start us, length us, event | category | flops | bytes accessed | tf_op | source)
XLA Modules:
  0.0 157.3 jit_solution(10870571729650551330)
XLA Ops:
  0.0 0.4 collective-permute-start.3
  0.5 1.5 collective-permute-start
  1.9 1.5 collective-permute-start.1
  3.5 0.5 collective-permute-start.2
  3.9 1.2 dynamic-slice_bitcast_fusion
  5.2 1.3 collective-permute-start.4
  6.5 0.1 dynamic-slice_bitcast_fusion.4
  6.7 0.6 copy-done.15
  7.3 0.2 copy.15
  7.5 0.1 reshape.37
  7.8 15.5 %collective-permute-done.4.refs_9_.refs_15_ = bf16[768,256]{1,0:T(8,128)(2,1)} collective-permute-done((bf16[768,256]{1,0:T(8,128)(2,1)S(1)}, bf16[768,256]{1,0:T(8,128)(2,1)}, u32[]{:S(2)}, u32[]{:S(2)}) %collective-permute-start.4) | collective-permute-done | bytes 393248 | tf_op jit(solution)/shard_map/ppermute | solution.py:244
  23.3 1.8 %collective-permute-done.3.refs_0_ = bf16[128,2048]{1,0:T(8,128)(2,1)S(1)} collective-permute-done((bf16[128,2048]{1,0:T(8,128)(2,1)}, bf16[128,2048]{1,0:T(8,128)(2,1)S(1)}, u32[]{:S(2)}, u32[]{:S(2)}) %collective-permute-start.3) | collective-permute-done | bytes 524320 | tf_op jit(solution)/shard_map/ppermute | solution.py:244
  25.1 0.8 collective-permute-start.6
  25.9 0.7 collective-permute-done.1.refs_2_
  26.6 0.9 collective-permute-start.7
  27.5 1.5 collective-permute-start.8
  29.0 1.1 collective-permute-start.9
  30.1 11.4 %collective-permute-done.7.refs_1_ = bf16[128,2048]{1,0:T(8,128)(2,1)S(1)} collective-permute-done((bf16[128,2048]{1,0:T(8,128)(2,1)S(1)}, bf16[128,2048]{1,0:T(8,128)(2,1)S(1)}, u32[]{:S(2)}, u32[]{:S(2)}) %collective-permute-start.7) | collective-permute-done | bytes 524320 | tf_op jit(solution)/shard_map/ppermute | solution.py:250
  41.5 10.5 %collective-permute-done.8.refs_2_ = bf16[128,2048]{1,0:T(8,128)(2,1)S(1)} collective-permute-done((bf16[128,2048]{1,0:T(8,128)(2,1)S(1)}, bf16[128,2048]{1,0:T(8,128)(2,1)S(1)}, u32[]{:S(2)}, u32[]{:S(2)}) %collective-permute-start.8) | collective-permute-done | bytes 524320 | tf_op jit(solution)/shard_map/ppermute | solution.py:250
  52.0 10.0 %collective-permute-done.5.refs_8_ = bf16[256,1536]{1,0:T(8,128)(2,1)} collective-permute-done((bf16[256,1536]{1,0:T(8,128)(2,1)S(1)}, bf16[256,1536]{1,0:T(8,128)(2,1)}, u32[]{:S(2)}, u32[]{:S(2)}) %collective-permute-start.5) | collective-permute-done | bytes 786464 | tf_op jit(solution)/shard_map/ppermute | solution.py:244
  62.0 0.3 collective-permute-start.14
  62.4 0.2 collective-permute-start.11
  62.6 0.3 collective-permute-start.10
  62.9 2.2 %collective-permute-start.13 = (bf16[256,1536]{1,0:T(8,128)(2,1)}, bf16[256,1536]{1,0:T(8,128)(2,1)S(1)}, u32[]{:S(2)}, u32[]{:S(2)}) collective-permute-start(bf16[256,1536]{1,0:T(8,128)(2,1)} %collective-permute-done.5.refs_8_), channel_id=1, source_target_pairs={{0,8},{4,12},{8,0},{12,4},{16,24},{20,28},{24,16},{28,20},{1,9},{5... | collective-permute-start | bytes 2359304 | tf_op jit(solution)/shard_map/ppermute | solution.py:244
  65.1 17.2 %collective-permute-done.14.refs_19_.refs_2_ = bf16[784,256]{1,0:T(8,128)(2,1)S(1)} collective-permute-done((bf16[784,256]{1,0:T(8,128)(2,1)S(1)}, bf16[784,256]{1,0:T(8,128)(2,1)S(1)}, u32[]{:S(2)}, u32[]{:S(2)}) %collective-permute-start.14) | collective-permute-done | bytes 401440 | tf_op jit(solution)/shard_map/ppermute | solution.py:244
  82.4 0.5 collective-permute-start.15
  82.9 0.6 concatenate.23.numbers_ref
  83.5 0.6 stack.163.numbers_ref
  84.1 0.6 concatenate.18.numbers_ref
  84.8 7.4 %shard_map.64 = (f32[512,768]{1,0:T(8,128)}, f32[512,768]{1,0:T(8,128)}) custom-call(s32[9]{0:T(128)} %stack.163.numbers_ref, bf16[128,2048]{1,0:T(8,128)(2,1)} %copy-done.9, bf16[128,2048]{1,0:T(8,128)(2,1)} %copy-done.10, bf16[128,2048]{1,0:T(8,128)(2,1)} %copy-done.11, bf16[128,2048]{1,0:T(8,128)(2,1)} %copy-done.12, bf16[256,1536]{1,0:T(8,128)(2,1)} %copy-done.7, ...), custom_call_target="tpu_custom_call" | custom-call | tf_op jit(solution)/shard_map/pallas_call | solution.py:159
  92.4 0.2 collective-permute-start.17
  92.6 0.3 collective-permute-start.18
  92.9 0.1 pad_add_fusion.2.numbers_ref
  93.0 0.1 pad_add_fusion.1
  93.1 0.1 copy-done.6
  93.2 0.1 iota_compare_fusion.1
  93.3 0.2 collective-permute-start.21
  93.5 0.8 collective-permute-done.17.refs_5_.refs_11_
  94.3 0.6 collective-permute-done.18.refs_6_.refs_12_
  94.8 6.3 %shard_map.65 = (bf16[512,768]{1,0:T(8,128)(2,1)}, bf16[128,1024]{1,0:T(8,128)(2,1)}, bf16[128,1024]{1,0:T(8,128)(2,1)}, bf16[128,1024]{1,0:T(8,128)(2,1)}, bf16[128,1024]{1,0:T(8,128)(2,1)}) custom-call(s32[7]{0:T(128)} %concatenate.23.numbers_ref, bf16[128,2048]{1,0:T(8,128)(2,1)} %copy-done.9, bf16[128,2048]{1,0:T(8,128)(2,1)} %copy-done.10, ...), custom_call_target="tpu_custom_call" | custom-call | tf_op jit(solution)/shard_map/pallas_call | solution.py:186
  101.2 2.4 %collective-permute-done.19.refs_17_.refs_0_ = bf16[784,256]{1,0:T(8,128)(2,1)S(1)} collective-permute-done((bf16[784,256]{1,0:T(8,128)(2,1)S(1)}, bf16[784,256]{1,0:T(8,128)(2,1)S(1)}, u32[]{:S(2)}, u32[]{:S(2)}) %collective-permute-start.19) | collective-permute-done | bytes 401440 | tf_op jit(solution)/shard_map/ppermute | solution.py:244
  103.6 1.6 collective-permute-start.25
  105.2 0.1 add.106
  105.3 1.6 collective-permute-start.26
  106.9 0.5 collective-permute-start.27
  107.4 1.3 copy-done.4
  108.7 2.4 %shard_map.67 = (bf16[128,1024]{1,0:T(8,128)(2,1)S(1)}, bf16[128,1024]{1,0:T(8,128)(2,1)}, bf16[128,1024]{1,0:T(8,128)(2,1)}, bf16[128,1024]{1,0:T(8,128)(2,1)}) custom-call(s32[4]{0:T(128)S(1)} %pad_add_fusion.2.numbers_ref, bf16[512,768]{1,0:T(8,128)(2,1)S(1)} %copy-done.4, bf16[784,256]{1,0:T(8,128)(2,1)S(1)} %collective-permute-done.19.refs_17_.refs_0_, ...), custom_call_target="tpu_custom_call" | custom-call | tf_op jit(solution)/shard_map/pallas_call | solution.py:212
  111.0 1.5 collective-permute-start.29
  112.5 0.1 select_reduce_fusion
  112.6 1.6 %collective-permute-start.30 = (bf16[128,1024]{1,0:T(8,128)(2,1)}, bf16[128,1024]{1,0:T(8,128)(2,1)}, u32[]{:S(2)}, u32[]{:S(2)}) collective-permute-start(bf16[128,1024]{1,0:T(8,128)(2,1)} %get-tuple-element.65), channel_id=1, source_target_pairs={{0,2},{1,3},{2,0},{3,1},{4,6},{5,7},{6,4},{7,5},{8,10},{9,11},{10,... | collective-permute-start | bytes 786440 | tf_op jit(solution)/shard_map/ppermute | solution.py:250
  114.2 1.3 collective-permute-start.31
  115.6 11.0 %shard_map.66 = (bf16[128,2048]{1,0:T(8,128)(2,1)}, bf16[128,2048]{1,0:T(8,128)(2,1)}, bf16[128,2048]{1,0:T(8,128)(2,1)}, bf16[128,2048]{1,0:T(8,128)(2,1)}) custom-call(s32[20]{0:T(128)} %concatenate.18.numbers_ref, bf16[128,2048]{1,0:T(8,128)(2,1)} %refs_0_.1, bf16[128,2048]{1,0:T(8,128)(2,1)} %collective-permute-done.refs_1_, ...), custom_call_target="tpu_custom_call" | custom-call | tf_op jit(solution)/shard_map/pallas_call | solution.py:186
  126.6 0.7 collective-permute-start.22
  127.3 1.5 collective-permute-start.23
  128.8 1.3 collective-permute-start.24
  130.2 1.5 add_convert_fusion.1
  131.6 0.3 collective-permute-start.28
  132.0 2.1 %add_convert_fusion = bf16[128,1024]{1,0:T(8,128)(2,1)} fusion(bf16[128,1024]{1,0:T(8,128)(2,1)} %collective-permute-done.31, bf16[128,1024]{1,0:T(8,128)(2,1)} %collective-permute-done.30, bf16[128,1024]{1,0:T(8,128)(2,1)} %collective-permute-done.29, bf16[128,1024]{1,0:T(8,128)(2,1)S(1)} %get-tuple-element.62, f32[128]{0:T(128)S(1)} %get-tuple-element.83, ...), kind=kLoop, calls=%fused_computation.2 | loop fusion | flops 1572864 | bytes 1312768 | tf_op jit(solution)/shard_map/convert_element_type | solution.py:335
  134.1 1.7 %collective-permute-start.32 = (bf16[128,1024]{1,0:T(8,128)(2,1)}, bf16[128,1024]{1,0:T(8,128)(2,1)S(1)}, u32[]{:S(2)}, u32[]{:S(2)}) collective-permute-start(bf16[128,1024]{1,0:T(8,128)(2,1)} %add_convert_fusion), channel_id=1, source_target_pairs={{0,24},{4,28},{8,16},{12,20},{16,8},{20,12},{24,0},{28,4},{1,25},{... | collective-permute-start | bytes 786440 | tf_op jit(solution)/shard_map/ppermute | solution.py:244
  135.8 0.1 pad_add_fusion.bases_ref
  135.9 0.1 copy.17.gates_ref
  136.0 14.6 %collective-permute-done.28.refs_4_ = bf16[128,1024]{1,0:T(8,128)(2,1)S(1)} collective-permute-done((bf16[128,1024]{1,0:T(8,128)(2,1)S(1)}, bf16[128,1024]{1,0:T(8,128)(2,1)S(1)}, u32[]{:S(2)}, u32[]{:S(2)}) %collective-permute-start.28) | collective-permute-done | bytes 262176 | tf_op jit(solution)/shard_map/ppermute | solution.py:244
  150.6 4.8 %collective-permute-done.32.refs_5_ = bf16[128,1024]{1,0:T(8,128)(2,1)S(1)} collective-permute-done((bf16[128,1024]{1,0:T(8,128)(2,1)}, bf16[128,1024]{1,0:T(8,128)(2,1)S(1)}, u32[]{:S(2)}, u32[]{:S(2)}) %collective-permute-start.32) | collective-permute-done | bytes 262176 | tf_op jit(solution)/shard_map/ppermute | solution.py:244
  155.4 1.9 %shard_map.68 = bf16[128,2048]{1,0:T(8,128)(2,1)} custom-call(s32[2]{0:T(128)S(1)} %pad_add_fusion.bases_ref, f32[128,4]{1,0:T(8,128)S(1)} %copy.17.gates_ref, bf16[128,2048]{1,0:T(8,128)(2,1)S(1)} %copy-done.5, bf16[128,2048]{1,0:T(8,128)(2,1)S(1)} %collective-permute-done.22.refs_1_, bf16[128,2048]{1,0:T(8,128)(2,1)S(1)} %collective-permute-done.23.refs_2_, ...), custom_call_target="tpu_custom_call" | custom-call | tf_op jit(solution)/shard_map/pallas_call | solution.py:366
  (70 shorter events, 0.5 us)
Async XLA Ops:
  0.0 6.5 %copy-start.13 = (bf16[2,256,768]{2,1,0:T(8,128)(2,1)S(1)}, bf16[2,256,768]{2,1,0:T(8,128)(2,1)}, u32[]{:S(2)}) copy-start(bf16[2,256,768]{2,1,0:T(8,128)(2,1)} %param.11) | copy-start | bytes 2359300
  0.0 25.1 %collective-permute-start.3 = (bf16[128,2048]{1,0:T(8,128)(2,1)}, bf16[128,2048]{1,0:T(8,128)(2,1)S(1)}, u32[]{:S(2)}, u32[]{:S(2)}) collective-permute-start(bf16[128,2048]{1,0:T(8,128)(2,1)} %refs_0_.1), channel_id=1, source_target_pairs={{0,24},{4,28},{8,16},{12,20},{16,8},{20,12},{24,0},{28,4},{1,25},{... | collective-permute-start | bytes 1572872 | tf_op jit(solution)/shard_map/ppermute | solution.py:244
  0.5 25.4 %collective-permute-start = (bf16[128,2048]{1,0:T(8,128)(2,1)}, bf16[128,2048]{1,0:T(8,128)(2,1)}, u32[]{:S(2)}, u32[]{:S(2)}) collective-permute-start(bf16[128,2048]{1,0:T(8,128)(2,1)} %refs_0_.1), channel_id=1, source_target_pairs={{0,1},{1,0},{2,3},{3,2},{4,5},{5,4},{6,7},{7,6},{8,9},{9,8},{10,11... | collective-permute-start | bytes 1572872 | tf_op jit(solution)/shard_map/ppermute | solution.py:250
  1.9 24.7 %collective-permute-start.1 = (bf16[128,2048]{1,0:T(8,128)(2,1)}, bf16[128,2048]{1,0:T(8,128)(2,1)}, u32[]{:S(2)}, u32[]{:S(2)}) collective-permute-start(bf16[128,2048]{1,0:T(8,128)(2,1)} %refs_0_.1), channel_id=1, source_target_pairs={{0,2},{1,3},{2,0},{3,1},{4,6},{5,7},{6,4},{7,5},{8,10},{9,11},{10,... | collective-permute-start | bytes 1572872 | tf_op jit(solution)/shard_map/ppermute | solution.py:250
  3.5 25.5 %collective-permute-start.2 = (bf16[128,2048]{1,0:T(8,128)(2,1)}, bf16[128,2048]{1,0:T(8,128)(2,1)}, u32[]{:S(2)}, u32[]{:S(2)}) collective-permute-start(bf16[128,2048]{1,0:T(8,128)(2,1)} %refs_0_.1), channel_id=1, source_target_pairs={{0,3},{1,2},{2,1},{3,0},{4,7},{5,6},{6,5},{7,4},{8,11},{9,10},{10,... | collective-permute-start | bytes 1572872 | tf_op jit(solution)/shard_map/ppermute | solution.py:250
  3.9 2.5 %copy-start.14 = (bf16[2,256,768]{2,1,0:T(8,128)(2,1)S(1)}, bf16[2,256,768]{2,1,0:T(8,128)(2,1)}, u32[]{:S(2)}) copy-start(bf16[2,256,768]{2,1,0:T(8,128)(2,1)} %param.10) | copy-start | bytes 2359300
  5.2 77.2 %copy-start.8 = (bf16[768,256]{1,0:T(8,128)(2,1)}, bf16[768,256]{1,0:T(8,128)(2,1)S(1)}, u32[]{:S(2)}) copy-start(bf16[768,256]{1,0:T(8,128)(2,1)S(1)} %get-tuple-element.47.refs_7_.refs_13_) | copy-start | bytes 1179652
  5.2 18.1 %collective-permute-start.4 = (bf16[768,256]{1,0:T(8,128)(2,1)S(1)}, bf16[768,256]{1,0:T(8,128)(2,1)}, u32[]{:S(2)}, u32[]{:S(2)}) collective-permute-start(bf16[768,256]{1,0:T(8,128)(2,1)S(1)} %get-tuple-element.47.refs_7_.refs_13_), channel_id=1, source_target_pairs={{0,8},{4,12},{8,0},{12,4},{16,24},{20,28},{24,16},{28,20},{1,9},{5... | collective-permute-start | bytes 1179656 | tf_op jit(solution)/shard_map/ppermute | solution.py:244
  6.6 0.7 copy-start.15
  6.6 0.7 copy-start.16
  7.3 75.0 %copy-start.7 = (bf16[256,1536]{1,0:T(8,128)(2,1)}, bf16[256,1536]{1,0:T(8,128)(2,1)S(1)}, u32[]{:S(2)}) copy-start(bf16[256,1536]{1,0:T(8,128)(2,1)S(1)} %pad_maximum_fusion.refs_4_) | copy-start | bytes 2359300
  25.1 57.8 %copy-start.9 = (bf16[128,2048]{1,0:T(8,128)(2,1)}, bf16[128,2048]{1,0:T(8,128)(2,1)S(1)}, u32[]{:S(2)}) copy-start(bf16[128,2048]{1,0:T(8,128)(2,1)S(1)} %collective-permute-done.3.refs_0_) | copy-start | bytes 1572868
  25.1 26.9 %collective-permute-start.6 = (bf16[256,1536]{1,0:T(8,128)(2,1)S(1)}, bf16[256,1536]{1,0:T(8,128)(2,1)}, u32[]{:S(2)}, u32[]{:S(2)}) collective-permute-start(bf16[256,1536]{1,0:T(8,128)(2,1)S(1)} %pad_maximum_fusion.refs_4_), channel_id=1, source_target_pairs={{0,8},{4,12},{8,0},{12,4},{16,24},{20,28},{24,16},{28,20},{1,9},{5... | collective-permute-start | bytes 2359304 | tf_op jit(solution)/shard_map/ppermute | solution.py:244
  25.9 36.1 %collective-permute-start.5 = (bf16[256,1536]{1,0:T(8,128)(2,1)S(1)}, bf16[256,1536]{1,0:T(8,128)(2,1)}, u32[]{:S(2)}, u32[]{:S(2)}) collective-permute-start(bf16[256,1536]{1,0:T(8,128)(2,1)S(1)} %pad_maximum_fusion.1), channel_id=1, source_target_pairs={{0,24},{4,28},{8,16},{12,20},{16,8},{20,12},{24,0},{28,4},{1,25},{... | collective-permute-start | bytes 2359304 | tf_op jit(solution)/shard_map/ppermute | solution.py:244
  26.6 14.9 %collective-permute-start.7 = (bf16[128,2048]{1,0:T(8,128)(2,1)S(1)}, bf16[128,2048]{1,0:T(8,128)(2,1)S(1)}, u32[]{:S(2)}, u32[]{:S(2)}) collective-permute-start(bf16[128,2048]{1,0:T(8,128)(2,1)S(1)} %collective-permute-done.3.refs_0_), channel_id=1, source_target_pairs={{0,1},{1,0},{2,3},{3,2},{4,5},{5,4},{6,7},{7,6},{8,9},{9,8},{10,11... | collective-permute-start | bytes 1572872 | tf_op jit(solution)/shard_map/ppermute | solution.py:250
  27.5 24.5 %collective-permute-start.8 = (bf16[128,2048]{1,0:T(8,128)(2,1)S(1)}, bf16[128,2048]{1,0:T(8,128)(2,1)S(1)}, u32[]{:S(2)}, u32[]{:S(2)}) collective-permute-start(bf16[128,2048]{1,0:T(8,128)(2,1)S(1)} %collective-permute-done.3.refs_0_), channel_id=1, source_target_pairs={{0,2},{1,3},{2,0},{3,1},{4,6},{5,7},{6,4},{7,5},{8,10},{9,11},{10,... | collective-permute-start | bytes 1572872 | tf_op jit(solution)/shard_map/ppermute | solution.py:250
  29.0 23.0 %collective-permute-start.9 = (bf16[128,2048]{1,0:T(8,128)(2,1)S(1)}, bf16[128,2048]{1,0:T(8,128)(2,1)S(1)}, u32[]{:S(2)}, u32[]{:S(2)}) collective-permute-start(bf16[128,2048]{1,0:T(8,128)(2,1)S(1)} %collective-permute-done.3.refs_0_), channel_id=1, source_target_pairs={{0,3},{1,2},{2,1},{3,0},{4,7},{5,6},{6,5},{7,4},{8,11},{9,10},{10,... | collective-permute-start | bytes 1572872 | tf_op jit(solution)/shard_map/ppermute | solution.py:250
  41.5 20.6 %copy-start.10 = (bf16[128,2048]{1,0:T(8,128)(2,1)}, bf16[128,2048]{1,0:T(8,128)(2,1)S(1)}, u32[]{:S(2)}) copy-start(bf16[128,2048]{1,0:T(8,128)(2,1)S(1)} %collective-permute-done.7.refs_1_) | copy-start | bytes 1572868
  52.0 10.1 %copy-start.11 = (bf16[128,2048]{1,0:T(8,128)(2,1)}, bf16[128,2048]{1,0:T(8,128)(2,1)S(1)}, u32[]{:S(2)}) copy-start(bf16[128,2048]{1,0:T(8,128)(2,1)S(1)} %collective-permute-done.8.refs_2_) | copy-start | bytes 1572868
  52.0 10.6 %copy-start.12 = (bf16[128,2048]{1,0:T(8,128)(2,1)}, bf16[128,2048]{1,0:T(8,128)(2,1)S(1)}, u32[]{:S(2)}) copy-start(bf16[128,2048]{1,0:T(8,128)(2,1)S(1)} %collective-permute-done.9.refs_3_) | copy-start | bytes 1572868
  62.0 20.3 %collective-permute-start.12 = (bf16[256,1536]{1,0:T(8,128)(2,1)}, bf16[256,1536]{1,0:T(8,128)(2,1)}, u32[]{:S(2)}, u32[]{:S(2)}) collective-permute-start(bf16[256,1536]{1,0:T(8,128)(2,1)} %collective-permute-done.5.refs_8_), channel_id=1, source_target_pairs={{0,4},{4,0},{8,12},{12,8},{16,20},{20,16},{24,28},{28,24},{1,5},{5... | collective-permute-start | bytes 2359304 | tf_op jit(solution)/shard_map/ppermute | solution.py:247
  62.0 20.3 %collective-permute-start.14 = (bf16[784,256]{1,0:T(8,128)(2,1)S(1)}, bf16[784,256]{1,0:T(8,128)(2,1)S(1)}, u32[]{:S(2)}, u32[]{:S(2)}) collective-permute-start(bf16[784,256]{1,0:T(8,128)(2,1)S(1)} %pad_maximum_fusion.2), channel_id=1, source_target_pairs={{0,24},{4,28},{8,16},{12,20},{16,8},{20,12},{24,0},{28,4},{1,25},{... | collective-permute-start | bytes 1204232 | tf_op jit(solution)/shard_map/ppermute | solution.py:244
  62.4 22.4 %collective-permute-start.11 = (bf16[256,1536]{1,0:T(8,128)(2,1)}, bf16[256,1536]{1,0:T(8,128)(2,1)}, u32[]{:S(2)}, u32[]{:S(2)}) collective-permute-start(bf16[256,1536]{1,0:T(8,128)(2,1)} %collective-permute-done.6.refs_6_), channel_id=1, source_target_pairs={{0,4},{4,0},{8,12},{12,8},{16,20},{20,16},{24,28},{28,24},{1,5},{5... | collective-permute-start | bytes 2359304 | tf_op jit(solution)/shard_map/ppermute | solution.py:247
  62.6 22.2 %collective-permute-start.10 = (bf16[256,1536]{1,0:T(8,128)(2,1)S(1)}, bf16[256,1536]{1,0:T(8,128)(2,1)}, u32[]{:S(2)}, u32[]{:S(2)}) collective-permute-start(bf16[256,1536]{1,0:T(8,128)(2,1)S(1)} %pad_maximum_fusion.refs_4_), channel_id=1, source_target_pairs={{0,4},{4,0},{8,12},{12,8},{16,20},{20,16},{24,28},{28,24},{1,5},{5... | collective-permute-start | bytes 2359304 | tf_op jit(solution)/shard_map/ppermute | solution.py:247
  62.9 29.3 %collective-permute-start.13 = (bf16[256,1536]{1,0:T(8,128)(2,1)}, bf16[256,1536]{1,0:T(8,128)(2,1)S(1)}, u32[]{:S(2)}, u32[]{:S(2)}) collective-permute-start(bf16[256,1536]{1,0:T(8,128)(2,1)} %collective-permute-done.5.refs_8_), channel_id=1, source_target_pairs={{0,8},{4,12},{8,0},{12,4},{16,24},{20,28},{24,16},{28,20},{1,9},{5... | collective-permute-start | bytes 2359304 | tf_op jit(solution)/shard_map/ppermute | solution.py:244
  82.4 25.0 %copy-start = (bf16[784,256]{1,0:T(8,128)(2,1)}, bf16[784,256]{1,0:T(8,128)(2,1)S(1)}, u32[]{:S(2)}) copy-start(bf16[784,256]{1,0:T(8,128)(2,1)S(1)} %collective-permute-done.14.refs_19_.refs_2_) | copy-start | bytes 1204228
  82.4 9.9 %collective-permute-start.16 = (bf16[768,256]{1,0:T(8,128)(2,1)}, bf16[768,256]{1,0:T(8,128)(2,1)}, u32[]{:S(2)}, u32[]{:S(2)}) collective-permute-start(bf16[768,256]{1,0:T(8,128)(2,1)} %collective-permute-done.4.refs_9_.refs_15_), channel_id=1, source_target_pairs={{0,4},{4,0},{8,12},{12,8},{16,20},{20,16},{24,28},{28,24},{1,5},{5... | collective-permute-start | bytes 1179656 | tf_op jit(solution)/shard_map/ppermute | solution.py:247
  82.4 9.9 %collective-permute-start.15 = (bf16[768,256]{1,0:T(8,128)(2,1)S(1)}, bf16[768,256]{1,0:T(8,128)(2,1)}, u32[]{:S(2)}, u32[]{:S(2)}) collective-permute-start(bf16[768,256]{1,0:T(8,128)(2,1)S(1)} %get-tuple-element.47.refs_7_.refs_13_), channel_id=1, source_target_pairs={{0,4},{4,0},{8,12},{12,8},{16,20},{20,16},{24,28},{28,24},{1,5},{5... | collective-permute-start | bytes 1179656 | tf_op jit(solution)/shard_map/ppermute | solution.py:247
  92.2 11.4 %collective-permute-start.19 = (bf16[784,256]{1,0:T(8,128)(2,1)S(1)}, bf16[784,256]{1,0:T(8,128)(2,1)S(1)}, u32[]{:S(2)}, u32[]{:S(2)}) collective-permute-start(bf16[784,256]{1,0:T(8,128)(2,1)S(1)} %collective-permute-done.14.refs_19_.refs_2_), channel_id=1, source_target_pairs={{0,8},{4,12},{8,0},{12,4},{16,24},{20,28},{24,16},{28,20},{1,9},{5... | collective-permute-start | bytes 1204232 | tf_op jit(solution)/shard_map/ppermute | solution.py:244
  92.3 1.0 copy-start.6
  92.4 1.9 %collective-permute-start.17 = (bf16[256,768]{1,0:T(8,128)(2,1)S(1)}, bf16[256,768]{1,0:T(8,128)(2,1)}, u32[]{:S(2)}, u32[]{:S(2)}) collective-permute-start(bf16[256,768]{1,0:T(8,128)(2,1)S(1)} %get-tuple-element.72), channel_id=1, source_target_pairs={{0,4},{4,0},{8,12},{12,8},{16,20},{20,16},{24,28},{28,24},{1,5},{5... | collective-permute-start | bytes 1179656 | tf_op jit(solution)/shard_map/ppermute | solution.py:247
  92.6 2.3 %collective-permute-start.18 = (bf16[256,768]{1,0:T(8,128)(2,1)S(1)}, bf16[256,768]{1,0:T(8,128)(2,1)}, u32[]{:S(2)}, u32[]{:S(2)}) collective-permute-start(bf16[256,768]{1,0:T(8,128)(2,1)S(1)} %get-tuple-element.71), channel_id=1, source_target_pairs={{0,4},{4,0},{8,12},{12,8},{16,20},{20,16},{24,28},{28,24},{1,5},{5... | collective-permute-start | bytes 1179656 | tf_op jit(solution)/shard_map/ppermute | solution.py:247
  93.3 14.1 %collective-permute-start.21 = (bf16[784,256]{1,0:T(8,128)(2,1)S(1)}, bf16[784,256]{1,0:T(8,128)(2,1)S(1)}, u32[]{:S(2)}, u32[]{:S(2)}) collective-permute-start(bf16[784,256]{1,0:T(8,128)(2,1)S(1)} %collective-permute-done.14.refs_19_.refs_2_), channel_id=1, source_target_pairs={{0,4},{4,0},{8,12},{12,8},{16,20},{20,16},{24,28},{28,24},{1,5},{5... | collective-permute-start | bytes 1204232 | tf_op jit(solution)/shard_map/ppermute | solution.py:247
  103.6 12.0 %copy-start.1 = (bf16[784,256]{1,0:T(8,128)(2,1)}, bf16[784,256]{1,0:T(8,128)(2,1)S(1)}, u32[]{:S(2)}) copy-start(bf16[784,256]{1,0:T(8,128)(2,1)S(1)} %collective-permute-done.19.refs_17_.refs_0_) | copy-start | bytes 1204228
  103.6 3.8 %collective-permute-start.20 = (bf16[784,256]{1,0:T(8,128)(2,1)S(1)}, bf16[784,256]{1,0:T(8,128)(2,1)S(1)}, u32[]{:S(2)}, u32[]{:S(2)}) collective-permute-start(bf16[784,256]{1,0:T(8,128)(2,1)S(1)} %collective-permute-done.19.refs_17_.refs_0_), channel_id=1, source_target_pairs={{0,4},{4,0},{8,12},{12,8},{16,20},{20,16},{24,28},{28,24},{1,5},{5... | collective-permute-start | bytes 1204232 | tf_op jit(solution)/shard_map/ppermute | solution.py:247
  103.6 10.6 %collective-permute-start.25 = (bf16[128,1024]{1,0:T(8,128)(2,1)}, bf16[128,1024]{1,0:T(8,128)(2,1)}, u32[]{:S(2)}, u32[]{:S(2)}) collective-permute-start(bf16[128,1024]{1,0:T(8,128)(2,1)} %get-tuple-element.58), channel_id=1, source_target_pairs={{0,1},{1,0},{2,3},{3,2},{4,5},{5,4},{6,7},{7,6},{8,9},{9,8},{10,11... | collective-permute-start | bytes 786440 | tf_op jit(solution)/shard_map/ppermute | solution.py:250
  105.3 21.3 %collective-permute-start.26 = (bf16[128,1024]{1,0:T(8,128)(2,1)}, bf16[128,1024]{1,0:T(8,128)(2,1)}, u32[]{:S(2)}, u32[]{:S(2)}) collective-permute-start(bf16[128,1024]{1,0:T(8,128)(2,1)} %get-tuple-element.59), channel_id=1, source_target_pairs={{0,2},{1,3},{2,0},{3,1},{4,6},{5,7},{6,4},{7,5},{8,10},{9,11},{10,... | collective-permute-start | bytes 786440 | tf_op jit(solution)/shard_map/ppermute | solution.py:250
  106.9 20.4 %collective-permute-start.27 = (bf16[128,1024]{1,0:T(8,128)(2,1)}, bf16[128,1024]{1,0:T(8,128)(2,1)}, u32[]{:S(2)}, u32[]{:S(2)}) collective-permute-start(bf16[128,1024]{1,0:T(8,128)(2,1)} %get-tuple-element.60), channel_id=1, source_target_pairs={{0,3},{1,2},{2,1},{3,0},{4,7},{5,6},{6,5},{7,4},{8,11},{9,10},{10,... | collective-permute-start | bytes 786440 | tf_op jit(solution)/shard_map/ppermute | solution.py:250
  107.4 8.2 %copy-start.2 = (bf16[784,256]{1,0:T(8,128)(2,1)}, bf16[784,256]{1,0:T(8,128)(2,1)S(1)}, u32[]{:S(2)}) copy-start(bf16[784,256]{1,0:T(8,128)(2,1)S(1)} %collective-permute-done.21.refs_20_.refs_3_) | copy-start | bytes 1204228
  107.4 1.3 copy-start.4
  108.7 6.9 %copy-start.3 = (bf16[784,256]{1,0:T(8,128)(2,1)}, bf16[784,256]{1,0:T(8,128)(2,1)S(1)}, u32[]{:S(2)}) copy-start(bf16[784,256]{1,0:T(8,128)(2,1)S(1)} %collective-permute-done.20.refs_18_.refs_1_) | copy-start | bytes 1204228
  111.0 17.8 %collective-permute-start.29 = (bf16[128,1024]{1,0:T(8,128)(2,1)}, bf16[128,1024]{1,0:T(8,128)(2,1)}, u32[]{:S(2)}, u32[]{:S(2)}) collective-permute-start(bf16[128,1024]{1,0:T(8,128)(2,1)} %get-tuple-element.63), channel_id=1, source_target_pairs={{0,1},{1,0},{2,3},{3,2},{4,5},{5,4},{6,7},{7,6},{8,9},{9,8},{10,11... | collective-permute-start | bytes 786440 | tf_op jit(solution)/shard_map/ppermute | solution.py:250
  112.6 19.0 %collective-permute-start.30 = (bf16[128,1024]{1,0:T(8,128)(2,1)}, bf16[128,1024]{1,0:T(8,128)(2,1)}, u32[]{:S(2)}, u32[]{:S(2)}) collective-permute-start(bf16[128,1024]{1,0:T(8,128)(2,1)} %get-tuple-element.65), channel_id=1, source_target_pairs={{0,2},{1,3},{2,0},{3,1},{4,6},{5,7},{6,4},{7,5},{8,10},{9,11},{10,... | collective-permute-start | bytes 786440 | tf_op jit(solution)/shard_map/ppermute | solution.py:250
  114.2 17.8 %collective-permute-start.31 = (bf16[128,1024]{1,0:T(8,128)(2,1)}, bf16[128,1024]{1,0:T(8,128)(2,1)}, u32[]{:S(2)}, u32[]{:S(2)}) collective-permute-start(bf16[128,1024]{1,0:T(8,128)(2,1)} %get-tuple-element.67), channel_id=1, source_target_pairs={{0,3},{1,2},{2,1},{3,0},{4,7},{5,6},{6,5},{7,4},{8,11},{9,10},{10,... | collective-permute-start | bytes 786440 | tf_op jit(solution)/shard_map/ppermute | solution.py:250
  126.6 28.8 %copy-start.5 = (bf16[128,2048]{1,0:T(8,128)(2,1)S(1)}, bf16[128,2048]{1,0:T(8,128)(2,1)}, u32[]{:S(2)}) copy-start(bf16[128,2048]{1,0:T(8,128)(2,1)} %get-tuple-element.53.refs_0_) | copy-start | bytes 1572868
  126.6 28.8 %collective-permute-start.22 = (bf16[128,2048]{1,0:T(8,128)(2,1)}, bf16[128,2048]{1,0:T(8,128)(2,1)S(1)}, u32[]{:S(2)}, u32[]{:S(2)}) collective-permute-start(bf16[128,2048]{1,0:T(8,128)(2,1)} %get-tuple-element.54), channel_id=1, source_target_pairs={{0,1},{1,0},{2,3},{3,2},{4,5},{5,4},{6,7},{7,6},{8,9},{9,8},{10,11... | collective-permute-start | bytes 1572872 | tf_op jit(solution)/shard_map/ppermute | solution.py:250
  127.3 28.1 %collective-permute-start.23 = (bf16[128,2048]{1,0:T(8,128)(2,1)}, bf16[128,2048]{1,0:T(8,128)(2,1)S(1)}, u32[]{:S(2)}, u32[]{:S(2)}) collective-permute-start(bf16[128,2048]{1,0:T(8,128)(2,1)} %get-tuple-element.55), channel_id=1, source_target_pairs={{0,2},{1,3},{2,0},{3,1},{4,6},{5,7},{6,4},{7,5},{8,10},{9,11},{10,... | collective-permute-start | bytes 1572872 | tf_op jit(solution)/shard_map/ppermute | solution.py:250
  128.8 26.6 %collective-permute-start.24 = (bf16[128,2048]{1,0:T(8,128)(2,1)}, bf16[128,2048]{1,0:T(8,128)(2,1)S(1)}, u32[]{:S(2)}, u32[]{:S(2)}) collective-permute-start(bf16[128,2048]{1,0:T(8,128)(2,1)} %get-tuple-element.56), channel_id=1, source_target_pairs={{0,3},{1,2},{2,1},{3,0},{4,7},{5,6},{6,5},{7,4},{8,11},{9,10},{10,... | collective-permute-start | bytes 1572872 | tf_op jit(solution)/shard_map/ppermute | solution.py:250
  131.6 18.9 %collective-permute-start.28 = (bf16[128,1024]{1,0:T(8,128)(2,1)S(1)}, bf16[128,1024]{1,0:T(8,128)(2,1)S(1)}, u32[]{:S(2)}, u32[]{:S(2)}) collective-permute-start(bf16[128,1024]{1,0:T(8,128)(2,1)S(1)} %add_convert_fusion.1), channel_id=1, source_target_pairs={{0,24},{4,28},{8,16},{12,20},{16,8},{20,12},{24,0},{28,4},{1,25},{... | collective-permute-start | bytes 786440 | tf_op jit(solution)/shard_map/ppermute | solution.py:244
  134.1 21.3 %collective-permute-start.32 = (bf16[128,1024]{1,0:T(8,128)(2,1)}, bf16[128,1024]{1,0:T(8,128)(2,1)S(1)}, u32[]{:S(2)}, u32[]{:S(2)}) collective-permute-start(bf16[128,1024]{1,0:T(8,128)(2,1)} %add_convert_fusion), channel_id=1, source_target_pairs={{0,24},{4,28},{8,16},{12,20},{16,8},{20,12},{24,0},{28,4},{1,25},{... | collective-permute-start | bytes 786440 | tf_op jit(solution)/shard_map/ppermute | solution.py:244
